TPU v7x, 512 devices: a whole 4x4x16 slice. The times are simulated.
512 devices in a mesh: gz: 8 (over x, core), gy: 64 (over y, z).
Axes of the slice: x: 4, y: 4, z: 16, core: 2. Of those that a mesh axis runs over, the one named last changes fastest.
Arguments:
- reference_scan: bfloat16 [128, 1024, 256], P('gz', 'gy'), may hold values from -6 to 6
- loaded_scan: bfloat16 [128, 1024, 256], P('gz', 'gy'), may hold values from -6 to 6
- partner: int32 [8, 64, 16, 1], P('gz', 'gy'), may hold values from 0 to 63; in each aligned block of 16 rows (0 to 15, 16 to 31, ..., all dimensions but the last counted through in order) at most 2 rows name the same one
- source: int32 [8, 64, 16], P('gz', 'gy'), may hold values from 0 to 15
Outputs:
- displacement: float32 [3, 8, 64, 17], P(None, 'gz', 'gy')
- misfit: float32 [8, 64, 16], P('gz', 'gy')
Inputs may be any that keep to these rules, and one draw needn't show every extreme that they name: At most 2 elements of one device name the same partner tile, and in every draw some device names some tile exactly 2 times.
All inputs are finite; a program needn't handle non-finite values.
Results may differ from a plain program's by a relative error of at most 0.0095.
Values may be sent and summed in bfloat16 or wider, within the bound.
No kernel may reach another device: no remote copies, remote signals or barrier semaphores. Data moves between devices by JAX's collectives and lax.ppermute only.
A program may use at most 128 MiB of HBM per device.

v0:
```python
import jax
import jax.numpy as jnp
import numpy as np
import ml_dtypes
from jax import lax
from jax.experimental import pallas as pl
from jax.experimental.pallas import tpu as pltpu
from jax.sharding import PartitionSpec as P

ES = 16
EX = 16
NXC = 256
ITERS = 3
SMOOTH = (0.03032, 0.249724, 0.439911, 0.249724, 0.03032)
DERIVATIVE = (-0.10455, -0.292315, 0.0, 0.292315, 0.10455)
PAIRS = ((0, 0), (0, 1), (0, 2), (1, 1), (1, 2), (2, 2))
F32 = jnp.float32
BF16 = jnp.bfloat16


def split(table):
    table = np.asarray(table, np.float64)
    high = table.astype(np.float32).astype(ml_dtypes.bfloat16)
    low = (table - high.astype(np.float64)).astype(np.float32).astype(ml_dtypes.bfloat16)
    return high, low


def column_filter():
    row = np.arange(NXC)
    place = (row % EX) * ES + row // EX
    smooth = np.zeros((NXC, NXC))
    slope = np.zeros((NXC, NXC))
    for k in range(-2, 3):
        at = place + k
        ok = (at >= 0) & (at < NXC)
        smooth[row[ok], at[ok]] = SMOOTH[k + 2]
        slope[row[ok], at[ok]] = DERIVATIVE[k + 2]
    order = np.zeros((NXC, NXC))
    order[row, place] = 1.0
    sh, sl = split(smooth)
    dh, dl = split(slope)
    return np.concatenate([sh, sl, dh, dl]), order.astype(ml_dtypes.bfloat16)


def plane_filter():
    zs, ys, real = [], [], []
    for z in range(16):
        for y in range(16):
            zs.append(z), ys.append(y), real.append(1)
    for z in (-2, -1, 16, 17):
        for y in range(16):
            zs.append(z), ys.append(y), real.append(1)
    for side in (-2, 16):
        for z in range(-2, 18):
            for j in range(2):
                zs.append(z), ys.append(side + j), real.append(1)
        for _ in range(8):
            zs.append(0), ys.append(0), real.append(0)
    zs, ys, real = np.array(zs), np.array(ys), np.array(real)
    zo, yo = np.arange(256) // 16, np.arange(256) % 16
    dz, dy = zs[:, None] - zo[None], ys[:, None] - yo[None]

    def tap(kernel, d):
        return np.where(np.abs(d) <= 2, np.array(kernel)[np.clip(d, -2, 2) + 2], 0.0)

    ok = real[:, None]
    depth = ok * tap(DERIVATIVE, dz) * tap(SMOOTH, dy)
    rows = ok * tap(SMOOTH, dz) * tap(DERIVATIVE, dy)
    both = ok * tap(SMOOTH, dz) * tap(SMOOTH, dy)
    return split(np.concatenate([depth, rows, both], axis=1))


def linear(t, side):
    w = (t + 0.5) / ES
    return w if side else 1.0 - w


def plane_weights():
    z, y = np.arange(256) // 16, np.arange(256) % 16
    quad = np.zeros((6, 256, 256))
    lin = np.zeros((4, 256, 128))
    for h in range(2):
        for l in range(2):
            for a in range(3):
                lin[a, :, h * 8 + l * 4 + a] = linear(z, h) * linear(y, l)
                for hh in range(2):
                    for ll in range(2):
                        for b in range(3):
                            col = ((hh * 2 + ll) * 3 + b) * 16 + h * 8 + l * 4 + a
                            ch = PAIRS.index((min(a, b), max(a, b)))
                            quad[ch, :, col] = (
                                linear(z, h) * linear(z, hh) * linear(y, l) * linear(y, ll)
                            )
    lin[3, :, 3] = 1.0
    return split(quad.reshape(1536, 256)) + split(lin.reshape(1024, 128))


def column_weights():
    row = np.arange(256)
    c, ex = row // EX, row % EX
    quad = np.zeros((256, 128))
    lin = np.zeros((256, 256))
    for f in range(2):
        np.add.at(lin, (row, ex + f), linear(c, f))
        lin[row, 128 + f * 32 + ex] = linear(c, f)
        for ff in range(2):
            quad[row, f * 32 + ff * 16 + ex] = linear(c, f) * linear(c, ff)
    qh, ql = split(quad)
    return qh, ql, lin.astype(ml_dtypes.bfloat16)


def side_rows():
    pick = np.zeros((96, 320))
    for side in range(2):
        for zz in range(20):
            for j in range(2):
                y = (14 if side == 0 else 0) + j
                if zz < 2:
                    at = 256 + zz * 16 + y
                elif zz < 18:
                    at = (zz - 2) * 16 + y
                else:
                    at = 288 + (zz - 18) * 16 + y
                pick[side * 48 + zz * 2 + j, at] = 1.0
    return pick.astype(ml_dtypes.bfloat16)


def dot(a, b):
    return jnp.dot(a, b, preferred_element_type=F32)


def dot_nt(a, b):
    return lax.dot_general(a, b, (((1,), (1,)), ((), ())), preferred_element_type=F32)


def halves(v):
    high = v.astype(BF16)
    return high, (v - high.astype(F32)).astype(BF16)


def dot3(v, wh, wl):
    h, l = halves(v)
    return dot(h, wh) + dot(l, wh) + dot(h, wl)


def lanes(shape):
    return lax.broadcasted_iota(jnp.int32, shape, 1)


def call(kernel, outs, *args, smem=(), flops=0):
    specs = [
        pl.BlockSpec(memory_space=pltpu.SMEM if i in smem else pltpu.VMEM) for i in range(len(args))
    ]
    return pl.pallas_call(
        kernel,
        out_shape=[jax.ShapeDtypeStruct(s, d) for s, d in outs],
        in_specs=specs,
        out_specs=[pl.BlockSpec(memory_space=pltpu.VMEM)] * len(outs),
        compiler_params=pltpu.CompilerParams(vmem_limit_bytes=40 * 1024 * 1024),
        cost_estimate=pl.CostEstimate(flops=flops, bytes_accessed=1 << 16, transcendentals=0),
    )(*args)


def spread_kernel(partner_ref, source_ref, scan_ref, order_ref, out_ref):
    turned = dot_nt(order_ref[...], scan_ref[...].reshape(256, 256))
    lane = lanes((8, 128))
    sub = lax.broadcasted_iota(jnp.int32, (8, 128), 0)
    group = lane // 32
    want = jnp.zeros((8, 128), F32)
    for e in range(EX):
        half, row = e // 8, e % 8
        tile = partner_ref[0, 0, e, 0].astype(F32)
        block = source_ref[0, 0, e].astype(F32)
        here = sub == row
        want = jnp.where(here & (group == 2 * half), tile, want)
        want = jnp.where(here & (group == 2 * half + 1), block, want)
    low = lane < 64
    for c in range(16):
        for v in range(2):
            a0 = turned[c * 16 : c * 16 + 8, v * 128 : v * 128 + 128]
            a1 = turned[c * 16 + 8 : c * 16 + 16, v * 128 : v * 128 + 128]
            p = c * 4 + v * 2
            even = jnp.where(low, a0, pltpu.roll(a1, 64, 1))
            odd = jnp.where(low, pltpu.roll(a0, 64, 1), a1)
            out_ref[p] = jnp.concatenate([even, want], axis=0).astype(BF16)
            out_ref[p + 1] = jnp.concatenate([odd, want], axis=0).astype(BF16)


def gather_kernel(in_ref, out_ref):
    seen = in_ref[...].astype(F32)
    table = seen[:, 0:8, :].reshape(512, 128).astype(BF16)
    want = seen[:, 8:16, :].reshape(512, 128)
    spot = lax.broadcasted_iota(jnp.int32, (512, 512), 1).astype(F32)
    lane = lanes((512, 128))
    halves_out = []
    for half in range(2):
        tile = want[:, half * 64 : half * 64 + 1]
        block = want[:, half * 64 + 32 : half * 64 + 33]
        upper = block >= 8.0
        key = tile * 8.0 + jnp.where(upper, block - 8.0, block)
        pick = jnp.where(spot == key, 1.0, 0.0).astype(BF16)
        found = dot(pick, table)
        swapped = pltpu.roll(found, 64, 1)
        if half == 0:
            halves_out.append(jnp.where(upper, swapped, found))
        else:
            halves_out.append(jnp.where(upper, found, swapped))
    out_ref[...] = jnp.where(lane < 64, halves_out[0], halves_out[1]).astype(BF16)


def sides_kernel(idx_ref, scan_ref, lo_ref, hi_ref, pick_ref, up_ref, down_ref):
    gz = idx_ref[0]
    zero = jnp.zeros((32, 256), BF16)
    lo = jnp.where(gz > 0, lo_ref[...].reshape(32, 256), zero)
    hi = jnp.where(gz < idx_ref[2] - 1, hi_ref[...].reshape(32, 256), zero)
    rows = jnp.concatenate([scan_ref[...].reshape(256, 256), lo, hi], axis=0)
    out = dot(pick_ref[...], rows).astype(BF16)
    up_ref[...] = out[0:48]
    down_ref[...] = out[48:96]


def slopes_kernel(
    idx_ref, scan_ref, zlo_ref, zhi_ref, ylo_ref, yhi_ref, cols_ref, order_ref, ph_ref, pl_ref,
    qh_ref, ql_ref, lh_ref, ll_ref, ch_ref, cl_ref, clin_ref, slope_ref, ref_ref, hess_ref, lump_ref,
):
    gz, gy = idx_ref[0], idx_ref[1]
    scan = scan_ref[...].reshape(256, 256)
    z32 = jnp.zeros((32, 256), BF16)
    z48 = jnp.zeros((48, 256), BF16)
    sides = jnp.concatenate(
        [
            jnp.where(gz > 0, zlo_ref[...].reshape(32, 256), z32),
            jnp.where(gz < idx_ref[2] - 1, zhi_ref[...].reshape(32, 256), z32),
            jnp.where(gy > 0, ylo_ref[...], z48),
            jnp.where(gy < idx_ref[3] - 1, yhi_ref[...], z48),
        ],
        axis=0,
    )
    ref_ref[...] = dot_nt(order_ref[...], scan).astype(BF16)
    mid = dot_nt(cols_ref[...], scan)
    rim = dot_nt(cols_ref[...], sides)
    smooth = (mid[0:256] + mid[256:512], rim[0:256] + rim[256:512])
    slope = (mid[512:768] + mid[768:1024], rim[512:768] + rim[768:1024])

    def plane(parts, lo, hi):
        return dot3(parts[0], ph_ref[0:256, lo:hi], pl_ref[0:256, lo:hi]) + dot3(
            parts[1], ph_ref[256:416, lo:hi], pl_ref[256:416, lo:hi]
        )

    g01 = plane(smooth, 0, 512)
    g2 = plane(slope, 512, 768)
    rounded = [g01[:, 0:256].astype(BF16), g01[:, 256:512].astype(BF16), g2.astype(BF16)]
    for a in range(3):
        slope_ref[:, a * 256 : a * 256 + 256] = rounded[a]
    g = [v.astype(F32) for v in rounded]
    total = jnp.zeros((256, 256), F32)
    for i, (a, b) in enumerate(PAIRS):
        at = slice(i * 256, i * 256 + 256)
        total = total + dot3(g[a] * g[b], qh_ref[at, :], ql_ref[at, :])
    turned = total.T
    hess_ref[...] = dot3(turned, ch_ref[...], cl_ref[...])[0:192]
    mags = [jnp.abs(v) for v in g]
    whole = mags[0] + mags[1] + mags[2]
    lump = jnp.zeros((256, 128), F32)
    for a in range(3):
        at = slice(a * 256, a * 256 + 256)
        lump = lump + dot3(mags[a] * whole, lh_ref[at, :], ll_ref[at, :])
    lh, ll = halves(lump.T)
    lin = clin_ref[:, 0:128]
    lump_ref[...] = (dot(lh, lin) + dot(ll, lin))[0:16]


def forcing_kernel(
    moved_ref, ref_ref, slope_ref, lump_ref, lh_ref, ll_ref, clin_ref, n0_ref, n1_ref, elem_ref, diff_ref
):
    low = lanes((8, 128)) < 64
    for c in range(16):
        for v in range(2):
            p = (c * 4 + v * 2) * 8
            both = moved_ref[p : p + 16, :].astype(F32)
            m0, m1 = both[0:8], both[8:16]
            diff_ref[c * 16 : c * 16 + 8, v * 128 : v * 128 + 128] = jnp.where(
                low, m0, pltpu.roll(m1, 64, 1)
            )
            diff_ref[c * 16 + 8 : c * 16 + 16, v * 128 : v * 128 + 128] = jnp.where(
                low, pltpu.roll(m0, 64, 1), m1
            )
    diff = ref_ref[...].astype(F32) - diff_ref[...]
    total = dot3(diff * diff, lh_ref[768:1024, :], ll_ref[768:1024, :])
    for a in range(3):
        at = slice(a * 256, a * 256 + 256)
        total = total + dot3(slope_ref[:, at].astype(F32) * diff, lh_ref[at, :], ll_ref[at, :])
    h, l = halves(total.T)
    out = (dot(h, clin_ref[...]) + dot(l, clin_ref[...]))[0:16]
    elem_ref[...] = out[:, 128:256]
    nodes = out[:, 0:128] + pltpu.roll(lump_ref[...], 64, 1)
    n0_ref[...] = nodes[0:8]
    n1_ref[...] = nodes[8:16]


def layers_kernel(idx_ref, n0_ref, n1_ref, lo_ref, hi_ref, left_ref, right_ref):
    gz = idx_ref[0]
    t0 = n0_ref[...] + jnp.where(gz > 0, lo_ref[...], 0.0)
    t1 = n1_ref[...] + jnp.where(gz < idx_ref[2] - 1, hi_ref[...], 0.0)
    left_ref[...] = jnp.concatenate([t0[0:4], t1[0:4]], axis=0)
    right_ref[...] = jnp.concatenate([t0[4:8], t1[4:8]], axis=0)


def apply_hessian(hess_ref, nodes):
    lane = lanes((16, 128))
    pair = jnp.where(lane < 16, nodes, pltpu.roll(nodes, 15, 1))
    spread = jnp.where(lane < 32, pair, pltpu.roll(pair, 32, 1))
    out = jnp.zeros((16, 128), F32)
    for hh in range(2):
        for ll in range(2):
            for b in range(3):
                row = hh * 8 + ll * 4 + b
                blk = ((hh * 2 + ll) * 3 + b) * 16
                out = out + hess_ref[blk : blk + 16, :] * spread[row : row + 1, :]
    return out + pltpu.roll(out, 128 - 16, 1)


def to_nodes(pushed):
    lane = lanes((16, 128))
    first = jnp.where(lane < 16, pushed, 0.0)
    second = jnp.where((lane >= 1) & (lane < 17), pltpu.roll(pushed, 128 - 31, 1), 0.0)
    return first + second


def totals(idx_ref, left_ref, right_ref, fl_ref, fr_ref):
    gy = idx_ref[1]
    left = left_ref[...] + jnp.where(gy > 0, fl_ref[...], 0.0)
    right = right_ref[...] + jnp.where(gy < idx_ref[3] - 1, fr_ref[...], 0.0)
    return jnp.concatenate([left[0:4], right[0:4], left[4:8], right[4:8]], axis=0)


def free_nodes(idx_ref):
    sub = lax.broadcasted_iota(jnp.int32, (16, 128), 0)
    lane = lanes((16, 128))
    held = ((sub >= 8) & (idx_ref[0] == idx_ref[2] - 1)) | (
        ((sub // 4) % 2 == 1) & (idx_ref[1] == idx_ref[3] - 1)
    )
    return jnp.logical_not(held | (lane >= 17) | (sub % 4 == 3))


def first_kernel(
    idx_ref, left_ref, right_ref, fl_ref, fr_ref, force_ref, hess_ref, u_ref, d_ref, n0_ref, n1_ref
):
    summed = totals(idx_ref, left_ref, right_ref, fl_ref, fr_ref)
    diag = pltpu.roll(summed, 64, 1) + 1.0
    u = jnp.where(free_nodes(idx_ref), summed / diag, 0.0)
    u_ref[...] = u
    d_ref[...] = diag
    nodes = force_ref[...] - to_nodes(apply_hessian(hess_ref, u))
    n0_ref[...] = nodes[0:8]
    n1_ref[...] = nodes[8:16]


def step(idx_ref, left_ref, right_ref, fl_ref, fr_ref, u_ref, d_ref):
    summed = totals(idx_ref, left_ref, right_ref, fl_ref, fr_ref)
    u = u_ref[...]
    return jnp.where(free_nodes(idx_ref), u + (summed - u) / d_ref[...], 0.0)


def next_kernel(
    idx_ref, left_ref, right_ref, fl_ref, fr_ref, u_in, d_ref, force_ref, hess_ref, u_ref, n0_ref, n1_ref
):
    u = step(idx_ref, left_ref, right_ref, fl_ref, fr_ref, u_in, d_ref)
    u_ref[...] = u
    nodes = force_ref[...] - to_nodes(apply_hessian(hess_ref, u))
    n0_ref[...] = nodes[0:8]
    n1_ref[...] = nodes[8:16]


def last_kernel(
    idx_ref, left_ref, right_ref, fl_ref, fr_ref, u_in, d_ref, elem_ref, hess_ref, disp_ref, mis_ref
):
    u = step(idx_ref, left_ref, right_ref, fl_ref, fr_ref, u_in, d_ref)
    for a in range(3):
        disp_ref[a, 0] = u[a : a + 1, 0:17]
    lane = lanes((16, 128))
    sub = lax.broadcasted_iota(jnp.int32, (16, 128), 0)
    pushed = apply_hessian(hess_ref, u)
    corner = jnp.where(lane < 32, u, pltpu.roll(u, 31, 1))
    elem = elem_ref[...]
    term = jnp.where(sub % 4 == 3, elem, corner * (pushed - 2.0 * elem))
    term = jnp.where((lane < 16) | ((lane >= 32) & (lane < 48)), term, 0.0)
    row = jnp.sum(term, axis=0, keepdims=True)
    row = jnp.broadcast_to(row, (8, 128))
    row = (row + pltpu.roll(row, 128 - 32, 1)) / ES**3
    mis_ref[0] = row[0:1, 0:16]


def shift(value, axis, by):
    count = lax.axis_size(axis)
    return lax.ppermute(value, axis, [(i, (i + by) % count) for i in range(count)])


def body(reference_scan, loaded_scan, partner, source):
    cols, order = column_filter()
    plane_h, plane_l = plane_filter()
    quad_h, quad_l, lin_h, lin_l = plane_weights()
    col_h, col_l, col_lin = column_weights()
    idx = jnp.stack(
        [lax.axis_index("gz"), lax.axis_index("gy"), lax.axis_size("gz"), lax.axis_size("gy")]
    ).astype(jnp.int32)
    (outgoing,) = call(
        spread_kernel, [((64, 16, 128), BF16)], partner, source, loaded_scan, order, smem=(0, 1)
    )
    pieces = lax.all_to_all(outgoing, "gy", split_axis=0, concat_axis=0, tiled=True)
    zlo = shift(reference_scan[14:16], "gz", 1)
    zhi = shift(reference_scan[0:2], "gz", -1)
    up, down = call(
        sides_kernel, [((48, 256), BF16)] * 2, idx, reference_scan, zlo, zhi, side_rows(), smem=(0,)
    )
    ylo = shift(up, "gy", 1)
    yhi = shift(down, "gy", -1)
    (found,) = call(gather_kernel, [((512, 128), BF16)], pieces)
    moved = lax.all_to_all(found.reshape(64, 8, 128), "gy", split_axis=0, concat_axis=0, tiled=True)
    slopes, turned, hess, lump = call(
        slopes_kernel,
        [((256, 768), BF16), ((256, 256), BF16), ((192, 128), F32), ((16, 128), F32)],
        idx, reference_scan, zlo, zhi, ylo, yhi, cols, order, plane_h, plane_l,
        quad_h, quad_l, lin_h, lin_l, col_h, col_l, col_lin,
        smem=(0,),
        flops=4_000_000_000,
    )
    n0, n1, elem = pl.pallas_call(
        forcing_kernel,
        out_shape=[
            jax.ShapeDtypeStruct((8, 128), F32),
            jax.ShapeDtypeStruct((8, 128), F32),
            jax.ShapeDtypeStruct((16, 128), F32),
        ],
        scratch_shapes=[pltpu.VMEM((256, 256), F32)],
        compiler_params=pltpu.CompilerParams(vmem_limit_bytes=40 * 1024 * 1024),
    )(moved.reshape(512, 128), turned, slopes, lump, lin_h, lin_l, col_lin)
    force = jnp.concatenate([n0, n1])
    disp = mis = u = diag = None
    for iteration in range(ITERS):
        lo = shift(n1, "gz", 1)
        hi = shift(n0, "gz", -1)
        left, right = call(
            layers_kernel, [((8, 128), F32)] * 2, idx, n0, n1, lo, hi, smem=(0,)
        )
        fl = shift(right, "gy", 1)
        fr = shift(left, "gy", -1)
        edge = (idx, left, right, fl, fr)
        state = ((16, 128), F32)
        half = ((8, 128), F32)
        if iteration == 0:
            u, diag, n0, n1 = call(
                first_kernel, [state, state, half, half], *edge, force, hess, smem=(0,)
            )
        elif iteration < ITERS - 1:
            u, n0, n1 = call(
                next_kernel, [state, half, half], *edge, u, diag, force, hess, smem=(0,)
            )
        else:
            disp, mis = call(
                last_kernel, [((3, 1, 1, 17), F32), ((1, 1, 16), F32)], *edge, u, diag, elem, hess, smem=(0,)
            )
    return disp, mis


def solution(mesh):
    return jax.shard_map(
        body,
        mesh=mesh,
        in_specs=(
            P("gz", "gy", None),
            P("gz", "gy", None),
            P("gz", "gy", None, None),
            P("gz", "gy", None),
        ),
        out_specs=(P(None, "gz", "gy", None), P("gz", "gy", None)),
        check_vma=False,
    )
```

profile of v0, /device:TPU:1, one launch (start us, length us, event | category | flops | bytes accessed | tf_op | source)
XLA Modules:
  0.0 130.7 jit_solution(12711072047559830906)
XLA Ops:
  0.6 0.0 copy-start.8
  0.6 0.7 copy.18.partner_ref
  1.4 0.0 copy-done.8
  1.4 0.9 copy-done.3
  2.3 0.9 copy-done.5
  3.2 1.0 shard_map.167
  4.2 0.0 copy-start.7
  4.2 0.0 copy-start.15
  4.2 38.3 %all_to_all.10.in_ref = bf16[64,16,128]{2,1,0:T(8,128)(2,1)S(1)} all-to-all(bf16[64,16,128]{2,1,0:T(8,128)(2,1)S(1)} %shard_map.167), channel_id=1, replica_groups=mesh['gz'=8,'gy'=64] {'gy'}, dimensions={0} | all-to-all | bytes 524288 | tf_op jit(solution)/shard_map/all_to_all | solution.py:410
  42.5 1.3 %shard_map.168 = bf16[512,128]{1,0:T(8,128)(2,1)} custom-call(bf16[64,16,128]{2,1,0:T(8,128)(2,1)S(1)} %all_to_all.10.in_ref), custom_call_target="tpu_custom_call" | custom-call | bytes 65536 | tf_op jit(solution)/shard_map/pallas_call | solution.py:154
  43.8 7.7 %all-to-all-start.1 = ((bf16[64,8,128]{2,1,0:T(8,128)(2,1)}), bf16[64,8,128]{2,1,0:T(8,128)(2,1)S(1)}, u32[]{:S(2)}, u32[]{:S(2)}) async-start(bf16[64,8,128]{2,1,0:T(8,128)(2,1)} %bitcast.2), calls=%async_computation.1 | async-start | bytes 262144 | tf_op jit(solution)/shard_map/all_to_all | solution.py:419
  51.5 0.0 copy-done.2
  51.6 1.7 %collective-permute-start.1 = (bf16[2,16,256]{2,1,0:T(8,128)(2,1)S(1)}, bf16[2,16,256]{2,1,0:T(8,128)(2,1)S(1)}, u32[]{:S(2)}, u32[]{:S(2)}) collective-permute-start(bf16[2,16,256]{2,1,0:T(8,128)(2,1)S(1)} %get-tuple-element.46), channel_id=1, source_target_pairs={{0,448},{64,0},{128,64},{192,128},{256,192},{320,256},{384,320},{4... | collective-permute-start | bytes 49160 | tf_op jit(solution)/shard_map/ppermute | solution.py:396
  53.3 1.1 collective-permute-start
  54.4 0.1 pad_add_fusion.idx_ref
  54.5 1.4 %collective-permute-done.1.hi_ref.zhi_ref = bf16[2,16,256]{2,1,0:T(8,128)(2,1)S(1)} collective-permute-done((bf16[2,16,256]{2,1,0:T(8,128)(2,1)S(1)}, bf16[2,16,256]{2,1,0:T(8,128)(2,1)S(1)}, u32[]{:S(2)}, u32[]{:S(2)}) %collective-permute-start.1) | collective-permute-done | bytes 16416 | tf_op jit(solution)/shard_map/ppermute | solution.py:396
  55.9 0.0 collective-permute-done.lo_ref.zlo_ref
  55.9 0.7 shard_map.169
  56.6 3.4 %collective-permute-start.2 = (bf16[48,256]{1,0:T(8,128)(2,1)S(1)}, bf16[48,256]{1,0:T(8,128)(2,1)S(1)}, u32[]{:S(2)}, u32[]{:S(2)}) collective-permute-start(bf16[48,256]{1,0:T(8,128)(2,1)S(1)} %get-tuple-element.24), channel_id=1, source_target_pairs={{0,1},{1,2},{2,3},{3,4},{4,5},{5,6},{6,7},{7,8},{8,9},{9,10},{10,1... | collective-permute-start | bytes 73736 | tf_op jit(solution)/shard_map/ppermute | solution.py:396
  60.0 5.6 %collective-permute-start.3 = (bf16[48,256]{1,0:T(8,128)(2,1)S(1)}, bf16[48,256]{1,0:T(8,128)(2,1)S(1)}, u32[]{:S(2)}, u32[]{:S(2)}) collective-permute-start(bf16[48,256]{1,0:T(8,128)(2,1)S(1)} %get-tuple-element.25), channel_id=1, source_target_pairs={{0,63},{1,0},{2,1},{3,2},{4,3},{5,4},{6,5},{7,6},{8,7},{9,8},{10,9... | collective-permute-start | bytes 73736 | tf_op jit(solution)/shard_map/ppermute | solution.py:396
  65.6 0.0 collective-permute-done.2.ylo_ref
  65.6 0.9 collective-permute-done.3.yhi_ref
  66.5 0.0 copy-done.9
  66.5 0.0 copy-done
  66.6 0.0 copy-done.1
  66.6 0.0 copy-done.14
  66.6 0.0 copy-start.10
  66.6 1.1 copy-done.10
  67.7 1.1 copy-done.11
  68.8 1.1 copy-done.12
  69.9 1.0 copy-done.13
  70.9 4.0 %shard_map.170 = (bf16[256,768]{1,0:T(8,128)(2,1)S(1)}, bf16[256,256]{1,0:T(8,128)(2,1)S(1)}, f32[192,128]{1,0:T(8,128)S(1)}, f32[16,128]{1,0:T(8,128)S(1)}) custom-call(s32[4]{0:T(128)S(1)} %pad_add_fusion.idx_ref, bf16[16,16,256]{2,1,0:T(8,128)(2,1)S(1)} %copy-done.2, bf16[2,16,256]{2,1,0:T(8,128)(2,1)S(1)} %collective-permute-done.lo_ref.zlo_ref, ...), custom_call_target="tpu_custom_call" | custom-call | flops 4000000000 | bytes 65536 | tf_op jit(solution)/shard_map/pallas_call | solution.py:154
  74.9 0.0 all-to-all-done.1
  74.9 0.9 shard_map.171
  75.8 3.7 %collective-permute-start.5 = (f32[8,128]{1,0:T(8,128)S(1)}, f32[8,128]{1,0:T(8,128)S(1)}, u32[]{:S(2)}, u32[]{:S(2)}) collective-permute-start(f32[8,128]{1,0:T(8,128)S(1)} %get-tuple-element.29.n0_ref), channel_id=1, source_target_pairs={{0,448},{64,0},{128,64},{192,128},{256,192},{320,256},{384,320},{4... | collective-permute-start | bytes 12296 | tf_op jit(solution)/shard_map/ppermute | solution.py:396
  79.5 0.0 collective-permute-start.4
  79.5 0.8 collective-permute-done.5.hi_ref
  80.3 0.3 collective-permute-done.4.lo_ref
  80.7 0.5 shard_map.172
  81.2 7.3 %collective-permute-start.7 = (f32[8,128]{1,0:T(8,128)S(1)}, f32[8,128]{1,0:T(8,128)S(1)}, u32[]{:S(2)}, u32[]{:S(2)}) collective-permute-start(f32[8,128]{1,0:T(8,128)S(1)} %get-tuple-element.31.left_ref), channel_id=1, source_target_pairs={{0,63},{1,0},{2,1},{3,2},{4,3},{5,4},{6,5},{7,6},{8,7},{9,8},{10,9... | collective-permute-start | bytes 12296 | tf_op jit(solution)/shard_map/ppermute | solution.py:396
  88.5 1.9 %collective-permute-start.6 = (f32[8,128]{1,0:T(8,128)S(1)}, f32[8,128]{1,0:T(8,128)S(1)}, u32[]{:S(2)}, u32[]{:S(2)}) collective-permute-start(f32[8,128]{1,0:T(8,128)S(1)} %get-tuple-element.32.right_ref), channel_id=1, source_target_pairs={{0,1},{1,2},{2,3},{3,4},{4,5},{5,6},{6,7},{7,8},{8,9},{9,10},{10,1... | collective-permute-start | bytes 12296 | tf_op jit(solution)/shard_map/ppermute | solution.py:396
  90.4 0.0 collective-permute-done.7.fr_ref
  90.4 5.7 %collective-permute-done.6.fl_ref = f32[8,128]{1,0:T(8,128)S(1)} collective-permute-done((f32[8,128]{1,0:T(8,128)S(1)}, f32[8,128]{1,0:T(8,128)S(1)}, u32[]{:S(2)}, u32[]{:S(2)}) %collective-permute-start.6) | collective-permute-done | bytes 4128 | tf_op jit(solution)/shard_map/ppermute | solution.py:396
  96.2 0.9 shard_map.173
  97.1 4.5 %collective-permute-start.9 = (f32[8,128]{1,0:T(8,128)S(1)}, f32[8,128]{1,0:T(8,128)S(1)}, u32[]{:S(2)}, u32[]{:S(2)}) collective-permute-start(f32[8,128]{1,0:T(8,128)S(1)} %get-tuple-element.34.n0_ref), channel_id=1, source_target_pairs={{0,448},{64,0},{128,64},{192,128},{256,192},{320,256},{384,320},{4... | collective-permute-start | bytes 12296 | tf_op jit(solution)/shard_map/ppermute | solution.py:396
  101.6 0.0 collective-permute-start.8
  101.6 0.8 collective-permute-done.9.hi_ref
  102.4 0.3 collective-permute-done.8.lo_ref
  102.8 0.5 shard_map.174
  103.3 1.9 %collective-permute-start.11 = (f32[8,128]{1,0:T(8,128)S(1)}, f32[8,128]{1,0:T(8,128)S(1)}, u32[]{:S(2)}, u32[]{:S(2)}) collective-permute-start(f32[8,128]{1,0:T(8,128)S(1)} %get-tuple-element.36.left_ref), channel_id=1, source_target_pairs={{0,63},{1,0},{2,1},{3,2},{4,3},{5,4},{6,5},{7,6},{8,7},{9,8},{10,9... | collective-permute-start | bytes 12296 | tf_op jit(solution)/shard_map/ppermute | solution.py:396
  105.3 3.4 %collective-permute-start.10 = (f32[8,128]{1,0:T(8,128)S(1)}, f32[8,128]{1,0:T(8,128)S(1)}, u32[]{:S(2)}, u32[]{:S(2)}) collective-permute-start(f32[8,128]{1,0:T(8,128)S(1)} %get-tuple-element.37.right_ref), channel_id=1, source_target_pairs={{0,1},{1,2},{2,3},{3,4},{4,5},{5,6},{6,7},{7,8},{8,9},{9,10},{10,1... | collective-permute-start | bytes 12296 | tf_op jit(solution)/shard_map/ppermute | solution.py:396
  108.6 0.0 collective-permute-done.11.fr_ref
  108.6 4.3 %collective-permute-done.10.fl_ref = f32[8,128]{1,0:T(8,128)S(1)} collective-permute-done((f32[8,128]{1,0:T(8,128)S(1)}, f32[8,128]{1,0:T(8,128)S(1)}, u32[]{:S(2)}, u32[]{:S(2)}) %collective-permute-start.10) | collective-permute-done | bytes 4128 | tf_op jit(solution)/shard_map/ppermute | solution.py:396
  112.9 0.8 shard_map.175
  113.8 4.2 %collective-permute-start.13 = (f32[8,128]{1,0:T(8,128)S(1)}, f32[8,128]{1,0:T(8,128)S(1)}, u32[]{:S(2)}, u32[]{:S(2)}) collective-permute-start(f32[8,128]{1,0:T(8,128)S(1)} %get-tuple-element.40.n0_ref), channel_id=1, source_target_pairs={{0,448},{64,0},{128,64},{192,128},{256,192},{320,256},{384,320},{4... | collective-permute-start | bytes 12296 | tf_op jit(solution)/shard_map/ppermute | solution.py:396
  118.0 0.0 collective-permute-start.12
  118.0 0.8 collective-permute-done.13.hi_ref
  118.8 0.3 collective-permute-done.12.lo_ref
  119.2 0.5 shard_map.176
  119.7 1.9 %collective-permute-start.15 = (f32[8,128]{1,0:T(8,128)S(1)}, f32[8,128]{1,0:T(8,128)S(1)}, u32[]{:S(2)}, u32[]{:S(2)}) collective-permute-start(f32[8,128]{1,0:T(8,128)S(1)} %get-tuple-element.42.left_ref), channel_id=1, source_target_pairs={{0,63},{1,0},{2,1},{3,2},{4,3},{5,4},{6,5},{7,6},{8,7},{9,8},{10,9... | collective-permute-start | bytes 12296 | tf_op jit(solution)/shard_map/ppermute | solution.py:396
  121.7 3.4 %collective-permute-start.14 = (f32[8,128]{1,0:T(8,128)S(1)}, f32[8,128]{1,0:T(8,128)S(1)}, u32[]{:S(2)}, u32[]{:S(2)}) collective-permute-start(f32[8,128]{1,0:T(8,128)S(1)} %get-tuple-element.43.right_ref), channel_id=1, source_target_pairs={{0,1},{1,2},{2,3},{3,4},{4,5},{5,6},{6,7},{7,8},{8,9},{9,10},{10,1... | collective-permute-start | bytes 12296 | tf_op jit(solution)/shard_map/ppermute | solution.py:396
  125.0 0.0 collective-permute-done.15.fr_ref
  125.0 4.3 %collective-permute-done.14.fl_ref = f32[8,128]{1,0:T(8,128)S(1)} collective-permute-done((f32[8,128]{1,0:T(8,128)S(1)}, f32[8,128]{1,0:T(8,128)S(1)}, u32[]{:S(2)}, u32[]{:S(2)}) %collective-permute-start.14) | collective-permute-done | bytes 4128 | tf_op jit(solution)/shard_map/ppermute | solution.py:396
  129.3 1.4 %shard_map.177 = (f32[3,1,1,17]{3,2,1,0:T(1,128)}, f32[1,1,16]{2,1,0:T(1,128)}) custom-call(s32[4]{0:T(128)S(1)} %pad_add_fusion.idx_ref, f32[8,128]{1,0:T(8,128)S(1)} %get-tuple-element.42.left_ref, f32[8,128]{1,0:T(8,128)S(1)} %get-tuple-element.43.right_ref, f32[8,128]{1,0:T(8,128)S(1)} %collective-permute-done.14.fl_ref, ...), custom_call_target="tpu_custom_call" | custom-call | bytes 65536 | tf_op jit(solution)/shard_map/pallas_call | solution.py:154
  (19 shorter events, 0.0 us)
Async XLA Ops:
  0.6 0.8 copy-start.8
  1.4 0.9 copy-start.3
  2.3 0.9 copy-start.5
  3.2 63.3 %copy-start.9 = (bf16[1536,256]{1,0:T(8,128)(2,1)S(1)}, bf16[1536,256]{1,0:T(8,128)(2,1)}, u32[]{:S(2)}) copy-start(bf16[1536,256]{1,0:T(8,128)(2,1)} %constant.43.clone.ql_ref) | copy-start | bytes 2359300
  4.2 51.7 %copy-start.7 = (bf16[96,320]{1,0:T(8,128)(2,1)S(1)}, bf16[96,320]{1,0:T(8,128)(2,1)}, u32[]{:S(2)}) copy-start(bf16[96,320]{1,0:T(8,128)(2,1)} %constant.38.clone.pick_ref) | copy-start | bytes 184324
  4.2 62.4 %copy-start.15 = (bf16[256,128]{1,0:T(8,128)(2,1)S(1)}, bf16[256,128]{1,0:T(8,128)(2,1)}, u32[]{:S(2)}) copy-start(bf16[256,128]{1,0:T(8,128)(2,1)} %constant.46.clone.ch_ref) | copy-start | bytes 196612
  42.5 9.1 %copy-start.2 = (bf16[16,16,256]{2,1,0:T(8,128)(2,1)S(1)}, bf16[16,16,256]{2,1,0:T(8,128)(2,1)}, u32[]{:S(2)}) copy-start(bf16[16,16,256]{2,1,0:T(8,128)(2,1)} %scan_ref.5) | copy-start | bytes 393220
  42.5 24.1 %copy-start.4 = (bf16[256,256]{1,0:T(8,128)(2,1)S(1)}, bf16[256,256]{1,0:T(8,128)(2,1)}, u32[]{:S(2)}) copy-start(bf16[256,256]{1,0:T(8,128)(2,1)} %constant.48.clone.clin_ref) | copy-start | bytes 393220
  42.5 24.1 %copy-start.6 = (bf16[256,256]{1,0:T(8,128)(2,1)S(1)}, bf16[256,256]{1,0:T(8,128)(2,1)}, u32[]{:S(2)}) copy-start(bf16[256,256]{1,0:T(8,128)(2,1)} %constant.37.clone.order_ref) | copy-start | bytes 393220
  43.8 22.7 %copy-start = (bf16[1024,128]{1,0:T(8,128)(2,1)S(1)}, bf16[1024,128]{1,0:T(8,128)(2,1)}, u32[]{:S(2)}) copy-start(bf16[1024,128]{1,0:T(8,128)(2,1)} %constant.45.clone.ll_ref) | copy-start | bytes 786436
  43.8 22.7 %copy-start.1 = (bf16[1024,128]{1,0:T(8,128)(2,1)S(1)}, bf16[1024,128]{1,0:T(8,128)(2,1)}, u32[]{:S(2)}) copy-start(bf16[1024,128]{1,0:T(8,128)(2,1)} %constant.44.clone.lh_ref) | copy-start | bytes 786436
  43.8 31.1 %all-to-all-start.1 = ((bf16[64,8,128]{2,1,0:T(8,128)(2,1)}), bf16[64,8,128]{2,1,0:T(8,128)(2,1)S(1)}, u32[]{:S(2)}, u32[]{:S(2)}) async-start(bf16[64,8,128]{2,1,0:T(8,128)(2,1)} %bitcast.2), calls=%async_computation.1 | async-start | bytes 262144 | tf_op jit(solution)/shard_map/all_to_all | solution.py:419
  51.6 4.3 %collective-permute-start.1 = (bf16[2,16,256]{2,1,0:T(8,128)(2,1)S(1)}, bf16[2,16,256]{2,1,0:T(8,128)(2,1)S(1)}, u32[]{:S(2)}, u32[]{:S(2)}) collective-permute-start(bf16[2,16,256]{2,1,0:T(8,128)(2,1)S(1)} %get-tuple-element.46), channel_id=1, source_target_pairs={{0,448},{64,0},{128,64},{192,128},{256,192},{320,256},{384,320},{4... | collective-permute-start | bytes 49160 | tf_op jit(solution)/shard_map/ppermute | solution.py:396
  53.3 2.6 %collective-permute-start = (bf16[2,16,256]{2,1,0:T(8,128)(2,1)S(1)}, bf16[2,16,256]{2,1,0:T(8,128)(2,1)S(1)}, u32[]{:S(2)}, u32[]{:S(2)}) collective-permute-start(bf16[2,16,256]{2,1,0:T(8,128)(2,1)S(1)} %get-tuple-element.47), channel_id=1, source_target_pairs={{0,64},{64,128},{128,192},{192,256},{256,320},{320,384},{384,448},... | collective-permute-start | bytes 49160 | tf_op jit(solution)/shard_map/ppermute | solution.py:396
  54.5 12.1 %copy-start.14 = (bf16[256,128]{1,0:T(8,128)(2,1)S(1)}, bf16[256,128]{1,0:T(8,128)(2,1)}, u32[]{:S(2)}) copy-start(bf16[256,128]{1,0:T(8,128)(2,1)} %constant.47.clone.cl_ref) | copy-start | bytes 196612
  56.6 9.0 %collective-permute-start.2 = (bf16[48,256]{1,0:T(8,128)(2,1)S(1)}, bf16[48,256]{1,0:T(8,128)(2,1)S(1)}, u32[]{:S(2)}, u32[]{:S(2)}) collective-permute-start(bf16[48,256]{1,0:T(8,128)(2,1)S(1)} %get-tuple-element.24), channel_id=1, source_target_pairs={{0,1},{1,2},{2,3},{3,4},{4,5},{5,6},{6,7},{7,8},{8,9},{9,10},{10,1... | collective-permute-start | bytes 73736 | tf_op jit(solution)/shard_map/ppermute | solution.py:396
  60.0 6.5 %collective-permute-start.3 = (bf16[48,256]{1,0:T(8,128)(2,1)S(1)}, bf16[48,256]{1,0:T(8,128)(2,1)S(1)}, u32[]{:S(2)}, u32[]{:S(2)}) collective-permute-start(bf16[48,256]{1,0:T(8,128)(2,1)S(1)} %get-tuple-element.25), channel_id=1, source_target_pairs={{0,63},{1,0},{2,1},{3,2},{4,3},{5,4},{6,5},{7,6},{8,7},{9,8},{10,9... | collective-permute-start | bytes 73736 | tf_op jit(solution)/shard_map/ppermute | solution.py:396
  66.6 1.1 copy-start.10
  67.7 1.1 copy-start.11
  68.8 1.1 copy-start.12
  69.9 1.0 copy-start.13
  75.8 4.5 %collective-permute-start.5 = (f32[8,128]{1,0:T(8,128)S(1)}, f32[8,128]{1,0:T(8,128)S(1)}, u32[]{:S(2)}, u32[]{:S(2)}) collective-permute-start(f32[8,128]{1,0:T(8,128)S(1)} %get-tuple-element.29.n0_ref), channel_id=1, source_target_pairs={{0,448},{64,0},{128,64},{192,128},{256,192},{320,256},{384,320},{4... | collective-permute-start | bytes 12296 | tf_op jit(solution)/shard_map/ppermute | solution.py:396
  79.5 1.2 collective-permute-start.4
  81.2 9.2 %collective-permute-start.7 = (f32[8,128]{1,0:T(8,128)S(1)}, f32[8,128]{1,0:T(8,128)S(1)}, u32[]{:S(2)}, u32[]{:S(2)}) collective-permute-start(f32[8,128]{1,0:T(8,128)S(1)} %get-tuple-element.31.left_ref), channel_id=1, source_target_pairs={{0,63},{1,0},{2,1},{3,2},{4,3},{5,4},{6,5},{7,6},{8,7},{9,8},{10,9... | collective-permute-start | bytes 12296 | tf_op jit(solution)/shard_map/ppermute | solution.py:396
  88.5 7.7 %collective-permute-start.6 = (f32[8,128]{1,0:T(8,128)S(1)}, f32[8,128]{1,0:T(8,128)S(1)}, u32[]{:S(2)}, u32[]{:S(2)}) collective-permute-start(f32[8,128]{1,0:T(8,128)S(1)} %get-tuple-element.32.right_ref), channel_id=1, source_target_pairs={{0,1},{1,2},{2,3},{3,4},{4,5},{5,6},{6,7},{7,8},{8,9},{9,10},{10,1... | collective-permute-start | bytes 12296 | tf_op jit(solution)/shard_map/ppermute | solution.py:396
  97.1 5.4 %collective-permute-start.9 = (f32[8,128]{1,0:T(8,128)S(1)}, f32[8,128]{1,0:T(8,128)S(1)}, u32[]{:S(2)}, u32[]{:S(2)}) collective-permute-start(f32[8,128]{1,0:T(8,128)S(1)} %get-tuple-element.34.n0_ref), channel_id=1, source_target_pairs={{0,448},{64,0},{128,64},{192,128},{256,192},{320,256},{384,320},{4... | collective-permute-start | bytes 12296 | tf_op jit(solution)/shard_map/ppermute | solution.py:396
  101.6 1.2 collective-permute-start.8
  103.3 5.3 %collective-permute-start.11 = (f32[8,128]{1,0:T(8,128)S(1)}, f32[8,128]{1,0:T(8,128)S(1)}, u32[]{:S(2)}, u32[]{:S(2)}) collective-permute-start(f32[8,128]{1,0:T(8,128)S(1)} %get-tuple-element.36.left_ref), channel_id=1, source_target_pairs={{0,63},{1,0},{2,1},{3,2},{4,3},{5,4},{6,5},{7,6},{8,7},{9,8},{10,9... | collective-permute-start | bytes 12296 | tf_op jit(solution)/shard_map/ppermute | solution.py:396
  105.3 7.7 %collective-permute-start.10 = (f32[8,128]{1,0:T(8,128)S(1)}, f32[8,128]{1,0:T(8,128)S(1)}, u32[]{:S(2)}, u32[]{:S(2)}) collective-permute-start(f32[8,128]{1,0:T(8,128)S(1)} %get-tuple-element.37.right_ref), channel_id=1, source_target_pairs={{0,1},{1,2},{2,3},{3,4},{4,5},{5,6},{6,7},{7,8},{8,9},{9,10},{10,1... | collective-permute-start | bytes 12296 | tf_op jit(solution)/shard_map/ppermute | solution.py:396
  113.8 5.1 %collective-permute-start.13 = (f32[8,128]{1,0:T(8,128)S(1)}, f32[8,128]{1,0:T(8,128)S(1)}, u32[]{:S(2)}, u32[]{:S(2)}) collective-permute-start(f32[8,128]{1,0:T(8,128)S(1)} %get-tuple-element.40.n0_ref), channel_id=1, source_target_pairs={{0,448},{64,0},{128,64},{192,128},{256,192},{320,256},{384,320},{4... | collective-permute-start | bytes 12296 | tf_op jit(solution)/shard_map/ppermute | solution.py:396
  118.0 1.2 collective-permute-start.12
  119.7 5.3 %collective-permute-start.15 = (f32[8,128]{1,0:T(8,128)S(1)}, f32[8,128]{1,0:T(8,128)S(1)}, u32[]{:S(2)}, u32[]{:S(2)}) collective-permute-start(f32[8,128]{1,0:T(8,128)S(1)} %get-tuple-element.42.left_ref), channel_id=1, source_target_pairs={{0,63},{1,0},{2,1},{3,2},{4,3},{5,4},{6,5},{7,6},{8,7},{9,8},{10,9... | collective-permute-start | bytes 12296 | tf_op jit(solution)/shard_map/ppermute | solution.py:396
  121.7 7.7 %collective-permute-start.14 = (f32[8,128]{1,0:T(8,128)S(1)}, f32[8,128]{1,0:T(8,128)S(1)}, u32[]{:S(2)}, u32[]{:S(2)}) collective-permute-start(f32[8,128]{1,0:T(8,128)S(1)} %get-tuple-element.43.right_ref), channel_id=1, source_target_pairs={{0,1},{1,2},{2,3},{3,4},{4,5},{5,6},{6,7},{7,8},{8,9},{9,10},{10,1... | collective-permute-start | bytes 12296 | tf_op jit(solution)/shard_map/ppermute | solution.py:396
where the time goes:
time: 132 us; the launch traced here: 131 us
  starting transfers between devices  51.8 us (39%)
  blocking collectives  38.3 us (29%)
  waiting for transfers between devices  20.1 us (15%)
  Pallas kernels  12.6 us (10%)
  local copies, waits for them, and re-layouts  6.93 us (5%)
    ppermute x16, starting transfers between devices, shift(): lax.ppermute(value, axis, [(i, (i + by) % count) for i in range(count)])  44.1 us
    all_to_all x1, blocking collectives, body(): lax.all_to_all(outgoing, 'gy', split_axis=0, concat_axis=0, tiled=True)  38.3 us
    ppermute x16, waiting for transfers between devices, shift(): lax.ppermute(value, axis, [(i, (i + by) % count) for i in range(count)])  20.1 us
    pallas_call x10, Pallas kernels, call(): pl.pallas_call(kernel, out_shape=[jax.ShapeDtypeStruct(s, d) for s, d in...  11.7 us
    all_to_all x1, starting transfers between devices, body(): lax.all_to_all(found.reshape(64, 8, 128), 'gy', split_axis=0, concat_axis...  7.72 us
    unnamed x34, local copies, waits for them, and re-layouts  6.92 us
  transfers between devices with their start and end apart: 17, of which 11 were waited for; matrix products, arithmetic and copies ran while one was open for 0% of the time, Pallas kernels for 4%

commit v1 on v0

v1 whole, which is shorter than its diff:
```python
import jax
import jax.numpy as jnp
import numpy as np
import ml_dtypes
from jax import lax
from jax.experimental import pallas as pl
from jax.experimental.pallas import tpu as pltpu
from jax.sharding import PartitionSpec as P

ES = 16
EX = 16
NXC = 256
ITERS = 3
SMOOTH = (0.03032, 0.249724, 0.439911, 0.249724, 0.03032)
DERIVATIVE = (-0.10455, -0.292315, 0.0, 0.292315, 0.10455)
PAIRS = ((0, 0), (0, 1), (0, 2), (1, 1), (1, 2), (2, 2))
F32 = jnp.float32
BF16 = jnp.bfloat16


def split(table):
    table = np.asarray(table, np.float64)
    high = table.astype(np.float32).astype(ml_dtypes.bfloat16)
    low = (table - high.astype(np.float64)).astype(np.float32).astype(ml_dtypes.bfloat16)
    return high, low


def column_filter():
    row = np.arange(NXC)
    place = (row % EX) * ES + row // EX
    smooth = np.zeros((NXC, NXC))
    slope = np.zeros((NXC, NXC))
    for k in range(-2, 3):
        at = place + k
        ok = (at >= 0) & (at < NXC)
        smooth[row[ok], at[ok]] = SMOOTH[k + 2]
        slope[row[ok], at[ok]] = DERIVATIVE[k + 2]
    sh, sl = split(smooth)
    dh, dl = split(slope)
    return np.concatenate([sh, sl, dh, dl])


def plane_filter():
    zs, ys, real = [], [], []
    for z in range(16):
        for y in range(16):
            zs.append(z), ys.append(y), real.append(1)
    for z in (-2, -1, 16, 17):
        for y in range(16):
            zs.append(z), ys.append(y), real.append(1)
    for side in (-2, 16):
        for z in range(-2, 18):
            for j in range(2):
                zs.append(z), ys.append(side + j), real.append(1)
        for _ in range(8):
            zs.append(0), ys.append(0), real.append(0)
    zs, ys, real = np.array(zs), np.array(ys), np.array(real)
    zo, yo = np.arange(256) // 16, np.arange(256) % 16
    dz, dy = zs[:, None] - zo[None], ys[:, None] - yo[None]

    def tap(kernel, d):
        return np.where(np.abs(d) <= 2, np.array(kernel)[np.clip(d, -2, 2) + 2], 0.0)

    ok = real[:, None]
    depth = ok * tap(DERIVATIVE, dz) * tap(SMOOTH, dy)
    rows = ok * tap(SMOOTH, dz) * tap(DERIVATIVE, dy)
    both = ok * tap(SMOOTH, dz) * tap(SMOOTH, dy)
    return split(np.concatenate([depth, rows, both], axis=1))


def linear(t, side):
    w = (t + 0.5) / ES
    return w if side else 1.0 - w


def plane_weights():
    z, y = np.arange(256) // 16, np.arange(256) % 16
    quad = np.zeros((6, 256, 128))
    lin = np.zeros((4, 256, 128))
    square = lambda t, m: linear(t, m > 1) * linear(t, m > 0)
    for mz in range(3):
        for my in range(3):
            for ch in range(6):
                quad[ch, :, ch * 9 + mz * 3 + my] = square(z, mz) * square(y, my)
    for a in range(3):
        for h in range(2):
            for l in range(2):
                lin[a, :, a * 4 + h * 2 + l] = linear(z, h) * linear(y, l)
    lin[3, :, 12] = 1.0
    return split(quad.reshape(1536, 128)) + split(lin.reshape(1024, 128))


def column_weights():
    row = np.arange(256)
    c, ex = row // EX, row % EX
    quad = np.zeros((256, 128))
    lin = np.zeros((256, 256))
    for f in range(2):
        np.add.at(lin, (row, ex + f), linear(c, f))
        lin[row, 128 + f * 32 + ex] = linear(c, f)
        for ff in range(2):
            quad[row, f * 32 + ff * 16 + ex] = linear(c, f) * linear(c, ff)
    qh, ql = split(quad)
    return qh, ql, lin.astype(ml_dtypes.bfloat16)


def side_rows():
    pick = np.zeros((96, 320))
    for side in range(2):
        for zz in range(20):
            for j in range(2):
                y = (14 if side == 0 else 0) + j
                if zz < 2:
                    at = 256 + zz * 16 + y
                elif zz < 18:
                    at = (zz - 2) * 16 + y
                else:
                    at = 288 + (zz - 18) * 16 + y
                pick[side * 48 + zz * 2 + j, at] = 1.0
    return pick.astype(ml_dtypes.bfloat16)


def dot(a, b):
    return jnp.dot(a, b, preferred_element_type=F32)


def dot_nt(a, b):
    return lax.dot_general(a, b, (((1,), (1,)), ((), ())), preferred_element_type=F32)


def halves(v):
    high = v.astype(BF16)
    return high, (v - high.astype(F32)).astype(BF16)


def dot3(v, wh, wl):
    h, l = halves(v)
    return dot(h, wh) + dot(l, wh) + dot(h, wl)


def lanes(shape):
    return lax.broadcasted_iota(jnp.int32, shape, 1)


def call(kernel, outs, *args, smem=(), anywhere=(), scratch=(), flops=0, vmem=24):
    def space(i):
        return pltpu.SMEM if i in smem else pl.ANY if i in anywhere else pltpu.VMEM

    return pl.pallas_call(
        kernel,
        out_shape=[jax.ShapeDtypeStruct(s, d) for s, d in outs],
        in_specs=[pl.BlockSpec(memory_space=space(i)) for i in range(len(args))],
        out_specs=[pl.BlockSpec(memory_space=pltpu.VMEM)] * len(outs),
        scratch_shapes=list(scratch),
        compiler_params=pltpu.CompilerParams(vmem_limit_bytes=vmem * 1024 * 1024),
        cost_estimate=pl.CostEstimate(flops=flops, bytes_accessed=1 << 16, transcendentals=0),
    )(*args)


def column_order():
    row = lax.broadcasted_iota(jnp.int32, (256, 256), 0)
    col = lax.broadcasted_iota(jnp.int32, (256, 256), 1)
    return jnp.where(col == (row % EX) * ES + row // EX, 1.0, 0.0).astype(BF16)


def spread_kernel(partner_ref, source_ref, scan_ref, out_ref):
    turned = dot_nt(column_order(), scan_ref[...].reshape(256, 256))
    lane = lanes((8, 128))
    sub = lax.broadcasted_iota(jnp.int32, (8, 128), 0)
    group = lane // 32
    want = jnp.zeros((8, 128), jnp.int32)
    for e in range(EX):
        here = sub == e % 8
        want = jnp.where(here & (group == e // 8 * 2), partner_ref[0, 0, e], want)
        want = jnp.where(here & (group == e // 8 * 2 + 1), source_ref[0, 0, e], want)
    want = want.astype(F32)
    low = lane < 64
    for c in range(16):
        for v in range(2):
            a0 = turned[c * 16 : c * 16 + 8, v * 128 : v * 128 + 128]
            a1 = turned[c * 16 + 8 : c * 16 + 16, v * 128 : v * 128 + 128]
            p = c * 4 + v * 2
            even = jnp.where(low, a0, pltpu.roll(a1, 64, 1))
            odd = jnp.where(low, pltpu.roll(a0, 64, 1), a1)
            out_ref[p] = jnp.concatenate([even, want], axis=0).astype(BF16)
            out_ref[p + 1] = jnp.concatenate([odd, want], axis=0).astype(BF16)


def gather_kernel(in_ref, out_ref):
    seen = in_ref[...].astype(F32)
    table = seen[:, 0:8, :].reshape(512, 128).astype(BF16)
    want = seen[:, 8:16, :].reshape(512, 128)
    spot = lax.broadcasted_iota(jnp.int32, (512, 512), 1).astype(F32)
    lane = lanes((512, 128))
    halves_out = []
    for half in range(2):
        tile = want[:, half * 64 : half * 64 + 1]
        block = want[:, half * 64 + 32 : half * 64 + 33]
        upper = block >= 8.0
        key = tile * 8.0 + jnp.where(upper, block - 8.0, block)
        pick = jnp.where(spot == key, 1.0, 0.0).astype(BF16)
        found = dot(pick, table)
        swapped = pltpu.roll(found, 64, 1)
        if half == 0:
            halves_out.append(jnp.where(upper, swapped, found))
        else:
            halves_out.append(jnp.where(upper, found, swapped))
    out_ref[...] = jnp.where(lane < 64, halves_out[0], halves_out[1]).astype(BF16)


def sides_kernel(idx_ref, scan_ref, lo_ref, hi_ref, pick_ref, up_ref, down_ref):
    gz = idx_ref[0]
    zero = jnp.zeros((32, 256), BF16)
    lo = jnp.where(gz > 0, lo_ref[...].reshape(32, 256), zero)
    hi = jnp.where(gz < idx_ref[2] - 1, hi_ref[...].reshape(32, 256), zero)
    rows = jnp.concatenate([scan_ref[...].reshape(256, 256), lo, hi], axis=0)
    out = dot(pick_ref[...], rows).astype(BF16)
    up_ref[...] = out[0:48]
    down_ref[...] = out[48:96]


def slopes_kernel(
    idx_ref, scan_ref, zlo_ref, zhi_ref, ylo_ref, yhi_ref, *refs
):
    table_ref, slope_ref, ref_ref, hess_ref, lump_ref, held, sems = refs
    copies = []
    for i, (low, high) in enumerate(((0, 1024), (1024, 3520), (3520, 6592))):
        at = slice(low, high)
        copies.append(pltpu.make_async_copy(table_ref.at[at], held.at[at], sems.at[i]))
    for copy in copies:
        copy.start()
    gz, gy = idx_ref[0], idx_ref[1]
    scan = scan_ref[...].reshape(256, 256)
    z32 = jnp.zeros((32, 256), BF16)
    z48 = jnp.zeros((48, 256), BF16)
    sides = jnp.concatenate(
        [
            jnp.where(gz > 0, zlo_ref[...].reshape(32, 256), z32),
            jnp.where(gz < idx_ref[2] - 1, zhi_ref[...].reshape(32, 256), z32),
            jnp.where(gy > 0, ylo_ref[...], z48),
            jnp.where(gy < idx_ref[3] - 1, yhi_ref[...], z48),
        ],
        axis=0,
    )
    ref_ref[...] = dot_nt(column_order(), scan).astype(BF16)
    copies[0].wait()
    mid = dot_nt(held[0:1024, :], scan)
    rim = dot_nt(held[0:1024, :], sides)
    smooth = (mid[0:256] + mid[256:512], rim[0:256] + rim[256:512])
    slope = (mid[512:768] + mid[768:1024], rim[512:768] + rim[768:1024])
    copies[1].wait()

    def plane(parts, i):
        high, low = 1024 + i * 416, 2272 + i * 416
        return dot3(parts[0], held[high : high + 256, :], held[low : low + 256, :]) + dot3(
            parts[1], held[high + 256 : high + 416, :], held[low + 256 : low + 416, :]
        )

    rounded = [plane(smooth, 0).astype(BF16), plane(smooth, 1).astype(BF16), plane(slope, 2).astype(BF16)]
    for a in range(3):
        slope_ref[:, a * 256 : a * 256 + 256] = rounded[a]
    g = [v.astype(F32) for v in rounded]
    copies[2].wait()
    total = jnp.zeros((256, 128), F32)
    for i, (a, b) in enumerate(PAIRS):
        at = slice(3520 + i * 256, 3776 + i * 256)
        total = total + dot3(g[a] * g[b], held[at, 0:128], held[at, 128:256])
    pairs = dot3(total.T, held[5056:5312, 0:128], held[5056:5312, 128:256])
    lane = lanes((32, 128))
    hess_ref[...] = jnp.where(lane < 64, pairs[0:32], pltpu.roll(pairs[32:64], 64, 1))
    mags = [jnp.abs(v) for v in g]
    whole = mags[0] + mags[1] + mags[2]
    lump = jnp.zeros((256, 128), F32)
    for a in range(3):
        at = slice(5568 + a * 256, 5824 + a * 256)
        lump = lump + dot3(mags[a] * whole, held[at, 0:128], held[at, 128:256])
    lh, ll = halves(lump.T)
    lin = held[5312:5568, 0:128]
    lump_ref[...] = (dot(lh, lin) + dot(ll, lin))[0:16]


def forcing_kernel(
    moved_ref, ref_ref, slope_ref, lump_ref, lh_ref, ll_ref, clin_ref, wire_ref, elem_ref, diff_ref
):
    low = lanes((8, 128)) < 64
    for c in range(16):
        for v in range(2):
            p = (c * 4 + v * 2) * 8
            both = moved_ref[p : p + 16, :].astype(F32)
            m0, m1 = both[0:8], both[8:16]
            diff_ref[c * 16 : c * 16 + 8, v * 128 : v * 128 + 128] = jnp.where(
                low, m0, pltpu.roll(m1, 64, 1)
            )
            diff_ref[c * 16 + 8 : c * 16 + 16, v * 128 : v * 128 + 128] = jnp.where(
                low, pltpu.roll(m0, 64, 1), m1
            )
    diff = ref_ref[...].astype(F32) - diff_ref[...]
    total = dot3(diff * diff, lh_ref[768:1024, :], ll_ref[768:1024, :])
    for a in range(3):
        at = slice(a * 256, a * 256 + 256)
        total = total + dot3(slope_ref[:, at].astype(F32) * diff, lh_ref[at, :], ll_ref[at, :])
    h, l = halves(total.T)
    out = (dot(h, clin_ref[...]) + dot(l, clin_ref[...]))[0:16]
    elem_ref[...] = out[:, 128:256]
    nodes = out[:, 0:128] + pltpu.roll(lump_ref[...], 64, 1)
    wire = nodes[0:4] + pltpu.roll(nodes[4:8], 21, 1) + pltpu.roll(nodes[8:12], 42, 1)
    for p in range(wire_ref.shape[0]):
        wire_ref[p] = wire


def rows_kernel(idx_ref, wire_ref, out_ref):
    gy, n = idx_ref[1], idx_ref[3]
    rows = []
    for k in range(-3, 4):
        at = gy + k
        row = wire_ref[jnp.clip(at, 0, n - 1)]
        rows.append(jnp.where((at >= 0) & (at < n), row, 0.0))
    empty = jnp.zeros((2, 128), F32)
    lines = []
    for h in range(2):
        for k in range(6):
            lines.append(rows[k][2 * h + 1 : 2 * h + 2] + rows[k + 1][2 * h : 2 * h + 1])
        lines.append(empty)
    block = jnp.concatenate(lines, axis=0)
    for p in range(out_ref.shape[0]):
        out_ref[p] = block


def stack_kernel(y0_ref, y1_ref, y2_ref, y3_ref, y4_ref, out_ref):
    for yc, ref in enumerate((y0_ref, y1_ref, y2_ref, y3_ref, y4_ref)):
        for zc in range(5):
            packed = ref[zc * 32 : zc * 32 + 32, :]
            out_ref[pl.ds(zc * 512 + yc, 32, stride=8), :] = packed
            out_ref[pl.ds(zc * 512 + 256 + yc, 32, stride=8), :] = pltpu.roll(packed, 64, 1)


def join_kernel(z0_ref, z1_ref, z2_ref, z3_ref, z4_ref, out_ref):
    for zc, ref in enumerate((z0_ref, z1_ref, z2_ref, z3_ref, z4_ref)):
        out_ref[zc * 32 : zc * 32 + 32, :] = ref[...]


def solve_kernel(idx_ref, wire_ref, hess_ref, elem_ref, disp_ref, mis_ref):
    gz, gy, nz, ny = idx_ref[0], idx_ref[1], idx_ref[2], idx_ref[3]
    lane = lanes((8, 128))
    sub = lax.broadcasted_iota(jnp.int32, (8, 128), 0)
    zero = jnp.zeros((8, 128), F32)
    layers = []
    for k in range(-3, 4):
        at = gz + k
        layer = wire_ref[jnp.clip(at, 0, nz - 1)]
        layers.append(jnp.where((at >= 0) & (at < nz), layer, 0.0))
    force = [layers[k][8:16] + layers[k + 1][0:8] for k in range(6)]
    diag = [pltpu.roll(v, 64, 1) + 1.0 for v in force]
    line_y = gy - 2 + sub
    own_lanes = (lane < 63) & (line_y >= 0) & (line_y < ny)
    column_y = (line_y >= 0) & (line_y < ny)

    def line_ok(k):
        return own_lanes & (gz - 2 + k >= 0) & (gz - 2 + k < nz)

    def node_first(line, a):
        return line if a == 0 else pltpu.roll(line, 128 - 21 * a, 1)

    def operands(lines):
        out = {}
        for k, line in lines.items():
            for b in range(3):
                nodes = node_first(line, b)
                pair = jnp.where(lane < 16, nodes, pltpu.roll(nodes, 15, 1))
                wide = jnp.where(lane < 32, pair, pltpu.roll(pair, 32, 1))
                out[k, 0, b] = wide
                out[k, 1, b] = pltpu.roll(wide, 7, 0)
        return out

    def column(zc, given):
        ok = column_y & (gz - 2 + zc >= 0) & (gz - 2 + zc < nz)
        out = {}
        for a in range(3):
            for h in range(2):
                for l in range(2):
                    total = None
                    for b in range(3):
                        ch = PAIRS.index((min(a, b), max(a, b)))
                        for hh in range(2):
                            for ll in range(2):
                                m = ch * 9 + (h + hh) * 3 + l + ll
                                row = zc * 512 + m * 8
                                term = hess_ref[row : row + 8, :] * given[zc + hh, ll, b]
                                total = term if total is None else total + term
                    out[a, h, l] = jnp.where(ok, total, 0.0)
        return out

    def pushed(zl, columns):
        placed = zero
        for a in range(3):
            total = zero
            for h in range(2):
                found = columns[zl - h]
                total = total + found[a, h, 0] + pltpu.roll(found[a, h, 1], 1, 0)
            total = total + pltpu.roll(total, 128 - 16, 1)
            first = jnp.where(lane < 16, total, 0.0)
            second = jnp.where((lane >= 1) & (lane < 17), pltpu.roll(total, 128 - 31, 1), 0.0)
            nodes = first + second
            placed = placed + (nodes if a == 0 else pltpu.roll(nodes, 21 * a, 1))
        return placed

    u = {k: jnp.where(line_ok(k), force[k] / diag[k], 0.0) for k in range(6)}
    for step in range(1, ITERS):
        given = operands(u)
        columns = {zc: column(zc, given) for zc in range(step - 1, 6 - step)}
        u = {
            k: jnp.where(line_ok(k), u[k] + (force[k] - pushed(k, columns) - u[k]) / diag[k], 0.0)
            for k in range(step, 6 - step)
        }
    given = operands(u)
    found = column(2, given)
    total = zero
    for a in range(3):
        nodes = node_first(u[2], a)
        disp_ref[a, 0] = nodes[2:3, 0:17]
        for h in range(2):
            nodes = node_first(u[2 + h], a)
            corner = jnp.where(lane < 32, nodes, pltpu.roll(nodes, 31, 1))
            for l in range(2):
                row = a * 4 + h * 2 + l
                here = corner if l == 0 else pltpu.roll(corner, 7, 0)
                push = found[a, h, l]
                push = push + pltpu.roll(push, 128 - 16, 1)
                total = total + here * (push - 2.0 * elem_ref[row : row + 1, :])
    total = total + elem_ref[12:13, :]
    total = (total + pltpu.roll(total, 128 - 32, 1)) / ES**3
    mis_ref[0] = total[2:3, 0:16]


def shift(value, axis, by):
    count = lax.axis_size(axis)
    return lax.ppermute(value, axis, [(i, (i + by) % count) for i in range(count)])


def body(reference_scan, loaded_scan, partner, source):
    cols = column_filter()
    plane_h, plane_l = plane_filter()
    quad_h, quad_l, lin_h, lin_l = plane_weights()
    col_h, col_l, col_lin = column_weights()
    beside = lambda a, b: np.concatenate([a, b], axis=1)
    planes = [t[:, a * 256 : a * 256 + 256] for t in (plane_h, plane_l) for a in range(3)]
    table = np.concatenate(
        [cols, *planes, beside(quad_h, quad_l), beside(col_h, col_l), col_lin, beside(lin_h, lin_l)]
    )
    n_gz, n_gy = lax.axis_size("gz"), lax.axis_size("gy")
    idx = jnp.stack([lax.axis_index("gz"), lax.axis_index("gy"), n_gz, n_gy]).astype(jnp.int32)
    zlo = shift(reference_scan[14:16], "gz", 1)
    zhi = shift(reference_scan[0:2], "gz", -1)
    (outgoing,) = call(
        spread_kernel, [((64, 16, 128), BF16)], partner.reshape(1, 1, EX), source, loaded_scan, smem=(0, 1), vmem=60
    )
    outgoing, zlo, zhi = lax.optimization_barrier((outgoing, zlo, zhi))
    pieces = lax.all_to_all(outgoing, "gy", split_axis=0, concat_axis=0, tiled=True)
    up, down = call(
        sides_kernel, [((48, 256), BF16)] * 2, idx, reference_scan, zlo, zhi, side_rows(), smem=(0,)
    )
    ylo = shift(up, "gy", 1)
    yhi = shift(down, "gy", -1)
    pieces, ylo, yhi = lax.optimization_barrier((pieces, ylo, yhi))
    (found,) = call(gather_kernel, [((512, 128), BF16)], pieces)
    found, ylo, yhi = lax.optimization_barrier((found, ylo, yhi))
    moved = lax.all_to_all(found.reshape(64, 8, 128), "gy", split_axis=0, concat_axis=0, tiled=True)
    slopes, turned, hess, lump = call(
        slopes_kernel,
        [((256, 768), BF16), ((256, 256), BF16), ((32, 128), F32), ((16, 128), F32)],
        idx, reference_scan, zlo, zhi, ylo, yhi, table,
        smem=(0,),
        anywhere=(6,),
        scratch=[pltpu.VMEM(table.shape, BF16), pltpu.SemaphoreType.DMA((3,))],
        flops=4_000_000_000,
        vmem=50,
    )
    z1, z3 = shift(hess, "gz", 1), shift(hess, "gz", -1)
    z0, z4 = shift(z1, "gz", 1), shift(z3, "gz", -1)
    (layers,) = call(join_kernel, [((160, 128), F32)], z0, z1, hess, z3, z4)
    moved, layers = lax.optimization_barrier((moved, layers))
    wire, elem = call(
        forcing_kernel,
        [((n_gy, 4, 128), F32), ((16, 128), F32)],
        moved.reshape(512, 128), turned, slopes, lump, lin_h, lin_l, col_lin,
        scratch=[pltpu.VMEM((256, 256), F32)],
    )
    wire, layers = lax.optimization_barrier((wire, layers))
    rows = lax.all_to_all(wire, "gy", split_axis=0, concat_axis=0, tiled=True)
    near = [shift(layers, "gy", by) for by in (2, 1)] + [layers] + [shift(layers, "gy", by) for by in (-1, -2)]
    (stacked,) = call(stack_kernel, [((2560, 128), F32)], *near)
    (lines,) = call(rows_kernel, [((n_gz, 16, 128), F32)], idx, rows, smem=(0,))
    lines = lax.all_to_all(lines, "gz", split_axis=0, concat_axis=0, tiled=True)
    disp, mis = call(
        solve_kernel, [((3, 1, 1, 17), F32), ((1, 1, 16), F32)], idx, lines, stacked, elem, smem=(0,)
    )
    return disp, mis


def solution(mesh):
    return jax.shard_map(
        body,
        mesh=mesh,
        in_specs=(
            P("gz", "gy", None),
            P("gz", "gy", None),
            P("gz", "gy", None, None),
            P("gz", "gy", None),
        ),
        out_specs=(P(None, "gz", "gy", None), P("gz", "gy", None)),
        check_vma=False,
    )
```

time: 132 us -> 117 us (0.89)
  blocking collectives: 38.3 us -> 0 us
  starting transfers between devices: 51.8 us -> 83.9 us
  waiting for transfers between devices: 20.1 us -> 13.5 us
  local copies, waits for them, and re-layouts: 6.93 us -> 3.44 us
  Pallas kernels: 12.6 us -> 14.3 us
    all_to_all x1 -> x0, blocking collectives: 38.3 us -> none  [body(): lax.all_to_all(outgoing, 'gy', split_axis=0, concat_axis=0, tiled=True)]
    all_to_all x0 -> x3, starting transfers between devices: none -> 36.8 us  [the longest x1 14.3 us: body(): rows = lax.all_to_all(wire, 'gy', split_axis=0, concat_axis=0, tiled=True)]
    ppermute x16 -> x12, waiting for transfers between devices: 20.1 us -> 5 us  [shift(): lax.ppermute(value, axis, [(i, (i + by) % count) for i in range(count)])]
    all_to_all x0 -> x3, waiting for transfers between devices: none -> 8.54 us  [the longest x1 4.61 us: body(): lines = lax.all_to_all(lines, 'gz', split_axis=0, concat_axis=0, tiled=True)]
    ppermute x16 -> x12, starting transfers between devices: 44.1 us -> 36.4 us  [shift(): lax.ppermute(value, axis, [(i, (i + by) % count) for i in range(count)])]
    unnamed x34 -> x12, local copies, waits for them, and re-layouts: 6.92 us -> 2.7 us
    all_to_all x1, starting transfers between devices: 7.72 us -> 10.7 us  [body(): lax.all_to_all(found.reshape(64, 8, 128), 'gy', split_axis=0, concat_axis...]
    pallas_call x10 -> x9, Pallas kernels: 11.7 us -> 14.3 us  [call(): pl.pallas_call(kernel, out_shape=[jax.ShapeDtypeStruct(s, d) for s, d in...]
  transfers between devices with their start and end apart: 17 -> 16, of which waited for: 11 -> 7; matrix products, arithmetic and copies ran while one was open for 0% -> 0% of each run, Pallas kernels for 4% -> 8%
where the time goes in v1:
time: 117 us; the launch traced here: 116 us
  starting transfers between devices  83.9 us (72%)
  Pallas kernels  14.3 us (12%)
  waiting for transfers between devices  13.5 us (12%)
  local copies, waits for them, and re-layouts  3.44 us (3%)
    ppermute x12, starting transfers between devices, shift(): lax.ppermute(value, axis, [(i, (i + by) % count) for i in range(count)])  36.4 us
    pallas_call x9, Pallas kernels, call(): pl.pallas_call(kernel, out_shape=[jax.ShapeDtypeStruct(s, d) for s, d in...  14.3 us
    all_to_all x1, starting transfers between devices, body(): rows = lax.all_to_all(wire, 'gy', split_axis=0, concat_axis=0, tiled=True)  14.3 us
    all_to_all x1, starting transfers between devices, body(): lax.all_to_all(outgoing, 'gy', split_axis=0, concat_axis=0, tiled=True)  14.2 us
    all_to_all x1, starting transfers between devices, body(): lax.all_to_all(found.reshape(64, 8, 128), 'gy', split_axis=0, concat_axis...  10.7 us
    all_to_all x1, starting transfers between devices, body(): lines = lax.all_to_all(lines, 'gz', split_axis=0, concat_axis=0, tiled=True)  8.35 us
    ppermute x12, waiting for transfers between devices, shift(): lax.ppermute(value, axis, [(i, (i + by) % count) for i in range(count)])  5 us
    all_to_all x1, waiting for transfers between devices, body(): lines = lax.all_to_all(lines, 'gz', split_axis=0, concat_axis=0, tiled=True)  4.61 us
  transfers between devices with their start and end apart: 16, of which 7 were waited for; matrix products, arithmetic and copies ran while one was open for 0% of the time, Pallas kernels for 8%

profile of v1, /device:TPU:1, one launch (start us, length us, event | category | flops | bytes accessed | tf_op | source)
XLA Modules:
  0.0 116.1 jit_solution(17304337620675246021)
XLA Ops:
  0.6 0.7 fusion
  1.4 6.9 %collective-permute-start.1 = (bf16[2,16,256]{2,1,0:T(8,128)(2,1)S(1)}, bf16[2,16,256]{2,1,0:T(8,128)(2,1)S(1)}, u32[]{:S(2)}, u32[]{:S(2)}) collective-permute-start(bf16[2,16,256]{2,1,0:T(8,128)(2,1)S(1)} %get-tuple-element.44), channel_id=1, source_target_pairs={{0,448},{64,0},{128,64},{192,128},{256,192},{320,256},{384,320},{4... | collective-permute-start | bytes 49160 | tf_op jit(solution)/shard_map/ppermute | solution.py:437
  8.2 0.0 collective-permute-start
  8.3 1.9 %shard_map.104 = bf16[64,16,128]{2,1,0:T(8,128)(2,1)} custom-call(s32[1,1,16]{2,1,0:T(1,128)} %bitcast.6, s32[1,1,16]{2,1,0:T(1,128)} %source_ref.1, bf16[16,16,256]{2,1,0:T(8,128)(2,1)} %scan_ref.3), custom_call_target="tpu_custom_call" | custom-call | bytes 65536 | tf_op jit(solution)/shard_map/pallas_call | solution.py:149
  10.2 0.0 collective-permute-done.1.hi_ref.zhi_ref
  10.2 0.0 collective-permute-done.lo_ref.zlo_ref
  10.2 14.2 %all-to-all-start = ((bf16[64,16,128]{2,1,0:T(8,128)(2,1)}), bf16[64,16,128]{2,1,0:T(8,128)(2,1)S(1)}, u32[]{:S(2)}, u32[]{:S(2)}) async-start(bf16[64,16,128]{2,1,0:T(8,128)(2,1)} %shard_map.104), calls=%async_computation | async-start | bytes 524288 | tf_op jit(solution)/shard_map/all_to_all | solution.py:458
  24.4 0.1 pad_add_fusion.idx_ref
  24.4 0.0 copy-start.2
  24.4 0.9 copy-done.2
  25.3 0.0 copy-start.5
  25.4 0.9 copy-done.5
  26.2 0.7 shard_map.105
  26.9 2.9 %collective-permute-start.2 = (bf16[48,256]{1,0:T(8,128)(2,1)S(1)}, bf16[48,256]{1,0:T(8,128)(2,1)S(1)}, u32[]{:S(2)}, u32[]{:S(2)}) collective-permute-start(bf16[48,256]{1,0:T(8,128)(2,1)S(1)} %get-tuple-element.26), channel_id=1, source_target_pairs={{0,1},{1,2},{2,3},{3,4},{4,5},{5,6},{6,7},{7,8},{8,9},{9,10},{10,1... | collective-permute-start | bytes 73736 | tf_op jit(solution)/shard_map/ppermute | solution.py:437
  29.9 5.7 %collective-permute-start.3 = (bf16[48,256]{1,0:T(8,128)(2,1)S(1)}, bf16[48,256]{1,0:T(8,128)(2,1)S(1)}, u32[]{:S(2)}, u32[]{:S(2)}) collective-permute-start(bf16[48,256]{1,0:T(8,128)(2,1)S(1)} %get-tuple-element.27), channel_id=1, source_target_pairs={{0,63},{1,0},{2,1},{3,2},{4,3},{5,4},{6,5},{7,6},{8,7},{9,8},{10,9... | collective-permute-start | bytes 73736 | tf_op jit(solution)/shard_map/ppermute | solution.py:437
  35.6 0.6 collective-permute-done.2.ylo_ref
  36.1 0.6 collective-permute-done.3.yhi_ref
  36.8 3.9 %all-to-all-done.in_ref = bf16[64,16,128]{2,1,0:T(8,128)(2,1)S(1)} async-done(((bf16[64,16,128]{2,1,0:T(8,128)(2,1)}), bf16[64,16,128]{2,1,0:T(8,128)(2,1)S(1)}, u32[]{:S(2)}, u32[]{:S(2)}) %all-to-all-start) | async-done | bytes 262176 | tf_op jit(solution)/shard_map/all_to_all | solution.py:458
  40.7 1.3 %shard_map.106 = bf16[512,128]{1,0:T(8,128)(2,1)} custom-call(bf16[64,16,128]{2,1,0:T(8,128)(2,1)S(1)} %all-to-all-done.in_ref), custom_call_target="tpu_custom_call" | custom-call | bytes 65536 | tf_op jit(solution)/shard_map/pallas_call | solution.py:149
  42.0 10.7 %all-to-all-start.1 = ((bf16[64,8,128]{2,1,0:T(8,128)(2,1)}), bf16[64,8,128]{2,1,0:T(8,128)(2,1)S(1)}, u32[]{:S(2)}, u32[]{:S(2)}) async-start(bf16[64,8,128]{2,1,0:T(8,128)(2,1)} %bitcast.3), calls=%async_computation.1 | async-start | bytes 262144 | tf_op jit(solution)/shard_map/all_to_all | solution.py:467
  52.7 0.0 copy-start.3
  52.7 0.9 copy-done.3
  53.6 0.0 copy-start
  53.6 0.0 copy-start.1
  53.6 0.0 copy-start.4
  53.6 4.9 %shard_map.107 = (bf16[256,768]{1,0:T(8,128)(2,1)S(1)}, bf16[256,256]{1,0:T(8,128)(2,1)S(1)}, f32[32,128]{1,0:T(8,128)S(1)}, f32[16,128]{1,0:T(8,128)S(1)}) custom-call(s32[4]{0:T(128)S(1)} %pad_add_fusion.idx_ref, bf16[16,16,256]{2,1,0:T(8,128)(2,1)S(1)} %copy-done.3, bf16[2,16,256]{2,1,0:T(8,128)(2,1)S(1)} %collective-permute-done.lo_ref.zlo_ref, ...), custom_call_target="tpu_custom_call" | custom-call | flops 4000000000 | bytes 65536 | tf_op jit(solution)/shard_map/pallas_call | solution.py:149
  58.5 3.9 %collective-permute-start.6 = (f32[32,128]{1,0:T(8,128)S(1)}, f32[32,128]{1,0:T(8,128)S(1)}, u32[]{:S(2)}, u32[]{:S(2)}) collective-permute-start(f32[32,128]{1,0:T(8,128)S(1)} %get-tuple-element.34.z2_ref), channel_id=1, source_target_pairs={{0,448},{64,0},{128,64},{192,128},{256,192},{320,256},{384,320},{4... | collective-permute-start | bytes 49160 | tf_op jit(solution)/shard_map/ppermute | solution.py:437
  62.5 0.0 collective-permute-start.4
  62.5 0.8 collective-permute-done.6.z3_ref
  63.3 1.4 %collective-permute-start.7 = (f32[32,128]{1,0:T(8,128)S(1)}, f32[32,128]{1,0:T(8,128)S(1)}, u32[]{:S(2)}, u32[]{:S(2)}) collective-permute-start(f32[32,128]{1,0:T(8,128)S(1)} %collective-permute-done.6.z3_ref), channel_id=1, source_target_pairs={{0,448},{64,0},{128,64},{192,128},{256,192},{320,256},{384,320},{4... | collective-permute-start | bytes 49160 | tf_op jit(solution)/shard_map/ppermute | solution.py:437
  64.7 0.0 collective-permute-done.4.z1_ref
  64.7 1.0 collective-permute-start.5
  65.6 1.1 collective-permute-done.7.z4_ref
  66.8 1.8 %collective-permute-done.5.z0_ref = f32[32,128]{1,0:T(8,128)S(1)} collective-permute-done((f32[32,128]{1,0:T(8,128)S(1)}, f32[32,128]{1,0:T(8,128)S(1)}, u32[]{:S(2)}, u32[]{:S(2)}) %collective-permute-start.5) | collective-permute-done | bytes 16416 | tf_op jit(solution)/shard_map/ppermute | solution.py:437
  68.6 0.0 all-to-all-done.1
  68.6 0.0 copy-done
  68.6 0.0 copy-done.1
  68.6 0.0 copy-done.4
  68.6 1.6 %shard_map.109 = (f32[64,4,128]{2,1,0:T(4,128)}, f32[16,128]{1,0:T(8,128)S(1)}) custom-call(bf16[512,128]{1,0:T(8,128)(2,1)S(1)} %bitcast.5, bf16[256,256]{1,0:T(8,128)(2,1)S(1)} %get-tuple-element.36.ref_ref, bf16[256,768]{1,0:T(8,128)(2,1)S(1)} %get-tuple-element.37.slope_ref, f32[16,128]{1,0:T(8,128)S(1)} %get-tuple-element.38.lump_ref, ...), custom_call_target="tpu_custom_call" | custom-call | bytes 65536 | tf_op jit(solution)/shard_map/pallas_call | solution.py:149
  70.2 14.3 %all-to-all-start.2 = ((f32[64,4,128]{2,1,0:T(4,128)}), f32[64,4,128]{2,1,0:T(4,128)S(1)}, u32[]{:S(2)}, u32[]{:S(2)}) async-start(f32[64,4,128]{2,1,0:T(4,128)} %get-tuple-element.41), calls=%async_computation.2 | async-start | bytes 262144 | tf_op jit(solution)/shard_map/all_to_all | solution.py:489
  84.5 7.4 %collective-permute-start.11 = (f32[160,128]{1,0:T(8,128)S(1)}, f32[160,128]{1,0:T(8,128)S(1)}, u32[]{:S(2)}, u32[]{:S(2)}) collective-permute-start(f32[160,128]{1,0:T(8,128)S(1)} %shard_map.108.y2_ref), channel_id=1, source_target_pairs={{0,62},{1,63},{2,0},{3,1},{4,2},{5,3},{6,4},{7,5},{8,6},{9,7},{10,... | collective-permute-start | bytes 245768 | tf_op jit(solution)/shard_map/ppermute | solution.py:437
  92.0 3.1 %collective-permute-start.10 = (f32[160,128]{1,0:T(8,128)S(1)}, f32[160,128]{1,0:T(8,128)S(1)}, u32[]{:S(2)}, u32[]{:S(2)}) collective-permute-start(f32[160,128]{1,0:T(8,128)S(1)} %shard_map.108.y2_ref), channel_id=1, source_target_pairs={{0,63},{1,0},{2,1},{3,2},{4,3},{5,4},{6,5},{7,6},{8,7},{9,8},{10,9... | collective-permute-start | bytes 245768 | tf_op jit(solution)/shard_map/ppermute | solution.py:437
  95.1 2.2 %collective-permute-start.9 = (f32[160,128]{1,0:T(8,128)S(1)}, f32[160,128]{1,0:T(8,128)S(1)}, u32[]{:S(2)}, u32[]{:S(2)}) collective-permute-start(f32[160,128]{1,0:T(8,128)S(1)} %shard_map.108.y2_ref), channel_id=1, source_target_pairs={{0,1},{1,2},{2,3},{3,4},{4,5},{5,6},{6,7},{7,8},{8,9},{9,10},{10,1... | collective-permute-start | bytes 245768 | tf_op jit(solution)/shard_map/ppermute | solution.py:437
  97.3 1.9 %collective-permute-start.8 = (f32[160,128]{1,0:T(8,128)S(1)}, f32[160,128]{1,0:T(8,128)S(1)}, u32[]{:S(2)}, u32[]{:S(2)}) collective-permute-start(f32[160,128]{1,0:T(8,128)S(1)} %shard_map.108.y2_ref), channel_id=1, source_target_pairs={{0,2},{1,3},{2,4},{3,5},{4,6},{5,7},{6,8},{7,9},{8,10},{9,11},{10,... | collective-permute-start | bytes 245768 | tf_op jit(solution)/shard_map/ppermute | solution.py:437
  99.2 0.0 all-to-all-done.2.wire_ref
  99.2 1.2 %shard_map.110 = f32[8,16,128]{2,1,0:T(8,128)} custom-call(s32[4]{0:T(128)S(1)} %pad_add_fusion.idx_ref, f32[64,4,128]{2,1,0:T(4,128)S(1)} %all-to-all-done.2.wire_ref), custom_call_target="tpu_custom_call" | custom-call | bytes 65536 | tf_op jit(solution)/shard_map/pallas_call | solution.py:149
  100.4 8.3 %all-to-all-start.3 = ((f32[8,16,128]{2,1,0:T(8,128)}), f32[8,16,128]{2,1,0:T(8,128)S(1)}, u32[]{:S(2)}, u32[]{:S(2)}) async-start(f32[8,16,128]{2,1,0:T(8,128)} %shard_map.110), calls=%async_computation.3 | async-start | bytes 131072 | tf_op jit(solution)/shard_map/all_to_all | solution.py:493
  108.8 0.0 collective-permute-done.11.y4_ref
  108.8 0.0 collective-permute-done.10.y3_ref
  108.8 0.0 collective-permute-done.9.y1_ref
  108.8 0.0 collective-permute-done.8.y0_ref
  108.8 0.2 shard_map.111.hess_ref
  109.0 4.6 %all-to-all-done.3.wire_ref = f32[8,16,128]{2,1,0:T(8,128)S(1)} async-done(((f32[8,16,128]{2,1,0:T(8,128)}), f32[8,16,128]{2,1,0:T(8,128)S(1)}, u32[]{:S(2)}, u32[]{:S(2)}) %all-to-all-start.3) | async-done | bytes 65568 | tf_op jit(solution)/shard_map/all_to_all | solution.py:493
  113.6 2.5 %shard_map.112 = (f32[3,1,1,17]{3,2,1,0:T(1,128)}, f32[1,1,16]{2,1,0:T(1,128)}) custom-call(s32[4]{0:T(128)S(1)} %pad_add_fusion.idx_ref, f32[8,16,128]{2,1,0:T(8,128)S(1)} %all-to-all-done.3.wire_ref, f32[2560,128]{1,0:T(8,128)S(1)} %shard_map.111.hess_ref, f32[16,128]{1,0:T(8,128)S(1)} %get-tuple-element.43.elem_ref), custom_call_target="tpu_custom_call" | custom-call | bytes 65536 | tf_op jit(solution)/shard_map/pallas_call | solution.py:149
  (1 shorter events, 0.0 us)
Async XLA Ops:
  1.4 8.8 %collective-permute-start.1 = (bf16[2,16,256]{2,1,0:T(8,128)(2,1)S(1)}, bf16[2,16,256]{2,1,0:T(8,128)(2,1)S(1)}, u32[]{:S(2)}, u32[]{:S(2)}) collective-permute-start(bf16[2,16,256]{2,1,0:T(8,128)(2,1)S(1)} %get-tuple-element.44), channel_id=1, source_target_pairs={{0,448},{64,0},{128,64},{192,128},{256,192},{320,256},{384,320},{4... | collective-permute-start | bytes 49160 | tf_op jit(solution)/shard_map/ppermute | solution.py:437
  8.2 1.9 %collective-permute-start = (bf16[2,16,256]{2,1,0:T(8,128)(2,1)S(1)}, bf16[2,16,256]{2,1,0:T(8,128)(2,1)S(1)}, u32[]{:S(2)}, u32[]{:S(2)}) collective-permute-start(bf16[2,16,256]{2,1,0:T(8,128)(2,1)S(1)} %get-tuple-element.45), channel_id=1, source_target_pairs={{0,64},{64,128},{128,192},{192,256},{256,320},{320,384},{384,448},... | collective-permute-start | bytes 49160 | tf_op jit(solution)/shard_map/ppermute | solution.py:437
  10.2 30.5 %all-to-all-start = ((bf16[64,16,128]{2,1,0:T(8,128)(2,1)}), bf16[64,16,128]{2,1,0:T(8,128)(2,1)S(1)}, u32[]{:S(2)}, u32[]{:S(2)}) async-start(bf16[64,16,128]{2,1,0:T(8,128)(2,1)} %shard_map.104), calls=%async_computation | async-start | bytes 524288 | tf_op jit(solution)/shard_map/all_to_all | solution.py:458
  24.4 0.9 copy-start.2
  25.3 0.9 copy-start.5
  26.9 9.2 %collective-permute-start.2 = (bf16[48,256]{1,0:T(8,128)(2,1)S(1)}, bf16[48,256]{1,0:T(8,128)(2,1)S(1)}, u32[]{:S(2)}, u32[]{:S(2)}) collective-permute-start(bf16[48,256]{1,0:T(8,128)(2,1)S(1)} %get-tuple-element.26), channel_id=1, source_target_pairs={{0,1},{1,2},{2,3},{3,4},{4,5},{5,6},{6,7},{7,8},{8,9},{9,10},{10,1... | collective-permute-start | bytes 73736 | tf_op jit(solution)/shard_map/ppermute | solution.py:437
  29.9 6.9 %collective-permute-start.3 = (bf16[48,256]{1,0:T(8,128)(2,1)S(1)}, bf16[48,256]{1,0:T(8,128)(2,1)S(1)}, u32[]{:S(2)}, u32[]{:S(2)}) collective-permute-start(bf16[48,256]{1,0:T(8,128)(2,1)S(1)} %get-tuple-element.27), channel_id=1, source_target_pairs={{0,63},{1,0},{2,1},{3,2},{4,3},{5,4},{6,5},{7,6},{8,7},{9,8},{10,9... | collective-permute-start | bytes 73736 | tf_op jit(solution)/shard_map/ppermute | solution.py:437
  42.0 26.6 %all-to-all-start.1 = ((bf16[64,8,128]{2,1,0:T(8,128)(2,1)}), bf16[64,8,128]{2,1,0:T(8,128)(2,1)S(1)}, u32[]{:S(2)}, u32[]{:S(2)}) async-start(bf16[64,8,128]{2,1,0:T(8,128)(2,1)} %bitcast.3), calls=%async_computation.1 | async-start | bytes 262144 | tf_op jit(solution)/shard_map/all_to_all | solution.py:467
  52.7 0.9 copy-start.3
  53.6 15.0 %copy-start = (bf16[1024,128]{1,0:T(8,128)(2,1)S(1)}, bf16[1024,128]{1,0:T(8,128)(2,1)}, u32[]{:S(2)}) copy-start(bf16[1024,128]{1,0:T(8,128)(2,1)} %constant.26.clone.ll_ref) | copy-start | bytes 786436
  53.6 15.0 %copy-start.1 = (bf16[1024,128]{1,0:T(8,128)(2,1)S(1)}, bf16[1024,128]{1,0:T(8,128)(2,1)}, u32[]{:S(2)}) copy-start(bf16[1024,128]{1,0:T(8,128)(2,1)} %constant.25.clone.lh_ref) | copy-start | bytes 786436
  53.6 15.0 %copy-start.4 = (bf16[256,256]{1,0:T(8,128)(2,1)S(1)}, bf16[256,256]{1,0:T(8,128)(2,1)}, u32[]{:S(2)}) copy-start(bf16[256,256]{1,0:T(8,128)(2,1)} %constant.27.clone.clin_ref) | copy-start | bytes 393220
  58.5 4.8 %collective-permute-start.6 = (f32[32,128]{1,0:T(8,128)S(1)}, f32[32,128]{1,0:T(8,128)S(1)}, u32[]{:S(2)}, u32[]{:S(2)}) collective-permute-start(f32[32,128]{1,0:T(8,128)S(1)} %get-tuple-element.34.z2_ref), channel_id=1, source_target_pairs={{0,448},{64,0},{128,64},{192,128},{256,192},{320,256},{384,320},{4... | collective-permute-start | bytes 49160 | tf_op jit(solution)/shard_map/ppermute | solution.py:437
  62.5 2.2 %collective-permute-start.4 = (f32[32,128]{1,0:T(8,128)S(1)}, f32[32,128]{1,0:T(8,128)S(1)}, u32[]{:S(2)}, u32[]{:S(2)}) collective-permute-start(f32[32,128]{1,0:T(8,128)S(1)} %get-tuple-element.34.z2_ref), channel_id=1, source_target_pairs={{0,64},{64,128},{128,192},{192,256},{256,320},{320,384},{384,448},... | collective-permute-start | bytes 49160 | tf_op jit(solution)/shard_map/ppermute | solution.py:437
  63.3 3.5 %collective-permute-start.7 = (f32[32,128]{1,0:T(8,128)S(1)}, f32[32,128]{1,0:T(8,128)S(1)}, u32[]{:S(2)}, u32[]{:S(2)}) collective-permute-start(f32[32,128]{1,0:T(8,128)S(1)} %collective-permute-done.6.z3_ref), channel_id=1, source_target_pairs={{0,448},{64,0},{128,64},{192,128},{256,192},{320,256},{384,320},{4... | collective-permute-start | bytes 49160 | tf_op jit(solution)/shard_map/ppermute | solution.py:437
  64.7 3.9 %collective-permute-start.5 = (f32[32,128]{1,0:T(8,128)S(1)}, f32[32,128]{1,0:T(8,128)S(1)}, u32[]{:S(2)}, u32[]{:S(2)}) collective-permute-start(f32[32,128]{1,0:T(8,128)S(1)} %collective-permute-done.4.z1_ref), channel_id=1, source_target_pairs={{0,64},{64,128},{128,192},{192,256},{256,320},{320,384},{384,448},... | collective-permute-start | bytes 49160 | tf_op jit(solution)/shard_map/ppermute | solution.py:437
  70.2 29.0 %all-to-all-start.2 = ((f32[64,4,128]{2,1,0:T(4,128)}), f32[64,4,128]{2,1,0:T(4,128)S(1)}, u32[]{:S(2)}, u32[]{:S(2)}) async-start(f32[64,4,128]{2,1,0:T(4,128)} %get-tuple-element.41), calls=%async_computation.2 | async-start | bytes 262144 | tf_op jit(solution)/shard_map/all_to_all | solution.py:489
  84.5 24.2 %collective-permute-start.11 = (f32[160,128]{1,0:T(8,128)S(1)}, f32[160,128]{1,0:T(8,128)S(1)}, u32[]{:S(2)}, u32[]{:S(2)}) collective-permute-start(f32[160,128]{1,0:T(8,128)S(1)} %shard_map.108.y2_ref), channel_id=1, source_target_pairs={{0,62},{1,63},{2,0},{3,1},{4,2},{5,3},{6,4},{7,5},{8,6},{9,7},{10,... | collective-permute-start | bytes 245768 | tf_op jit(solution)/shard_map/ppermute | solution.py:437
  92.0 16.8 %collective-permute-start.10 = (f32[160,128]{1,0:T(8,128)S(1)}, f32[160,128]{1,0:T(8,128)S(1)}, u32[]{:S(2)}, u32[]{:S(2)}) collective-permute-start(f32[160,128]{1,0:T(8,128)S(1)} %shard_map.108.y2_ref), channel_id=1, source_target_pairs={{0,63},{1,0},{2,1},{3,2},{4,3},{5,4},{6,5},{7,6},{8,7},{9,8},{10,9... | collective-permute-start | bytes 245768 | tf_op jit(solution)/shard_map/ppermute | solution.py:437
  95.1 13.7 %collective-permute-start.9 = (f32[160,128]{1,0:T(8,128)S(1)}, f32[160,128]{1,0:T(8,128)S(1)}, u32[]{:S(2)}, u32[]{:S(2)}) collective-permute-start(f32[160,128]{1,0:T(8,128)S(1)} %shard_map.108.y2_ref), channel_id=1, source_target_pairs={{0,1},{1,2},{2,3},{3,4},{4,5},{5,6},{6,7},{7,8},{8,9},{9,10},{10,1... | collective-permute-start | bytes 245768 | tf_op jit(solution)/shard_map/ppermute | solution.py:437
  97.3 11.5 %collective-permute-start.8 = (f32[160,128]{1,0:T(8,128)S(1)}, f32[160,128]{1,0:T(8,128)S(1)}, u32[]{:S(2)}, u32[]{:S(2)}) collective-permute-start(f32[160,128]{1,0:T(8,128)S(1)} %shard_map.108.y2_ref), channel_id=1, source_target_pairs={{0,2},{1,3},{2,4},{3,5},{4,6},{5,7},{6,8},{7,9},{8,10},{9,11},{10,... | collective-permute-start | bytes 245768 | tf_op jit(solution)/shard_map/ppermute | solution.py:437
  100.4 13.2 %all-to-all-start.3 = ((f32[8,16,128]{2,1,0:T(8,128)}), f32[8,16,128]{2,1,0:T(8,128)S(1)}, u32[]{:S(2)}, u32[]{:S(2)}) async-start(f32[8,16,128]{2,1,0:T(8,128)} %shard_map.110), calls=%async_computation.3 | async-start | bytes 131072 | tf_op jit(solution)/shard_map/all_to_all | solution.py:493

commit v2 on v1

--- a/solution.py
+++ b/solution.py
@@ -102,22 +102,6 @@
             quad[row, f * 32 + ff * 16 + ex] = linear(c, f) * linear(c, ff)
     qh, ql = split(quad)
     return qh, ql, lin.astype(ml_dtypes.bfloat16)
-
-
-def side_rows():
-    pick = np.zeros((96, 320))
-    for side in range(2):
-        for zz in range(20):
-            for j in range(2):
-                y = (14 if side == 0 else 0) + j
-                if zz < 2:
-                    at = 256 + zz * 16 + y
-                elif zz < 18:
-                    at = (zz - 2) * 16 + y
-                else:
-                    at = 288 + (zz - 18) * 16 + y
-                pick[side * 48 + zz * 2 + j, at] = 1.0
-    return pick.astype(ml_dtypes.bfloat16)
 
 
 def dot(a, b):
@@ -208,13 +192,25 @@
     out_ref[...] = jnp.where(lane < 64, halves_out[0], halves_out[1]).astype(BF16)
 
 
-def sides_kernel(idx_ref, scan_ref, lo_ref, hi_ref, pick_ref, up_ref, down_ref):
+def edge_picks(rows, first_z):
+    out = lax.broadcasted_iota(jnp.int32, (96, rows), 0)
+    at = lax.broadcasted_iota(jnp.int32, (96, rows), 1)
+    upper = out >= 48
+    place = jnp.where(upper, out - 48, out)
+    z = place // 2 - 2
+    y = place % 2 + jnp.where(upper, 0, 14)
+    hit = (place < 40) & (at // 16 + first_z == z) & (at % 16 == y)
+    return jnp.where(hit, 1.0, 0.0).astype(BF16)
+
+
+def sides_kernel(idx_ref, scan_ref, lo_ref, hi_ref, up_ref, down_ref):
     gz = idx_ref[0]
     zero = jnp.zeros((32, 256), BF16)
     lo = jnp.where(gz > 0, lo_ref[...].reshape(32, 256), zero)
     hi = jnp.where(gz < idx_ref[2] - 1, hi_ref[...].reshape(32, 256), zero)
-    rows = jnp.concatenate([scan_ref[...].reshape(256, 256), lo, hi], axis=0)
-    out = dot(pick_ref[...], rows).astype(BF16)
+    out = dot(edge_picks(256, 0), scan_ref[...].reshape(256, 256))
+    out = out + dot(edge_picks(32, -2), lo) + dot(edge_picks(32, 16), hi)
+    out = out.astype(BF16)
     up_ref[...] = out[0:48]
     down_ref[...] = out[48:96]
 
@@ -308,7 +304,7 @@
         wire_ref[p] = wire
 
 
-def rows_kernel(idx_ref, wire_ref, out_ref):
+def rows_kernel(idx_ref, wire_ref, n0_ref, n1_ref):
     gy, n = idx_ref[1], idx_ref[3]
     rows = []
     for k in range(-3, 4):
@@ -316,110 +312,122 @@
         row = wire_ref[jnp.clip(at, 0, n - 1)]
         rows.append(jnp.where((at >= 0) & (at < n), row, 0.0))
     empty = jnp.zeros((2, 128), F32)
-    lines = []
-    for h in range(2):
+    for h, out_ref in enumerate((n0_ref, n1_ref)):
+        lines = []
         for k in range(6):
             lines.append(rows[k][2 * h + 1 : 2 * h + 2] + rows[k + 1][2 * h : 2 * h + 1])
-        lines.append(empty)
-    block = jnp.concatenate(lines, axis=0)
-    for p in range(out_ref.shape[0]):
-        out_ref[p] = block
+        out_ref[...] = jnp.concatenate(lines + [empty], axis=0)
 
 
 def stack_kernel(y0_ref, y1_ref, y2_ref, y3_ref, y4_ref, out_ref):
     for yc, ref in enumerate((y0_ref, y1_ref, y2_ref, y3_ref, y4_ref)):
-        for zc in range(5):
-            packed = ref[zc * 32 : zc * 32 + 32, :]
-            out_ref[pl.ds(zc * 512 + yc, 32, stride=8), :] = packed
-            out_ref[pl.ds(zc * 512 + 256 + yc, 32, stride=8), :] = pltpu.roll(packed, 64, 1)
-
-
-def join_kernel(z0_ref, z1_ref, z2_ref, z3_ref, z4_ref, out_ref):
-    for zc, ref in enumerate((z0_ref, z1_ref, z2_ref, z3_ref, z4_ref)):
-        out_ref[zc * 32 : zc * 32 + 32, :] = ref[...]
-
-
-def solve_kernel(idx_ref, wire_ref, hess_ref, elem_ref, disp_ref, mis_ref):
-    gz, gy, nz, ny = idx_ref[0], idx_ref[1], idx_ref[2], idx_ref[3]
+        packed = ref[...]
+        out_ref[pl.ds(yc, 32, stride=8), :] = packed
+        out_ref[pl.ds(256 + yc, 32, stride=8), :] = pltpu.roll(packed, 64, 1)
+
+
+def free_lines(idx_ref):
     lane = lanes((8, 128))
-    sub = lax.broadcasted_iota(jnp.int32, (8, 128), 0)
-    zero = jnp.zeros((8, 128), F32)
-    layers = []
-    for k in range(-3, 4):
-        at = gz + k
-        layer = wire_ref[jnp.clip(at, 0, nz - 1)]
-        layers.append(jnp.where((at >= 0) & (at < nz), layer, 0.0))
-    force = [layers[k][8:16] + layers[k + 1][0:8] for k in range(6)]
+    line_y = idx_ref[1] - 2 + lax.broadcasted_iota(jnp.int32, (8, 128), 0)
+    inside = (line_y >= 0) & (line_y < idx_ref[3])
+    free = inside & (lane < 63)
+    return inside, (free, free & (idx_ref[0] < idx_ref[2] - 1))
+
+
+def received(idx_ref, n_refs, lo_ref, hi_ref):
+    below = jnp.where(idx_ref[0] > 0, lo_ref[...], 0.0)
+    above = jnp.where(idx_ref[0] < idx_ref[2] - 1, hi_ref[...], 0.0)
+    return n_refs[0][...] + below, n_refs[1][...] + above
+
+
+def node_first(line, a):
+    return line if a == 0 else pltpu.roll(line, 128 - 21 * a, 1)
+
+
+def apply_hessian(hess_ref, lines, inside):
+    lane = lanes((8, 128))
+    given = {}
+    for h, line in enumerate(lines):
+        for b in range(3):
+            nodes = node_first(line, b)
+            pair = jnp.where(lane < 16, nodes, pltpu.roll(nodes, 15, 1))
+            wide = jnp.where(lane < 32, pair, pltpu.roll(pair, 32, 1))
+            given[h, 0, b] = wide
+            given[h, 1, b] = pltpu.roll(wide, 7, 0)
+    out = {}
+    for a in range(3):
+        for h in range(2):
+            for l in range(2):
+                total = None
+                for b in range(3):
+                    ch = PAIRS.index((min(a, b), max(a, b)))
+                    for hh in range(2):
+                        for ll in range(2):
+                            row = (ch * 9 + (h + hh) * 3 + l + ll) * 8
+                            term = hess_ref[row : row + 8, :] * given[hh, ll, b]
+                            total = term if total is None else total + term
+                out[a, h, l] = jnp.where(inside, total, 0.0)
+    return out
+
+
+def to_lines(found, h):
+    lane = lanes((8, 128))
+    placed = jnp.zeros((8, 128), F32)
+    for a in range(3):
+        total = found[a, h, 0] + pltpu.roll(found[a, h, 1], 1, 0)
+        total = total + pltpu.roll(total, 128 - 16, 1)
+        first = jnp.where(lane < 16, total, 0.0)
+        second = jnp.where((lane >= 1) & (lane < 17), pltpu.roll(total, 128 - 31, 1), 0.0)
+        nodes = first + second
+        placed = placed + (nodes if a == 0 else pltpu.roll(nodes, 21 * a, 1))
+    return placed
+
+
+def first_kernel(idx_ref, n0_ref, n1_ref, lo_ref, hi_ref, hess_ref, u_ref, d_ref, m0_ref, m1_ref):
+    inside, free = free_lines(idx_ref)
+    force = received(idx_ref, (n0_ref, n1_ref), lo_ref, hi_ref)
     diag = [pltpu.roll(v, 64, 1) + 1.0 for v in force]
-    line_y = gy - 2 + sub
-    own_lanes = (lane < 63) & (line_y >= 0) & (line_y < ny)
-    column_y = (line_y >= 0) & (line_y < ny)
-
-    def line_ok(k):
-        return own_lanes & (gz - 2 + k >= 0) & (gz - 2 + k < nz)
-
-    def node_first(line, a):
-        return line if a == 0 else pltpu.roll(line, 128 - 21 * a, 1)
-
-    def operands(lines):
-        out = {}
-        for k, line in lines.items():
-            for b in range(3):
-                nodes = node_first(line, b)
-                pair = jnp.where(lane < 16, nodes, pltpu.roll(nodes, 15, 1))
-                wide = jnp.where(lane < 32, pair, pltpu.roll(pair, 32, 1))
-                out[k, 0, b] = wide
-                out[k, 1, b] = pltpu.roll(wide, 7, 0)
-        return out
-
-    def column(zc, given):
-        ok = column_y & (gz - 2 + zc >= 0) & (gz - 2 + zc < nz)
-        out = {}
-        for a in range(3):
-            for h in range(2):
-                for l in range(2):
-                    total = None
-                    for b in range(3):
-                        ch = PAIRS.index((min(a, b), max(a, b)))
-                        for hh in range(2):
-                            for ll in range(2):
-                                m = ch * 9 + (h + hh) * 3 + l + ll
-                                row = zc * 512 + m * 8
-                                term = hess_ref[row : row + 8, :] * given[zc + hh, ll, b]
-                                total = term if total is None else total + term
-                    out[a, h, l] = jnp.where(ok, total, 0.0)
-        return out
-
-    def pushed(zl, columns):
-        placed = zero
-        for a in range(3):
-            total = zero
-            for h in range(2):
-                found = columns[zl - h]
-                total = total + found[a, h, 0] + pltpu.roll(found[a, h, 1], 1, 0)
-            total = total + pltpu.roll(total, 128 - 16, 1)
-            first = jnp.where(lane < 16, total, 0.0)
-            second = jnp.where((lane >= 1) & (lane < 17), pltpu.roll(total, 128 - 31, 1), 0.0)
-            nodes = first + second
-            placed = placed + (nodes if a == 0 else pltpu.roll(nodes, 21 * a, 1))
-        return placed
-
-    u = {k: jnp.where(line_ok(k), force[k] / diag[k], 0.0) for k in range(6)}
-    for step in range(1, ITERS):
-        given = operands(u)
-        columns = {zc: column(zc, given) for zc in range(step - 1, 6 - step)}
-        u = {
-            k: jnp.where(line_ok(k), u[k] + (force[k] - pushed(k, columns) - u[k]) / diag[k], 0.0)
-            for k in range(step, 6 - step)
-        }
-    given = operands(u)
-    found = column(2, given)
-    total = zero
-    for a in range(3):
-        nodes = node_first(u[2], a)
-        disp_ref[a, 0] = nodes[2:3, 0:17]
+    u = [jnp.where(free[h], force[h] / diag[h], 0.0) for h in range(2)]
+    found = apply_hessian(hess_ref, u, inside)
+    m0_ref[...] = n0_ref[...] - to_lines(found, 0)
+    m1_ref[...] = n1_ref[...] - to_lines(found, 1)
+    for h in range(2):
+        u_ref[h] = u[h]
+        d_ref[h] = diag[h]
+
+
+def advance(idx_ref, m_refs, lo_ref, hi_ref, u_ref, d_ref, free):
+    left = received(idx_ref, m_refs, lo_ref, hi_ref)
+    return [
+        jnp.where(free[h], u_ref[h] + (left[h] - u_ref[h]) / d_ref[h], 0.0) for h in range(2)
+    ]
+
+
+def next_kernel(
+    idx_ref, m0_in, m1_in, lo_ref, hi_ref, n0_ref, n1_ref, u_in, d_ref, hess_ref, u_ref, m0_ref, m1_ref
+):
+    inside, free = free_lines(idx_ref)
+    u = advance(idx_ref, (m0_in, m1_in), lo_ref, hi_ref, u_in, d_ref, free)
+    found = apply_hessian(hess_ref, u, inside)
+    m0_ref[...] = n0_ref[...] - to_lines(found, 0)
+    m1_ref[...] = n1_ref[...] - to_lines(found, 1)
+    for h in range(2):
+        u_ref[h] = u[h]
+
+
+def last_kernel(
+    idx_ref, m0_in, m1_in, lo_ref, hi_ref, u_in, d_ref, hess_ref, elem_ref, disp_ref, mis_ref
+):
+    inside, free = free_lines(idx_ref)
+    u = advance(idx_ref, (m0_in, m1_in), lo_ref, hi_ref, u_in, d_ref, free)
+    found = apply_hessian(hess_ref, u, inside)
+    lane = lanes((8, 128))
+    total = jnp.zeros((8, 128), F32)
+    for a in range(3):
         for h in range(2):
-            nodes = node_first(u[2 + h], a)
+            nodes = node_first(u[h], a)
+            if h == 0:
+                disp_ref[a, 0] = nodes[2:3, 0:17]
             corner = jnp.where(lane < 32, nodes, pltpu.roll(nodes, 31, 1))
             for l in range(2):
                 row = a * 4 + h * 2 + l
@@ -454,10 +462,9 @@
     (outgoing,) = call(
         spread_kernel, [((64, 16, 128), BF16)], partner.reshape(1, 1, EX), source, loaded_scan, smem=(0, 1), vmem=60
     )
-    outgoing, zlo, zhi = lax.optimization_barrier((outgoing, zlo, zhi))
     pieces = lax.all_to_all(outgoing, "gy", split_axis=0, concat_axis=0, tiled=True)
     up, down = call(
-        sides_kernel, [((48, 256), BF16)] * 2, idx, reference_scan, zlo, zhi, side_rows(), smem=(0,)
+        sides_kernel, [((48, 256), BF16)] * 2, idx, reference_scan, zlo, zhi, smem=(0,)
     )
     ylo = shift(up, "gy", 1)
     yhi = shift(down, "gy", -1)
@@ -475,24 +482,35 @@
         flops=4_000_000_000,
         vmem=50,
     )
-    z1, z3 = shift(hess, "gz", 1), shift(hess, "gz", -1)
-    z0, z4 = shift(z1, "gz", 1), shift(z3, "gz", -1)
-    (layers,) = call(join_kernel, [((160, 128), F32)], z0, z1, hess, z3, z4)
-    moved, layers = lax.optimization_barrier((moved, layers))
+    moved, hess = lax.optimization_barrier((moved, hess))
     wire, elem = call(
         forcing_kernel,
         [((n_gy, 4, 128), F32), ((16, 128), F32)],
         moved.reshape(512, 128), turned, slopes, lump, lin_h, lin_l, col_lin,
         scratch=[pltpu.VMEM((256, 256), F32)],
     )
-    wire, layers = lax.optimization_barrier((wire, layers))
+    wire, hess = lax.optimization_barrier((wire, hess))
     rows = lax.all_to_all(wire, "gy", split_axis=0, concat_axis=0, tiled=True)
-    near = [shift(layers, "gy", by) for by in (2, 1)] + [layers] + [shift(layers, "gy", by) for by in (-1, -2)]
-    (stacked,) = call(stack_kernel, [((2560, 128), F32)], *near)
-    (lines,) = call(rows_kernel, [((n_gz, 16, 128), F32)], idx, rows, smem=(0,))
-    lines = lax.all_to_all(lines, "gz", split_axis=0, concat_axis=0, tiled=True)
+    near = [shift(hess, "gy", by) for by in (2, 1)] + [hess] + [shift(hess, "gy", by) for by in (-1, -2)]
+    (stacked,) = call(stack_kernel, [((512, 128), F32)], *near)
+    half, state = ((8, 128), F32), ((2, 8, 128), F32)
+    n0, n1 = call(rows_kernel, [half, half], idx, rows, smem=(0,))
+
+    def arrived(low, high):
+        return low, high, shift(high, "gz", 1), shift(low, "gz", -1)
+
+    u, diag, m0, m1 = call(
+        first_kernel, [state, state, half, half], idx, *arrived(n0, n1), stacked, smem=(0,)
+    )
+    for _ in range(ITERS - 2):
+        u, m0, m1 = call(
+            next_kernel, [state, half, half], idx, *arrived(m0, m1), n0, n1, u, diag, stacked, smem=(0,)
+        )
     disp, mis = call(
-        solve_kernel, [((3, 1, 1, 17), F32), ((1, 1, 16), F32)], idx, lines, stacked, elem, smem=(0,)
+        last_kernel,
+        [((3, 1, 1, 17), F32), ((1, 1, 16), F32)],
+        idx, *arrived(m0, m1), u, diag, stacked, elem,
+        smem=(0,),
     )
     return disp, mis
 

time: 117 us -> 113 us (0.966)
  starting transfers between devices: 83.9 us -> 77 us
  waiting for transfers between devices: 13.5 us -> 17.3 us
    all_to_all x1 -> x0, starting transfers between devices: 8.35 us -> none  [body(): lines = lax.all_to_all(lines, 'gz', split_axis=0, concat_axis=0, tiled=True)]
    all_to_all x1, waiting for transfers between devices: 0.01 us -> 8.16 us  [body(): lax.all_to_all(found.reshape(64, 8, 128), 'gy', split_axis=0, concat_axis...]
    all_to_all x1, starting transfers between devices: 14.3 us -> 6.43 us  [body(): rows = lax.all_to_all(wire, 'gy', split_axis=0, concat_axis=0, tiled=True)]
    all_to_all x1, starting transfers between devices: 14.2 us -> 19.3 us  [body(): lax.all_to_all(outgoing, 'gy', split_axis=0, concat_axis=0, tiled=True)]
    ppermute x12 -> x14, starting transfers between devices: 36.4 us -> 41.4 us  [shift(): lax.ppermute(value, axis, [(i, (i + by) % count) for i in range(count)])]
    all_to_all x1 -> x0, waiting for transfers between devices: 4.61 us -> none  [body(): lines = lax.all_to_all(lines, 'gz', split_axis=0, concat_axis=0, tiled=True)]
    ppermute x12 -> x14, waiting for transfers between devices: 5 us -> 5.94 us  [shift(): lax.ppermute(value, axis, [(i, (i + by) % count) for i in range(count)])]
    unnamed x12 -> x10, local copies, waits for them, and re-layouts: 2.7 us -> 1.82 us
  transfers between devices with their start and end apart: 16 -> 17, of which waited for: 7 -> 11; matrix products, arithmetic and copies ran while one was open for 0% -> 1% of each run, Pallas kernels for 8% -> 6%
where the time goes in v2:
time: 113 us; the launch traced here: 112 us
  starting transfers between devices  77 us (68%)
  waiting for transfers between devices  17.3 us (15%)
  Pallas kernels  14.6 us (13%)
  local copies, waits for them, and re-layouts  2.56 us (2%)
    ppermute x14, starting transfers between devices, shift(): lax.ppermute(value, axis, [(i, (i + by) % count) for i in range(count)])  41.4 us
    all_to_all x1, starting transfers between devices, body(): lax.all_to_all(outgoing, 'gy', split_axis=0, concat_axis=0, tiled=True)  19.3 us
    pallas_call x10, Pallas kernels, call(): pl.pallas_call(kernel, out_shape=[jax.ShapeDtypeStruct(s, d) for s, d in...  14.6 us
    all_to_all x1, starting transfers between devices, body(): lax.all_to_all(found.reshape(64, 8, 128), 'gy', split_axis=0, concat_axis...  9.91 us
    all_to_all x1, waiting for transfers between devices, body(): lax.all_to_all(found.reshape(64, 8, 128), 'gy', split_axis=0, concat_axis...  8.16 us
    all_to_all x1, starting transfers between devices, body(): rows = lax.all_to_all(wire, 'gy', split_axis=0, concat_axis=0, tiled=True)  6.43 us
    ppermute x14, waiting for transfers between devices, shift(): lax.ppermute(value, axis, [(i, (i + by) % count) for i in range(count)])  5.94 us
    all_to_all x1, waiting for transfers between devices, body(): lax.all_to_all(outgoing, 'gy', split_axis=0, concat_axis=0, tiled=True)  3.23 us
  transfers between devices with their start and end apart: 17, of which 11 were waited for; matrix products, arithmetic and copies ran while one was open for 1% of the time, Pallas kernels for 6%

profile of v2, /device:TPU:1, one launch (start us, length us, event | category | flops | bytes accessed | tf_op | source)
XLA Modules:
  0.0 112.4 jit_solution(14375359851244642501)
XLA Ops:
  0.6 1.9 %shard_map.95 = bf16[64,16,128]{2,1,0:T(8,128)(2,1)} custom-call(s32[1,1,16]{2,1,0:T(1,128)} %bitcast.6, s32[1,1,16]{2,1,0:T(1,128)} %source_ref.1, bf16[16,16,256]{2,1,0:T(8,128)(2,1)} %scan_ref.3), custom_call_target="tpu_custom_call" | custom-call | bytes 65536 | tf_op jit(solution)/shard_map/pallas_call | solution.py:133
  2.5 19.3 %all-to-all-start = ((bf16[64,16,128]{2,1,0:T(8,128)(2,1)}), bf16[64,16,128]{2,1,0:T(8,128)(2,1)S(1)}, u32[]{:S(2)}, u32[]{:S(2)}) async-start(bf16[64,16,128]{2,1,0:T(8,128)(2,1)} %shard_map.95), calls=%async_computation | async-start | bytes 524288 | tf_op jit(solution)/shard_map/all_to_all | solution.py:465
  21.8 0.7 fusion
  22.6 1.0 collective-permute-start.1
  23.5 1.1 collective-permute-start
  24.6 0.1 pad_add_fusion.idx_ref
  24.7 1.6 %collective-permute-done.1.hi_ref.zhi_ref = bf16[2,16,256]{2,1,0:T(8,128)(2,1)S(1)} collective-permute-done((bf16[2,16,256]{2,1,0:T(8,128)(2,1)S(1)}, bf16[2,16,256]{2,1,0:T(8,128)(2,1)S(1)}, u32[]{:S(2)}, u32[]{:S(2)}) %collective-permute-start.1) | collective-permute-done | bytes 16416 | tf_op jit(solution)/shard_map/ppermute | solution.py:445
  26.3 0.0 collective-permute-done.lo_ref.zlo_ref
  26.3 0.0 copy-start.2
  26.3 0.9 copy-done.2
  27.3 0.7 shard_map.96
  28.0 3.2 %collective-permute-start.2 = (bf16[48,256]{1,0:T(8,128)(2,1)S(1)}, bf16[48,256]{1,0:T(8,128)(2,1)S(1)}, u32[]{:S(2)}, u32[]{:S(2)}) collective-permute-start(bf16[48,256]{1,0:T(8,128)(2,1)S(1)} %get-tuple-element.29), channel_id=1, source_target_pairs={{0,1},{1,2},{2,3},{3,4},{4,5},{5,6},{6,7},{7,8},{8,9},{9,10},{10,1... | collective-permute-start | bytes 73736 | tf_op jit(solution)/shard_map/ppermute | solution.py:445
  31.2 5.6 %collective-permute-start.3 = (bf16[48,256]{1,0:T(8,128)(2,1)S(1)}, bf16[48,256]{1,0:T(8,128)(2,1)S(1)}, u32[]{:S(2)}, u32[]{:S(2)}) collective-permute-start(bf16[48,256]{1,0:T(8,128)(2,1)S(1)} %get-tuple-element.30), channel_id=1, source_target_pairs={{0,63},{1,0},{2,1},{3,2},{4,3},{5,4},{6,5},{7,6},{8,7},{9,8},{10,9... | collective-permute-start | bytes 73736 | tf_op jit(solution)/shard_map/ppermute | solution.py:445
  36.7 0.9 collective-permute-done.2.ylo_ref
  37.6 0.1 collective-permute-done.3.yhi_ref
  37.7 3.2 %all-to-all-done.in_ref = bf16[64,16,128]{2,1,0:T(8,128)(2,1)S(1)} async-done(((bf16[64,16,128]{2,1,0:T(8,128)(2,1)}), bf16[64,16,128]{2,1,0:T(8,128)(2,1)S(1)}, u32[]{:S(2)}, u32[]{:S(2)}) %all-to-all-start) | async-done | bytes 262176 | tf_op jit(solution)/shard_map/all_to_all | solution.py:465
  40.9 1.3 %shard_map.97 = bf16[512,128]{1,0:T(8,128)(2,1)} custom-call(bf16[64,16,128]{2,1,0:T(8,128)(2,1)S(1)} %all-to-all-done.in_ref), custom_call_target="tpu_custom_call" | custom-call | bytes 65536 | tf_op jit(solution)/shard_map/pallas_call | solution.py:133
  42.2 9.9 %all-to-all-start.1 = ((bf16[64,8,128]{2,1,0:T(8,128)(2,1)}), bf16[64,8,128]{2,1,0:T(8,128)(2,1)S(1)}, u32[]{:S(2)}, u32[]{:S(2)}) async-start(bf16[64,8,128]{2,1,0:T(8,128)(2,1)} %bitcast.3), calls=%async_computation.1 | async-start | bytes 262144 | tf_op jit(solution)/shard_map/all_to_all | solution.py:474
  52.2 0.0 copy-start.3
  52.2 0.9 copy-done.3
  53.1 0.0 copy-start
  53.1 0.0 copy-start.1
  53.1 0.0 copy-start.4
  53.1 4.9 %shard_map.98 = (bf16[256,768]{1,0:T(8,128)(2,1)S(1)}, bf16[256,256]{1,0:T(8,128)(2,1)S(1)}, f32[32,128]{1,0:T(8,128)S(1)}, f32[16,128]{1,0:T(8,128)S(1)}) custom-call(s32[4]{0:T(128)S(1)} %pad_add_fusion.idx_ref, bf16[16,16,256]{2,1,0:T(8,128)(2,1)S(1)} %copy-done.3, bf16[2,16,256]{2,1,0:T(8,128)(2,1)S(1)} %collective-permute-done.lo_ref.zlo_ref, ...), custom_call_target="tpu_custom_call" | custom-call | flops 4000000000 | bytes 65536 | tf_op jit(solution)/shard_map/pallas_call | solution.py:133
  58.0 8.2 %all-to-all-done.1 = bf16[64,8,128]{2,1,0:T(8,128)(2,1)S(1)} async-done(((bf16[64,8,128]{2,1,0:T(8,128)(2,1)}), bf16[64,8,128]{2,1,0:T(8,128)(2,1)S(1)}, u32[]{:S(2)}, u32[]{:S(2)}) %all-to-all-start.1) | async-done | bytes 131104 | tf_op jit(solution)/shard_map/all_to_all | solution.py:474
  66.1 0.0 copy-done
  66.1 0.0 copy-done.1
  66.1 0.0 copy-done.4
  66.1 1.6 %shard_map.99 = (f32[64,4,128]{2,1,0:T(4,128)}, f32[16,128]{1,0:T(8,128)S(1)}) custom-call(bf16[512,128]{1,0:T(8,128)(2,1)S(1)} %bitcast.5, bf16[256,256]{1,0:T(8,128)(2,1)S(1)} %get-tuple-element.39.ref_ref, bf16[256,768]{1,0:T(8,128)(2,1)S(1)} %get-tuple-element.40.slope_ref, f32[16,128]{1,0:T(8,128)S(1)} %get-tuple-element.41.lump_ref, ...), custom_call_target="tpu_custom_call" | custom-call | bytes 65536 | tf_op jit(solution)/shard_map/pallas_call | solution.py:133
  67.7 6.4 %all-to-all-start.2 = ((f32[64,4,128]{2,1,0:T(4,128)}), f32[64,4,128]{2,1,0:T(4,128)S(1)}, u32[]{:S(2)}, u32[]{:S(2)}) async-start(f32[64,4,128]{2,1,0:T(4,128)} %get-tuple-element.44), calls=%async_computation.2 | async-start | bytes 262144 | tf_op jit(solution)/shard_map/all_to_all | solution.py:493
  74.2 7.4 %collective-permute-start.9 = (f32[32,128]{1,0:T(8,128)S(1)}, f32[32,128]{1,0:T(8,128)S(1)}, u32[]{:S(2)}, u32[]{:S(2)}) collective-permute-start(f32[32,128]{1,0:T(8,128)S(1)} %get-tuple-element.47.y2_ref), channel_id=1, source_target_pairs={{0,62},{1,63},{2,0},{3,1},{4,2},{5,3},{6,4},{7,5},{8,6},{9,7},{10,... | collective-permute-start | bytes 49160 | tf_op jit(solution)/shard_map/ppermute | solution.py:445
  81.6 3.1 %collective-permute-start.8 = (f32[32,128]{1,0:T(8,128)S(1)}, f32[32,128]{1,0:T(8,128)S(1)}, u32[]{:S(2)}, u32[]{:S(2)}) collective-permute-start(f32[32,128]{1,0:T(8,128)S(1)} %get-tuple-element.47.y2_ref), channel_id=1, source_target_pairs={{0,63},{1,0},{2,1},{3,2},{4,3},{5,4},{6,5},{7,6},{8,7},{9,8},{10,9... | collective-permute-start | bytes 49160 | tf_op jit(solution)/shard_map/ppermute | solution.py:445
  84.7 2.2 %collective-permute-start.7 = (f32[32,128]{1,0:T(8,128)S(1)}, f32[32,128]{1,0:T(8,128)S(1)}, u32[]{:S(2)}, u32[]{:S(2)}) collective-permute-start(f32[32,128]{1,0:T(8,128)S(1)} %get-tuple-element.47.y2_ref), channel_id=1, source_target_pairs={{0,1},{1,2},{2,3},{3,4},{4,5},{5,6},{6,7},{7,8},{8,9},{9,10},{10,1... | collective-permute-start | bytes 49160 | tf_op jit(solution)/shard_map/ppermute | solution.py:445
  86.9 1.9 %collective-permute-start.6 = (f32[32,128]{1,0:T(8,128)S(1)}, f32[32,128]{1,0:T(8,128)S(1)}, u32[]{:S(2)}, u32[]{:S(2)}) collective-permute-start(f32[32,128]{1,0:T(8,128)S(1)} %get-tuple-element.47.y2_ref), channel_id=1, source_target_pairs={{0,2},{1,3},{2,4},{3,5},{4,6},{5,7},{6,8},{7,9},{8,10},{9,11},{10,... | collective-permute-start | bytes 49160 | tf_op jit(solution)/shard_map/ppermute | solution.py:445
  88.9 0.0 all-to-all-done.2.wire_ref
  88.9 0.6 shard_map.100
  89.5 6.6 %collective-permute-start.5 = (f32[8,128]{1,0:T(8,128)S(1)}, f32[8,128]{1,0:T(8,128)S(1)}, u32[]{:S(2)}, u32[]{:S(2)}) collective-permute-start(f32[8,128]{1,0:T(8,128)S(1)} %get-tuple-element.45.n0_ref), channel_id=1, source_target_pairs={{0,448},{64,0},{128,64},{192,128},{256,192},{320,256},{384,320},{4... | collective-permute-start | bytes 12296 | tf_op jit(solution)/shard_map/ppermute | solution.py:445
  96.1 0.0 collective-permute-done.9.y4_ref
  96.1 0.0 collective-permute-start.4
  96.1 0.0 collective-permute-done.8.y3_ref
  96.1 0.0 collective-permute-done.7.y1_ref
  96.1 0.0 collective-permute-done.6.y0_ref
  96.1 0.1 shard_map.101.hess_ref
  96.2 0.7 collective-permute-done.5.hi_ref
  96.9 0.3 collective-permute-done.4.lo_ref
  97.2 1.1 shard_map.102
  98.3 6.3 %collective-permute-start.11 = (f32[8,128]{1,0:T(8,128)S(1)}, f32[8,128]{1,0:T(8,128)S(1)}, u32[]{:S(2)}, u32[]{:S(2)}) collective-permute-start(f32[8,128]{1,0:T(8,128)S(1)} %get-tuple-element.48.m0_in), channel_id=1, source_target_pairs={{0,448},{64,0},{128,64},{192,128},{256,192},{320,256},{384,320},{4... | collective-permute-start | bytes 12296 | tf_op jit(solution)/shard_map/ppermute | solution.py:445
  104.5 0.0 collective-permute-start.10
  104.5 0.8 collective-permute-done.11.hi_ref
  105.4 0.3 collective-permute-done.10.lo_ref
  105.7 1.0 shard_map.103
  106.7 3.1 %collective-permute-start.13 = (f32[8,128]{1,0:T(8,128)S(1)}, f32[8,128]{1,0:T(8,128)S(1)}, u32[]{:S(2)}, u32[]{:S(2)}) collective-permute-start(f32[8,128]{1,0:T(8,128)S(1)} %get-tuple-element.52.m0_in), channel_id=1, source_target_pairs={{0,448},{64,0},{128,64},{192,128},{256,192},{320,256},{384,320},{4... | collective-permute-start | bytes 12296 | tf_op jit(solution)/shard_map/ppermute | solution.py:445
  109.8 0.0 collective-permute-start.12
  109.8 0.8 collective-permute-done.13.hi_ref
  110.6 0.3 collective-permute-done.12.lo_ref
  110.9 1.4 %shard_map.104 = (f32[3,1,1,17]{3,2,1,0:T(1,128)}, f32[1,1,16]{2,1,0:T(1,128)}) custom-call(s32[4]{0:T(128)S(1)} %pad_add_fusion.idx_ref, f32[8,128]{1,0:T(8,128)S(1)} %get-tuple-element.52.m0_in, f32[8,128]{1,0:T(8,128)S(1)} %get-tuple-element.53.m1_in, f32[8,128]{1,0:T(8,128)S(1)} %collective-permute-done.12.lo_ref, ...), custom_call_target="tpu_custom_call" | custom-call | bytes 65536 | tf_op jit(solution)/shard_map/pallas_call | solution.py:133
Async XLA Ops:
  2.5 38.4 %all-to-all-start = ((bf16[64,16,128]{2,1,0:T(8,128)(2,1)}), bf16[64,16,128]{2,1,0:T(8,128)(2,1)S(1)}, u32[]{:S(2)}, u32[]{:S(2)}) async-start(bf16[64,16,128]{2,1,0:T(8,128)(2,1)} %shard_map.95), calls=%async_computation | async-start | bytes 524288 | tf_op jit(solution)/shard_map/all_to_all | solution.py:465
  22.6 3.8 %collective-permute-start.1 = (bf16[2,16,256]{2,1,0:T(8,128)(2,1)S(1)}, bf16[2,16,256]{2,1,0:T(8,128)(2,1)S(1)}, u32[]{:S(2)}, u32[]{:S(2)}) collective-permute-start(bf16[2,16,256]{2,1,0:T(8,128)(2,1)S(1)} %get-tuple-element.56), channel_id=1, source_target_pairs={{0,448},{64,0},{128,64},{192,128},{256,192},{320,256},{384,320},{4... | collective-permute-start | bytes 49160 | tf_op jit(solution)/shard_map/ppermute | solution.py:445
  23.5 2.8 %collective-permute-start = (bf16[2,16,256]{2,1,0:T(8,128)(2,1)S(1)}, bf16[2,16,256]{2,1,0:T(8,128)(2,1)S(1)}, u32[]{:S(2)}, u32[]{:S(2)}) collective-permute-start(bf16[2,16,256]{2,1,0:T(8,128)(2,1)S(1)} %get-tuple-element.57), channel_id=1, source_target_pairs={{0,64},{64,128},{128,192},{192,256},{256,320},{320,384},{384,448},... | collective-permute-start | bytes 49160 | tf_op jit(solution)/shard_map/ppermute | solution.py:445
  26.3 0.9 copy-start.2
  28.0 9.6 %collective-permute-start.2 = (bf16[48,256]{1,0:T(8,128)(2,1)S(1)}, bf16[48,256]{1,0:T(8,128)(2,1)S(1)}, u32[]{:S(2)}, u32[]{:S(2)}) collective-permute-start(bf16[48,256]{1,0:T(8,128)(2,1)S(1)} %get-tuple-element.29), channel_id=1, source_target_pairs={{0,1},{1,2},{2,3},{3,4},{4,5},{5,6},{6,7},{7,8},{8,9},{9,10},{10,1... | collective-permute-start | bytes 73736 | tf_op jit(solution)/shard_map/ppermute | solution.py:445
  31.2 6.5 %collective-permute-start.3 = (bf16[48,256]{1,0:T(8,128)(2,1)S(1)}, bf16[48,256]{1,0:T(8,128)(2,1)S(1)}, u32[]{:S(2)}, u32[]{:S(2)}) collective-permute-start(bf16[48,256]{1,0:T(8,128)(2,1)S(1)} %get-tuple-element.30), channel_id=1, source_target_pairs={{0,63},{1,0},{2,1},{3,2},{4,3},{5,4},{6,5},{7,6},{8,7},{9,8},{10,9... | collective-permute-start | bytes 73736 | tf_op jit(solution)/shard_map/ppermute | solution.py:445
  42.2 23.9 %all-to-all-start.1 = ((bf16[64,8,128]{2,1,0:T(8,128)(2,1)}), bf16[64,8,128]{2,1,0:T(8,128)(2,1)S(1)}, u32[]{:S(2)}, u32[]{:S(2)}) async-start(bf16[64,8,128]{2,1,0:T(8,128)(2,1)} %bitcast.3), calls=%async_computation.1 | async-start | bytes 262144 | tf_op jit(solution)/shard_map/all_to_all | solution.py:474
  52.2 0.9 copy-start.3
  53.1 13.1 %copy-start = (bf16[1024,128]{1,0:T(8,128)(2,1)S(1)}, bf16[1024,128]{1,0:T(8,128)(2,1)}, u32[]{:S(2)}) copy-start(bf16[1024,128]{1,0:T(8,128)(2,1)} %constant.23.clone.ll_ref) | copy-start | bytes 786436
  53.1 13.1 %copy-start.1 = (bf16[1024,128]{1,0:T(8,128)(2,1)S(1)}, bf16[1024,128]{1,0:T(8,128)(2,1)}, u32[]{:S(2)}) copy-start(bf16[1024,128]{1,0:T(8,128)(2,1)} %constant.22.clone.lh_ref) | copy-start | bytes 786436
  53.1 13.1 %copy-start.4 = (bf16[256,256]{1,0:T(8,128)(2,1)S(1)}, bf16[256,256]{1,0:T(8,128)(2,1)}, u32[]{:S(2)}) copy-start(bf16[256,256]{1,0:T(8,128)(2,1)} %constant.24.clone.clin_ref) | copy-start | bytes 393220
  67.7 21.1 %all-to-all-start.2 = ((f32[64,4,128]{2,1,0:T(4,128)}), f32[64,4,128]{2,1,0:T(4,128)S(1)}, u32[]{:S(2)}, u32[]{:S(2)}) async-start(f32[64,4,128]{2,1,0:T(4,128)} %get-tuple-element.44), calls=%async_computation.2 | async-start | bytes 262144 | tf_op jit(solution)/shard_map/all_to_all | solution.py:493
  74.2 21.9 %collective-permute-start.9 = (f32[32,128]{1,0:T(8,128)S(1)}, f32[32,128]{1,0:T(8,128)S(1)}, u32[]{:S(2)}, u32[]{:S(2)}) collective-permute-start(f32[32,128]{1,0:T(8,128)S(1)} %get-tuple-element.47.y2_ref), channel_id=1, source_target_pairs={{0,62},{1,63},{2,0},{3,1},{4,2},{5,3},{6,4},{7,5},{8,6},{9,7},{10,... | collective-permute-start | bytes 49160 | tf_op jit(solution)/shard_map/ppermute | solution.py:445
  81.6 14.4 %collective-permute-start.8 = (f32[32,128]{1,0:T(8,128)S(1)}, f32[32,128]{1,0:T(8,128)S(1)}, u32[]{:S(2)}, u32[]{:S(2)}) collective-permute-start(f32[32,128]{1,0:T(8,128)S(1)} %get-tuple-element.47.y2_ref), channel_id=1, source_target_pairs={{0,63},{1,0},{2,1},{3,2},{4,3},{5,4},{6,5},{7,6},{8,7},{9,8},{10,9... | collective-permute-start | bytes 49160 | tf_op jit(solution)/shard_map/ppermute | solution.py:445
  84.7 11.3 %collective-permute-start.7 = (f32[32,128]{1,0:T(8,128)S(1)}, f32[32,128]{1,0:T(8,128)S(1)}, u32[]{:S(2)}, u32[]{:S(2)}) collective-permute-start(f32[32,128]{1,0:T(8,128)S(1)} %get-tuple-element.47.y2_ref), channel_id=1, source_target_pairs={{0,1},{1,2},{2,3},{3,4},{4,5},{5,6},{6,7},{7,8},{8,9},{9,10},{10,1... | collective-permute-start | bytes 49160 | tf_op jit(solution)/shard_map/ppermute | solution.py:445
  86.9 9.2 %collective-permute-start.6 = (f32[32,128]{1,0:T(8,128)S(1)}, f32[32,128]{1,0:T(8,128)S(1)}, u32[]{:S(2)}, u32[]{:S(2)}) collective-permute-start(f32[32,128]{1,0:T(8,128)S(1)} %get-tuple-element.47.y2_ref), channel_id=1, source_target_pairs={{0,2},{1,3},{2,4},{3,5},{4,6},{5,7},{6,8},{7,9},{8,10},{9,11},{10,... | collective-permute-start | bytes 49160 | tf_op jit(solution)/shard_map/ppermute | solution.py:445
  89.5 7.4 %collective-permute-start.5 = (f32[8,128]{1,0:T(8,128)S(1)}, f32[8,128]{1,0:T(8,128)S(1)}, u32[]{:S(2)}, u32[]{:S(2)}) collective-permute-start(f32[8,128]{1,0:T(8,128)S(1)} %get-tuple-element.45.n0_ref), channel_id=1, source_target_pairs={{0,448},{64,0},{128,64},{192,128},{256,192},{320,256},{384,320},{4... | collective-permute-start | bytes 12296 | tf_op jit(solution)/shard_map/ppermute | solution.py:445
  96.1 1.2 %collective-permute-start.4 = (f32[8,128]{1,0:T(8,128)S(1)}, f32[8,128]{1,0:T(8,128)S(1)}, u32[]{:S(2)}, u32[]{:S(2)}) collective-permute-start(f32[8,128]{1,0:T(8,128)S(1)} %get-tuple-element.46.n1_ref), channel_id=1, source_target_pairs={{0,64},{64,128},{128,192},{192,256},{256,320},{320,384},{384,448},... | collective-permute-start | bytes 12296 | tf_op jit(solution)/shard_map/ppermute | solution.py:445
  98.3 7.1 %collective-permute-start.11 = (f32[8,128]{1,0:T(8,128)S(1)}, f32[8,128]{1,0:T(8,128)S(1)}, u32[]{:S(2)}, u32[]{:S(2)}) collective-permute-start(f32[8,128]{1,0:T(8,128)S(1)} %get-tuple-element.48.m0_in), channel_id=1, source_target_pairs={{0,448},{64,0},{128,64},{192,128},{256,192},{320,256},{384,320},{4... | collective-permute-start | bytes 12296 | tf_op jit(solution)/shard_map/ppermute | solution.py:445
  104.5 1.2 %collective-permute-start.10 = (f32[8,128]{1,0:T(8,128)S(1)}, f32[8,128]{1,0:T(8,128)S(1)}, u32[]{:S(2)}, u32[]{:S(2)}) collective-permute-start(f32[8,128]{1,0:T(8,128)S(1)} %get-tuple-element.49.m1_in), channel_id=1, source_target_pairs={{0,64},{64,128},{128,192},{192,256},{256,320},{320,384},{384,448},... | collective-permute-start | bytes 12296 | tf_op jit(solution)/shard_map/ppermute | solution.py:445
  106.7 3.9 %collective-permute-start.13 = (f32[8,128]{1,0:T(8,128)S(1)}, f32[8,128]{1,0:T(8,128)S(1)}, u32[]{:S(2)}, u32[]{:S(2)}) collective-permute-start(f32[8,128]{1,0:T(8,128)S(1)} %get-tuple-element.52.m0_in), channel_id=1, source_target_pairs={{0,448},{64,0},{128,64},{192,128},{256,192},{320,256},{384,320},{4... | collective-permute-start | bytes 12296 | tf_op jit(solution)/shard_map/ppermute | solution.py:445
  109.8 1.2 %collective-permute-start.12 = (f32[8,128]{1,0:T(8,128)S(1)}, f32[8,128]{1,0:T(8,128)S(1)}, u32[]{:S(2)}, u32[]{:S(2)}) collective-permute-start(f32[8,128]{1,0:T(8,128)S(1)} %get-tuple-element.53.m1_in), channel_id=1, source_target_pairs={{0,64},{64,128},{128,192},{192,256},{256,320},{320,384},{384,448},... | collective-permute-start | bytes 12296 | tf_op jit(solution)/shard_map/ppermute | solution.py:445

commit v3 on v2

--- a/solution.py
+++ b/solution.py
@@ -35,6 +35,7 @@
         ok = (at >= 0) & (at < NXC)
         smooth[row[ok], at[ok]] = SMOOTH[k + 2]
         slope[row[ok], at[ok]] = DERIVATIVE[k + 2]
+    smooth, slope = smooth[:, place], slope[:, place]
     sh, sl = split(smooth)
     dh, dl = split(slope)
     return np.concatenate([sh, sl, dh, dl])
@@ -203,22 +204,27 @@
     return jnp.where(hit, 1.0, 0.0).astype(BF16)
 
 
-def sides_kernel(idx_ref, scan_ref, lo_ref, hi_ref, up_ref, down_ref):
+def edges_kernel(scan_ref, turned_ref, rows_ref):
+    scan = scan_ref[...].reshape(256, 256)
+    turned_ref[...] = dot_nt(column_order(), scan).astype(BF16)
+    rows_ref[...] = dot(edge_picks(256, 0), scan).astype(BF16)
+
+
+def sides_kernel(idx_ref, rows_ref, lo_ref, hi_ref, up_ref, down_ref):
     gz = idx_ref[0]
     zero = jnp.zeros((32, 256), BF16)
     lo = jnp.where(gz > 0, lo_ref[...].reshape(32, 256), zero)
     hi = jnp.where(gz < idx_ref[2] - 1, hi_ref[...].reshape(32, 256), zero)
-    out = dot(edge_picks(256, 0), scan_ref[...].reshape(256, 256))
-    out = out + dot(edge_picks(32, -2), lo) + dot(edge_picks(32, 16), hi)
-    out = out.astype(BF16)
+    out = dot(edge_picks(32, -2), lo) + dot(edge_picks(32, 16), hi)
+    out = (out + rows_ref[...].astype(F32)).astype(BF16)
     up_ref[...] = out[0:48]
     down_ref[...] = out[48:96]
 
 
 def slopes_kernel(
-    idx_ref, scan_ref, zlo_ref, zhi_ref, ylo_ref, yhi_ref, *refs
+    idx_ref, turned_ref, zlo_ref, zhi_ref, ylo_ref, yhi_ref, *refs
 ):
-    table_ref, slope_ref, ref_ref, hess_ref, lump_ref, held, sems = refs
+    table_ref, slope_ref, hess_ref, lump_ref, held, sems = refs
     copies = []
     for i, (low, high) in enumerate(((0, 1024), (1024, 3520), (3520, 6592))):
         at = slice(low, high)
@@ -226,7 +232,6 @@
     for copy in copies:
         copy.start()
     gz, gy = idx_ref[0], idx_ref[1]
-    scan = scan_ref[...].reshape(256, 256)
     z32 = jnp.zeros((32, 256), BF16)
     z48 = jnp.zeros((48, 256), BF16)
     sides = jnp.concatenate(
@@ -238,10 +243,10 @@
         ],
         axis=0,
     )
-    ref_ref[...] = dot_nt(column_order(), scan).astype(BF16)
+    rim = dot_nt(column_order(), sides).astype(BF16)
     copies[0].wait()
-    mid = dot_nt(held[0:1024, :], scan)
-    rim = dot_nt(held[0:1024, :], sides)
+    mid = dot(held[0:1024, :], turned_ref[...])
+    rim = dot(held[0:1024, :], rim)
     smooth = (mid[0:256] + mid[256:512], rim[0:256] + rim[256:512])
     slope = (mid[512:768] + mid[768:1024], rim[512:768] + rim[768:1024])
     copies[1].wait()
@@ -300,6 +305,7 @@
     elem_ref[...] = out[:, 128:256]
     nodes = out[:, 0:128] + pltpu.roll(lump_ref[...], 64, 1)
     wire = nodes[0:4] + pltpu.roll(nodes[4:8], 21, 1) + pltpu.roll(nodes[8:12], 42, 1)
+    wire = wire.astype(BF16)
     for p in range(wire_ref.shape[0]):
         wire_ref[p] = wire
 
@@ -309,7 +315,7 @@
     rows = []
     for k in range(-3, 4):
         at = gy + k
-        row = wire_ref[jnp.clip(at, 0, n - 1)]
+        row = wire_ref[jnp.clip(at, 0, n - 1)].astype(F32)
         rows.append(jnp.where((at >= 0) & (at < n), row, 0.0))
     empty = jnp.zeros((2, 128), F32)
     for h, out_ref in enumerate((n0_ref, n1_ref)):
@@ -319,9 +325,14 @@
         out_ref[...] = jnp.concatenate(lines + [empty], axis=0)
 
 
-def stack_kernel(y0_ref, y1_ref, y2_ref, y3_ref, y4_ref, out_ref):
-    for yc, ref in enumerate((y0_ref, y1_ref, y2_ref, y3_ref, y4_ref)):
-        packed = ref[...]
+def stack_kernel(idx_ref, own_ref, near_ref, out_ref):
+    layer = pl.multiple_of(idx_ref[0] % 2 * 32, 32)
+    for yc in range(5):
+        if yc == 2:
+            packed = own_ref[...]
+        else:
+            side, step = (1, 2 - yc) if yc < 2 else (0, yc - 2)
+            packed = near_ref[side, pl.ds((step - 1) * 64 + layer, 32), :]
         out_ref[pl.ds(yc, 32, stride=8), :] = packed
         out_ref[pl.ds(256 + yc, 32, stride=8), :] = pltpu.roll(packed, 64, 1)
 
@@ -463,36 +474,47 @@
         spread_kernel, [((64, 16, 128), BF16)], partner.reshape(1, 1, EX), source, loaded_scan, smem=(0, 1), vmem=60
     )
     pieces = lax.all_to_all(outgoing, "gy", split_axis=0, concat_axis=0, tiled=True)
-    up, down = call(
-        sides_kernel, [((48, 256), BF16)] * 2, idx, reference_scan, zlo, zhi, smem=(0,)
-    )
+    turned, inner = call(edges_kernel, [((256, 256), BF16), ((96, 256), BF16)], reference_scan)
+    up, down = call(sides_kernel, [((48, 256), BF16)] * 2, idx, inner, zlo, zhi, smem=(0,))
     ylo = shift(up, "gy", 1)
     yhi = shift(down, "gy", -1)
     pieces, ylo, yhi = lax.optimization_barrier((pieces, ylo, yhi))
     (found,) = call(gather_kernel, [((512, 128), BF16)], pieces)
-    found, ylo, yhi = lax.optimization_barrier((found, ylo, yhi))
+    found, ylo, yhi, turned = lax.optimization_barrier((found, ylo, yhi, turned))
     moved = lax.all_to_all(found.reshape(64, 8, 128), "gy", split_axis=0, concat_axis=0, tiled=True)
-    slopes, turned, hess, lump = call(
+    slopes, hess, lump = call(
         slopes_kernel,
-        [((256, 768), BF16), ((256, 256), BF16), ((32, 128), F32), ((16, 128), F32)],
-        idx, reference_scan, zlo, zhi, ylo, yhi, table,
+        [((256, 768), BF16), ((32, 128), F32), ((16, 128), F32)],
+        idx, turned, zlo, zhi, ylo, yhi, table,
         smem=(0,),
         anywhere=(6,),
         scratch=[pltpu.VMEM(table.shape, BF16), pltpu.SemaphoreType.DMA((3,))],
         flops=4_000_000_000,
-        vmem=50,
-    )
-    moved, hess = lax.optimization_barrier((moved, hess))
+        vmem=52,
+    )
+    pairs = [[k, k + 1] for k in range(0, n_gz, 2)]
+    both = lax.all_gather(hess, "gz", axis_index_groups=pairs, tiled=True)
+    moved, both = lax.optimization_barrier((moved, both))
     wire, elem = call(
         forcing_kernel,
-        [((n_gy, 4, 128), F32), ((16, 128), F32)],
+        [((n_gy, 4, 128), BF16), ((16, 128), F32)],
         moved.reshape(512, 128), turned, slopes, lump, lin_h, lin_l, col_lin,
         scratch=[pltpu.VMEM((256, 256), F32)],
     )
-    wire, hess = lax.optimization_barrier((wire, hess))
+    wire, both = lax.optimization_barrier((wire, both))
     rows = lax.all_to_all(wire, "gy", split_axis=0, concat_axis=0, tiled=True)
-    near = [shift(hess, "gy", by) for by in (2, 1)] + [hess] + [shift(hess, "gy", by) for by in (-1, -2)]
-    (stacked,) = call(stack_kernel, [((512, 128), F32)], *near)
+
+    def beyond(value, by):
+        to = [
+            (z * n_gy + y, z * n_gy + (y + (by if z % 2 else -by)) % n_gy)
+            for z in range(n_gz)
+            for y in range(n_gy)
+        ]
+        return lax.ppermute(value, ("gz", "gy"), to)
+
+    near = jnp.concatenate([beyond(both, 1), beyond(both, 2)])
+    near = lax.all_gather(near, "gz", axis_index_groups=pairs)
+    (stacked,) = call(stack_kernel, [((512, 128), F32)], idx, hess, near, smem=(0,))
     half, state = ((8, 128), F32), ((2, 8, 128), F32)
     n0, n1 = call(rows_kernel, [half, half], idx, rows, smem=(0,))
 

time: 113 us -> 111 us (0.982)
  starting transfers between devices: 77 us -> 65.4 us
  blocking collectives: 0 us -> 8.45 us
    ppermute x14 -> x10, starting transfers between devices: 41.4 us -> 18.1 us  [shift(): lax.ppermute(value, axis, [(i, (i + by) % count) for i in range(count)])]
    all_gather x0 -> x2, blocking collectives: none -> 8.45 us  [the longest x1 6.4 us: body(): both = lax.all_gather(hess, 'gz', axis_index_groups=pairs, tiled=True)]
    ppermute x0 -> x2, starting transfers between devices: none -> 6.91 us  [beyond(): return lax.ppermute(value, ('gz', 'gy'), to)]
    all_to_all x1, starting transfers between devices: 6.43 us -> 12.1 us  [body(): rows = lax.all_to_all(wire, 'gy', split_axis=0, concat_axis=0, tiled=True)]
    all_to_all x1, waiting for transfers between devices: 8.16 us -> 2.75 us  [body(): lax.all_to_all(found.reshape(64, 8, 128), 'gy', split_axis=0, concat_axis...]
    ppermute x0 -> x2, waiting for transfers between devices: none -> 5.29 us  [beyond(): return lax.ppermute(value, ('gz', 'gy'), to)]
    all_to_all x1, waiting for transfers between devices: 0.01 us -> 1.29 us  [body(): rows = lax.all_to_all(wire, 'gy', split_axis=0, concat_axis=0, tiled=True)]
    ppermute x14 -> x10, waiting for transfers between devices: 5.94 us -> 4.87 us  [shift(): lax.ppermute(value, axis, [(i, (i + by) % count) for i in range(count)])]
  transfers between devices with their start and end apart: 17 -> 15, of which waited for: 11 -> 11; matrix products, arithmetic and copies ran while one was open for 1% -> 1% of each run, Pallas kernels for 6% -> 6%
where the time goes in v3:
time: 111 us; the launch traced here: 109 us
  starting transfers between devices  65.4 us (59%)
  waiting for transfers between devices  17.8 us (16%)
  Pallas kernels  15.2 us (14%)
  blocking collectives  8.45 us (8%)
  local copies, waits for them, and re-layouts  1.67 us (2%)
    all_to_all x1, starting transfers between devices, body(): lax.all_to_all(outgoing, 'gy', split_axis=0, concat_axis=0, tiled=True)  19.3 us
    ppermute x10, starting transfers between devices, shift(): lax.ppermute(value, axis, [(i, (i + by) % count) for i in range(count)])  18.1 us
    pallas_call x11, Pallas kernels, call(): pl.pallas_call(kernel, out_shape=[jax.ShapeDtypeStruct(s, d) for s, d in...  15.2 us
    all_to_all x1, starting transfers between devices, body(): rows = lax.all_to_all(wire, 'gy', split_axis=0, concat_axis=0, tiled=True)  12.1 us
    all_to_all x1, starting transfers between devices, body(): lax.all_to_all(found.reshape(64, 8, 128), 'gy', split_axis=0, concat_axis...  8.99 us
    ppermute x2, starting transfers between devices, beyond(): return lax.ppermute(value, ('gz', 'gy'), to)  6.91 us
    all_gather x1, blocking collectives, body(): both = lax.all_gather(hess, 'gz', axis_index_groups=pairs, tiled=True)  6.4 us
    ppermute x2, waiting for transfers between devices, beyond(): return lax.ppermute(value, ('gz', 'gy'), to)  5.29 us
  transfers between devices with their start and end apart: 15, of which 11 were waited for; matrix products, arithmetic and copies ran while one was open for 1% of the time, Pallas kernels for 6%

profile of v3, /device:TPU:1, one launch (start us, length us, event | category | flops | bytes accessed | tf_op | source)
XLA Modules:
  0.0 109.4 jit_solution(10365019724973893231)
XLA Ops:
  0.6 1.9 %shard_map.95 = bf16[64,16,128]{2,1,0:T(8,128)(2,1)} custom-call(s32[1,1,16]{2,1,0:T(1,128)} %bitcast.8, s32[1,1,16]{2,1,0:T(1,128)} %source_ref.1, bf16[16,16,256]{2,1,0:T(8,128)(2,1)} %scan_ref.2), custom_call_target="tpu_custom_call" | custom-call | bytes 65536 | tf_op jit(solution)/shard_map/pallas_call | solution.py:134
  2.5 19.3 %all-to-all-start = ((bf16[64,16,128]{2,1,0:T(8,128)(2,1)}), bf16[64,16,128]{2,1,0:T(8,128)(2,1)S(1)}, u32[]{:S(2)}, u32[]{:S(2)}) async-start(bf16[64,16,128]{2,1,0:T(8,128)(2,1)} %shard_map.95), calls=%async_computation | async-start | bytes 524288 | tf_op jit(solution)/shard_map/all_to_all | solution.py:476
  21.8 0.7 fusion
  22.6 1.0 collective-permute-start.1
  23.5 1.1 %collective-permute-start = (bf16[2,16,256]{2,1,0:T(8,128)(2,1)S(1)}, bf16[2,16,256]{2,1,0:T(8,128)(2,1)S(1)}, u32[]{:S(2)}, u32[]{:S(2)}) collective-permute-start(bf16[2,16,256]{2,1,0:T(8,128)(2,1)S(1)} %get-tuple-element.61), channel_id=1, source_target_pairs={{0,64},{64,128},{128,192},{192,256},{256,320},{320,384},{384,448},... | collective-permute-start | bytes 49160 | tf_op jit(solution)/shard_map/ppermute | solution.py:456
  24.6 0.1 pad_add_fusion.idx_ref
  24.7 0.0 copy-start.2
  24.7 0.9 copy-done.2
  25.6 0.2 shard_map.96
  25.9 0.5 collective-permute-done.1.hi_ref.zhi_ref
  26.3 0.0 collective-permute-done.lo_ref.zlo_ref
  26.3 0.7 shard_map.97
  27.1 3.2 %collective-permute-start.2 = (bf16[48,256]{1,0:T(8,128)(2,1)S(1)}, bf16[48,256]{1,0:T(8,128)(2,1)S(1)}, u32[]{:S(2)}, u32[]{:S(2)}) collective-permute-start(bf16[48,256]{1,0:T(8,128)(2,1)S(1)} %get-tuple-element.32), channel_id=1, source_target_pairs={{0,1},{1,2},{2,3},{3,4},{4,5},{5,6},{6,7},{7,8},{8,9},{9,10},{10,1... | collective-permute-start | bytes 73736 | tf_op jit(solution)/shard_map/ppermute | solution.py:456
  30.3 5.6 %collective-permute-start.3 = (bf16[48,256]{1,0:T(8,128)(2,1)S(1)}, bf16[48,256]{1,0:T(8,128)(2,1)S(1)}, u32[]{:S(2)}, u32[]{:S(2)}) collective-permute-start(bf16[48,256]{1,0:T(8,128)(2,1)S(1)} %get-tuple-element.33), channel_id=1, source_target_pairs={{0,63},{1,0},{2,1},{3,2},{4,3},{5,4},{6,5},{7,6},{8,7},{9,8},{10,9... | collective-permute-start | bytes 73736 | tf_op jit(solution)/shard_map/ppermute | solution.py:456
  35.8 1.5 %collective-permute-done.2.ylo_ref = bf16[48,256]{1,0:T(8,128)(2,1)S(1)} collective-permute-done((bf16[48,256]{1,0:T(8,128)(2,1)S(1)}, bf16[48,256]{1,0:T(8,128)(2,1)S(1)}, u32[]{:S(2)}, u32[]{:S(2)}) %collective-permute-start.2) | collective-permute-done | bytes 24608 | tf_op jit(solution)/shard_map/ppermute | solution.py:456
  37.3 0.0 collective-permute-done.3.yhi_ref
  37.3 3.6 %all-to-all-done.in_ref = bf16[64,16,128]{2,1,0:T(8,128)(2,1)S(1)} async-done(((bf16[64,16,128]{2,1,0:T(8,128)(2,1)}), bf16[64,16,128]{2,1,0:T(8,128)(2,1)S(1)}, u32[]{:S(2)}, u32[]{:S(2)}) %all-to-all-start) | async-done | bytes 262176 | tf_op jit(solution)/shard_map/all_to_all | solution.py:476
  40.9 1.3 %shard_map.98 = bf16[512,128]{1,0:T(8,128)(2,1)} custom-call(bf16[64,16,128]{2,1,0:T(8,128)(2,1)S(1)} %all-to-all-done.in_ref), custom_call_target="tpu_custom_call" | custom-call | bytes 65536 | tf_op jit(solution)/shard_map/pallas_call | solution.py:134
  42.2 9.0 %all-to-all-start.1 = ((bf16[64,8,128]{2,1,0:T(8,128)(2,1)}), bf16[64,8,128]{2,1,0:T(8,128)(2,1)S(1)}, u32[]{:S(2)}, u32[]{:S(2)}) async-start(bf16[64,8,128]{2,1,0:T(8,128)(2,1)} %bitcast.3), calls=%async_computation.1 | async-start | bytes 262144 | tf_op jit(solution)/shard_map/all_to_all | solution.py:484
  51.2 0.0 copy-start
  51.2 0.0 copy-start.1
  51.3 0.0 copy-start.3
  51.3 4.8 %shard_map.99 = (bf16[256,768]{1,0:T(8,128)(2,1)S(1)}, f32[32,128]{1,0:T(8,128)S(1)}, f32[16,128]{1,0:T(8,128)S(1)}) custom-call(s32[4]{0:T(128)S(1)} %pad_add_fusion.idx_ref, bf16[256,256]{1,0:T(8,128)(2,1)S(1)} %get-tuple-element.39.turned_ref.ref_ref, bf16[2,16,256]{2,1,0:T(8,128)(2,1)S(1)} %collective-permute-done.lo_ref.zlo_ref, ...), custom_call_target="tpu_custom_call" | custom-call | flops 4000000000 | bytes 65536 | tf_op jit(solution)/shard_map/pallas_call | solution.py:134
  56.0 6.4 %all_gather.9 = f32[64,128]{1,0:T(8,128)S(1)} all-gather(f32[32,128]{1,0:T(8,128)S(1)} %get-tuple-element.42.own_ref), channel_id=1, replica_groups={{0,64},{128,192},{256,320},{384,448},{1,65},{129,193},{257,321},{385,44..., dimensions={0}, use_global_device_ids=true | all-gather | bytes 49152 | tf_op jit(solution)/shard_map/all_gather | solution.py:496
  62.4 2.7 %all-to-all-done.1 = bf16[64,8,128]{2,1,0:T(8,128)(2,1)S(1)} async-done(((bf16[64,8,128]{2,1,0:T(8,128)(2,1)}), bf16[64,8,128]{2,1,0:T(8,128)(2,1)S(1)}, u32[]{:S(2)}, u32[]{:S(2)}) %all-to-all-start.1) | async-done | bytes 131104 | tf_op jit(solution)/shard_map/all_to_all | solution.py:484
  65.2 0.0 copy-done
  65.2 0.0 copy-done.1
  65.2 0.0 copy-done.3
  65.2 1.6 %shard_map.100 = (bf16[64,4,128]{2,1,0:T(4,128)(2,1)}, f32[16,128]{1,0:T(8,128)S(1)}) custom-call(bf16[512,128]{1,0:T(8,128)(2,1)S(1)} %bitcast.6, bf16[256,256]{1,0:T(8,128)(2,1)S(1)} %get-tuple-element.39.turned_ref.ref_ref, bf16[256,768]{1,0:T(8,128)(2,1)S(1)} %get-tuple-element.44.slope_ref, f32[16,128]{1,0:T(8,128)S(1)} %get-tuple-element.45.lump_ref, ...), custom_call_target="tpu_custom_call" | custom-call | bytes 65536 | tf_op jit(solution)/shard_map/pallas_call | solution.py:134
  66.8 12.1 %all-to-all-start.2 = ((bf16[64,4,128]{2,1,0:T(4,128)(2,1)}), bf16[64,4,128]{2,1,0:T(4,128)(2,1)S(1)}, u32[]{:S(2)}, u32[]{:S(2)}) async-start(bf16[64,4,128]{2,1,0:T(4,128)(2,1)} %get-tuple-element.48), calls=%async_computation.2 | async-start | bytes 131072 | tf_op jit(solution)/shard_map/all_to_all | solution.py:505
  78.9 3.8 %collective-permute-start.7 = (f32[64,128]{1,0:T(8,128)S(1)}, f32[64,128]{1,0:T(8,128)S(1)}, u32[]{:S(2)}, u32[]{:S(2)}) collective-permute-start(f32[64,128]{1,0:T(8,128)S(1)} %all_gather.9), channel_id=1, source_target_pairs={{0,62},{1,63},{2,0},{3,1},{4,2},{5,3},{6,4},{7,5},{8,6},{9,7},{10,... | collective-permute-start | bytes 98312 | tf_op jit(solution)/shard_map/ppermute | solution.py:513
  82.7 3.1 %collective-permute-start.6 = (f32[64,128]{1,0:T(8,128)S(1)}, f32[64,128]{1,0:T(8,128)S(1)}, u32[]{:S(2)}, u32[]{:S(2)}) collective-permute-start(f32[64,128]{1,0:T(8,128)S(1)} %all_gather.9), channel_id=1, source_target_pairs={{0,63},{1,0},{2,1},{3,2},{4,3},{5,4},{6,5},{7,6},{8,7},{9,8},{10,9... | collective-permute-start | bytes 98312 | tf_op jit(solution)/shard_map/ppermute | solution.py:513
  85.8 2.4 %collective-permute-done.7 = f32[64,128]{1,0:T(8,128)S(1)} collective-permute-done((f32[64,128]{1,0:T(8,128)S(1)}, f32[64,128]{1,0:T(8,128)S(1)}, u32[]{:S(2)}, u32[]{:S(2)}) %collective-permute-start.7) | collective-permute-done | bytes 32800 | tf_op jit(solution)/shard_map/ppermute | solution.py:513
  88.3 2.8 %collective-permute-done.6 = f32[64,128]{1,0:T(8,128)S(1)} collective-permute-done((f32[64,128]{1,0:T(8,128)S(1)}, f32[64,128]{1,0:T(8,128)S(1)}, u32[]{:S(2)}, u32[]{:S(2)}) %collective-permute-start.6) | collective-permute-done | bytes 32800 | tf_op jit(solution)/shard_map/ppermute | solution.py:513
  91.1 1.3 %all-to-all-done.2.wire_ref = bf16[64,4,128]{2,1,0:T(4,128)(2,1)S(1)} async-done(((bf16[64,4,128]{2,1,0:T(4,128)(2,1)}), bf16[64,4,128]{2,1,0:T(4,128)(2,1)S(1)}, u32[]{:S(2)}, u32[]{:S(2)}) %all-to-all-start.2) | async-done | bytes 65568 | tf_op jit(solution)/shard_map/all_to_all | solution.py:505
  92.4 0.6 shard_map.101
  93.0 2.0 %collective-permute-start.5 = (f32[8,128]{1,0:T(8,128)S(1)}, f32[8,128]{1,0:T(8,128)S(1)}, u32[]{:S(2)}, u32[]{:S(2)}) collective-permute-start(f32[8,128]{1,0:T(8,128)S(1)} %get-tuple-element.49.n0_ref), channel_id=1, source_target_pairs={{0,448},{64,0},{128,64},{192,128},{256,192},{320,256},{384,320},{4... | collective-permute-start | bytes 12296 | tf_op jit(solution)/shard_map/ppermute | solution.py:456
  95.0 0.0 collective-permute-start.4
  95.0 2.0 %all-gather = f32[256,128]{1,0:T(8,128)S(1)} all-gather(f32[128,128]{1,0:T(8,128)S(1)} %pad_maximum_fusion), channel_id=2, replica_groups={{0,64},{128,192},{256,320},{384,448},{1,65},{129,193},{257,321},{385,44..., dimensions={0}, use_global_device_ids=true | all-gather | bytes 196608 | tf_op jit(solution)/shard_map/all_gather | solution.py:516
  97.0 0.6 shard_map.102.hess_ref
  97.7 0.0 collective-permute-done.5.hi_ref
  97.7 0.0 collective-permute-done.4.lo_ref
  97.7 1.1 shard_map.103
  98.7 1.6 %collective-permute-start.9 = (f32[8,128]{1,0:T(8,128)S(1)}, f32[8,128]{1,0:T(8,128)S(1)}, u32[]{:S(2)}, u32[]{:S(2)}) collective-permute-start(f32[8,128]{1,0:T(8,128)S(1)} %get-tuple-element.52.m0_in), channel_id=1, source_target_pairs={{0,448},{64,0},{128,64},{192,128},{256,192},{320,256},{384,320},{4... | collective-permute-start | bytes 12296 | tf_op jit(solution)/shard_map/ppermute | solution.py:456
  100.3 0.2 collective-permute-start.8
  100.5 1.3 %collective-permute-done.9.hi_ref = f32[8,128]{1,0:T(8,128)S(1)} collective-permute-done((f32[8,128]{1,0:T(8,128)S(1)}, f32[8,128]{1,0:T(8,128)S(1)}, u32[]{:S(2)}, u32[]{:S(2)}) %collective-permute-start.9) | collective-permute-done | bytes 4128 | tf_op jit(solution)/shard_map/ppermute | solution.py:456
  101.8 0.4 collective-permute-done.8.lo_ref
  102.2 1.0 shard_map.104
  103.2 3.6 %collective-permute-start.11 = (f32[8,128]{1,0:T(8,128)S(1)}, f32[8,128]{1,0:T(8,128)S(1)}, u32[]{:S(2)}, u32[]{:S(2)}) collective-permute-start(f32[8,128]{1,0:T(8,128)S(1)} %get-tuple-element.56.m0_in), channel_id=1, source_target_pairs={{0,448},{64,0},{128,64},{192,128},{256,192},{320,256},{384,320},{4... | collective-permute-start | bytes 12296 | tf_op jit(solution)/shard_map/ppermute | solution.py:456
  106.8 0.0 collective-permute-start.10
  106.8 0.8 collective-permute-done.11.hi_ref
  107.6 0.3 collective-permute-done.10.lo_ref
  108.0 1.4 %shard_map.105 = (f32[3,1,1,17]{3,2,1,0:T(1,128)}, f32[1,1,16]{2,1,0:T(1,128)}) custom-call(s32[4]{0:T(128)S(1)} %pad_add_fusion.idx_ref, f32[8,128]{1,0:T(8,128)S(1)} %get-tuple-element.56.m0_in, f32[8,128]{1,0:T(8,128)S(1)} %get-tuple-element.57.m1_in, f32[8,128]{1,0:T(8,128)S(1)} %collective-permute-done.10.lo_ref, ...), custom_call_target="tpu_custom_call" | custom-call | bytes 65536 | tf_op jit(solution)/shard_map/pallas_call | solution.py:134
  (1 shorter events, 0.0 us)
Async XLA Ops:
  2.5 38.4 %all-to-all-start = ((bf16[64,16,128]{2,1,0:T(8,128)(2,1)}), bf16[64,16,128]{2,1,0:T(8,128)(2,1)S(1)}, u32[]{:S(2)}, u32[]{:S(2)}) async-start(bf16[64,16,128]{2,1,0:T(8,128)(2,1)} %shard_map.95), calls=%async_computation | async-start | bytes 524288 | tf_op jit(solution)/shard_map/all_to_all | solution.py:476
  22.6 3.8 %collective-permute-start.1 = (bf16[2,16,256]{2,1,0:T(8,128)(2,1)S(1)}, bf16[2,16,256]{2,1,0:T(8,128)(2,1)S(1)}, u32[]{:S(2)}, u32[]{:S(2)}) collective-permute-start(bf16[2,16,256]{2,1,0:T(8,128)(2,1)S(1)} %get-tuple-element.60), channel_id=1, source_target_pairs={{0,448},{64,0},{128,64},{192,128},{256,192},{320,256},{384,320},{4... | collective-permute-start | bytes 49160 | tf_op jit(solution)/shard_map/ppermute | solution.py:456
  23.5 2.8 %collective-permute-start = (bf16[2,16,256]{2,1,0:T(8,128)(2,1)S(1)}, bf16[2,16,256]{2,1,0:T(8,128)(2,1)S(1)}, u32[]{:S(2)}, u32[]{:S(2)}) collective-permute-start(bf16[2,16,256]{2,1,0:T(8,128)(2,1)S(1)} %get-tuple-element.61), channel_id=1, source_target_pairs={{0,64},{64,128},{128,192},{192,256},{256,320},{320,384},{384,448},... | collective-permute-start | bytes 49160 | tf_op jit(solution)/shard_map/ppermute | solution.py:456
  24.7 0.9 copy-start.2
  27.1 10.2 %collective-permute-start.2 = (bf16[48,256]{1,0:T(8,128)(2,1)S(1)}, bf16[48,256]{1,0:T(8,128)(2,1)S(1)}, u32[]{:S(2)}, u32[]{:S(2)}) collective-permute-start(bf16[48,256]{1,0:T(8,128)(2,1)S(1)} %get-tuple-element.32), channel_id=1, source_target_pairs={{0,1},{1,2},{2,3},{3,4},{4,5},{5,6},{6,7},{7,8},{8,9},{9,10},{10,1... | collective-permute-start | bytes 73736 | tf_op jit(solution)/shard_map/ppermute | solution.py:456
  30.3 7.0 %collective-permute-start.3 = (bf16[48,256]{1,0:T(8,128)(2,1)S(1)}, bf16[48,256]{1,0:T(8,128)(2,1)S(1)}, u32[]{:S(2)}, u32[]{:S(2)}) collective-permute-start(bf16[48,256]{1,0:T(8,128)(2,1)S(1)} %get-tuple-element.33), channel_id=1, source_target_pairs={{0,63},{1,0},{2,1},{3,2},{4,3},{5,4},{6,5},{7,6},{8,7},{9,8},{10,9... | collective-permute-start | bytes 73736 | tf_op jit(solution)/shard_map/ppermute | solution.py:456
  42.2 23.0 %all-to-all-start.1 = ((bf16[64,8,128]{2,1,0:T(8,128)(2,1)}), bf16[64,8,128]{2,1,0:T(8,128)(2,1)S(1)}, u32[]{:S(2)}, u32[]{:S(2)}) async-start(bf16[64,8,128]{2,1,0:T(8,128)(2,1)} %bitcast.3), calls=%async_computation.1 | async-start | bytes 262144 | tf_op jit(solution)/shard_map/all_to_all | solution.py:484
  51.2 14.0 %copy-start = (bf16[1024,128]{1,0:T(8,128)(2,1)S(1)}, bf16[1024,128]{1,0:T(8,128)(2,1)}, u32[]{:S(2)}) copy-start(bf16[1024,128]{1,0:T(8,128)(2,1)} %constant.23.clone.ll_ref) | copy-start | bytes 786436
  51.2 13.9 %copy-start.1 = (bf16[1024,128]{1,0:T(8,128)(2,1)S(1)}, bf16[1024,128]{1,0:T(8,128)(2,1)}, u32[]{:S(2)}) copy-start(bf16[1024,128]{1,0:T(8,128)(2,1)} %constant.22.clone.lh_ref) | copy-start | bytes 786436
  51.3 13.9 %copy-start.3 = (bf16[256,256]{1,0:T(8,128)(2,1)S(1)}, bf16[256,256]{1,0:T(8,128)(2,1)}, u32[]{:S(2)}) copy-start(bf16[256,256]{1,0:T(8,128)(2,1)} %constant.24.clone.clin_ref) | copy-start | bytes 393220
  66.8 25.6 %all-to-all-start.2 = ((bf16[64,4,128]{2,1,0:T(4,128)(2,1)}), bf16[64,4,128]{2,1,0:T(4,128)(2,1)S(1)}, u32[]{:S(2)}, u32[]{:S(2)}) async-start(bf16[64,4,128]{2,1,0:T(4,128)(2,1)} %get-tuple-element.48), calls=%async_computation.2 | async-start | bytes 131072 | tf_op jit(solution)/shard_map/all_to_all | solution.py:505
  78.9 9.4 %collective-permute-start.7 = (f32[64,128]{1,0:T(8,128)S(1)}, f32[64,128]{1,0:T(8,128)S(1)}, u32[]{:S(2)}, u32[]{:S(2)}) collective-permute-start(f32[64,128]{1,0:T(8,128)S(1)} %all_gather.9), channel_id=1, source_target_pairs={{0,62},{1,63},{2,0},{3,1},{4,2},{5,3},{6,4},{7,5},{8,6},{9,7},{10,... | collective-permute-start | bytes 98312 | tf_op jit(solution)/shard_map/ppermute | solution.py:513
  82.7 8.4 %collective-permute-start.6 = (f32[64,128]{1,0:T(8,128)S(1)}, f32[64,128]{1,0:T(8,128)S(1)}, u32[]{:S(2)}, u32[]{:S(2)}) collective-permute-start(f32[64,128]{1,0:T(8,128)S(1)} %all_gather.9), channel_id=1, source_target_pairs={{0,63},{1,0},{2,1},{3,2},{4,3},{5,4},{6,5},{7,6},{8,7},{9,8},{10,9... | collective-permute-start | bytes 98312 | tf_op jit(solution)/shard_map/ppermute | solution.py:513
  93.0 4.7 %collective-permute-start.5 = (f32[8,128]{1,0:T(8,128)S(1)}, f32[8,128]{1,0:T(8,128)S(1)}, u32[]{:S(2)}, u32[]{:S(2)}) collective-permute-start(f32[8,128]{1,0:T(8,128)S(1)} %get-tuple-element.49.n0_ref), channel_id=1, source_target_pairs={{0,448},{64,0},{128,64},{192,128},{256,192},{320,256},{384,320},{4... | collective-permute-start | bytes 12296 | tf_op jit(solution)/shard_map/ppermute | solution.py:456
  95.0 2.7 %collective-permute-start.4 = (f32[8,128]{1,0:T(8,128)S(1)}, f32[8,128]{1,0:T(8,128)S(1)}, u32[]{:S(2)}, u32[]{:S(2)}) collective-permute-start(f32[8,128]{1,0:T(8,128)S(1)} %get-tuple-element.50.n1_ref), channel_id=1, source_target_pairs={{0,64},{64,128},{128,192},{192,256},{256,320},{320,384},{384,448},... | collective-permute-start | bytes 12296 | tf_op jit(solution)/shard_map/ppermute | solution.py:456
  98.7 3.0 %collective-permute-start.9 = (f32[8,128]{1,0:T(8,128)S(1)}, f32[8,128]{1,0:T(8,128)S(1)}, u32[]{:S(2)}, u32[]{:S(2)}) collective-permute-start(f32[8,128]{1,0:T(8,128)S(1)} %get-tuple-element.52.m0_in), channel_id=1, source_target_pairs={{0,448},{64,0},{128,64},{192,128},{256,192},{320,256},{384,320},{4... | collective-permute-start | bytes 12296 | tf_op jit(solution)/shard_map/ppermute | solution.py:456
  100.3 1.9 %collective-permute-start.8 = (f32[8,128]{1,0:T(8,128)S(1)}, f32[8,128]{1,0:T(8,128)S(1)}, u32[]{:S(2)}, u32[]{:S(2)}) collective-permute-start(f32[8,128]{1,0:T(8,128)S(1)} %get-tuple-element.53.m1_in), channel_id=1, source_target_pairs={{0,64},{64,128},{128,192},{192,256},{256,320},{320,384},{384,448},... | collective-permute-start | bytes 12296 | tf_op jit(solution)/shard_map/ppermute | solution.py:456
  103.2 4.4 %collective-permute-start.11 = (f32[8,128]{1,0:T(8,128)S(1)}, f32[8,128]{1,0:T(8,128)S(1)}, u32[]{:S(2)}, u32[]{:S(2)}) collective-permute-start(f32[8,128]{1,0:T(8,128)S(1)} %get-tuple-element.56.m0_in), channel_id=1, source_target_pairs={{0,448},{64,0},{128,64},{192,128},{256,192},{320,256},{384,320},{4... | collective-permute-start | bytes 12296 | tf_op jit(solution)/shard_map/ppermute | solution.py:456
  106.8 1.2 %collective-permute-start.10 = (f32[8,128]{1,0:T(8,128)S(1)}, f32[8,128]{1,0:T(8,128)S(1)}, u32[]{:S(2)}, u32[]{:S(2)}) collective-permute-start(f32[8,128]{1,0:T(8,128)S(1)} %get-tuple-element.57.m1_in), channel_id=1, source_target_pairs={{0,64},{64,128},{128,192},{192,256},{256,320},{320,384},{384,448},... | collective-permute-start | bytes 12296 | tf_op jit(solution)/shard_map/ppermute | solution.py:456

commit v4 on v3

--- a/solution.py
+++ b/solution.py
@@ -46,15 +46,16 @@
     for z in range(16):
         for y in range(16):
             zs.append(z), ys.append(y), real.append(1)
-    for z in (-2, -1, 16, 17):
-        for y in range(16):
-            zs.append(z), ys.append(y), real.append(1)
     for side in (-2, 16):
-        for z in range(-2, 18):
+        for k in range(2):
+            for y in range(-2, 18):
+                zs.append(side + k), ys.append(y), real.append(1)
+        for _ in range(8):
+            zs.append(0), ys.append(0), real.append(0)
+    for side in (-2, 16):
+        for z in range(16):
             for j in range(2):
                 zs.append(z), ys.append(side + j), real.append(1)
-        for _ in range(8):
-            zs.append(0), ys.append(0), real.append(0)
     zs, ys, real = np.array(zs), np.array(ys), np.array(real)
     zo, yo = np.arange(256) // 16, np.arange(256) % 16
     dz, dy = zs[:, None] - zo[None], ys[:, None] - yo[None]
@@ -151,14 +152,14 @@
 def spread_kernel(partner_ref, source_ref, scan_ref, out_ref):
     turned = dot_nt(column_order(), scan_ref[...].reshape(256, 256))
     lane = lanes((8, 128))
-    sub = lax.broadcasted_iota(jnp.int32, (8, 128), 0)
-    group = lane // 32
-    want = jnp.zeros((8, 128), jnp.int32)
+    sub = lax.broadcasted_iota(jnp.int32, (4, 128), 0)
+    group = lanes((4, 128)) // 16
+    want = jnp.zeros((4, 128), jnp.int32)
     for e in range(EX):
-        here = sub == e % 8
-        want = jnp.where(here & (group == e // 8 * 2), partner_ref[0, 0, e], want)
-        want = jnp.where(here & (group == e // 8 * 2 + 1), source_ref[0, 0, e], want)
-    want = want.astype(F32)
+        here = sub == e % 4
+        want = jnp.where(here & (group == e // 4 * 2), partner_ref[0, 0, e], want)
+        want = jnp.where(here & (group == e // 4 * 2 + 1), source_ref[0, 0, e], want)
+    want = want.astype(F32).astype(BF16)
     low = lane < 64
     for c in range(16):
         for v in range(2):
@@ -167,20 +168,23 @@
             p = c * 4 + v * 2
             even = jnp.where(low, a0, pltpu.roll(a1, 64, 1))
             odd = jnp.where(low, pltpu.roll(a0, 64, 1), a1)
-            out_ref[p] = jnp.concatenate([even, want], axis=0).astype(BF16)
-            out_ref[p + 1] = jnp.concatenate([odd, want], axis=0).astype(BF16)
+            for at, piece in ((p, even), (p + 1, odd)):
+                out_ref[at, 0] = piece[0:4].astype(BF16)
+                out_ref[at, 1] = piece[4:8].astype(BF16)
+                out_ref[at, 2] = want
 
 
 def gather_kernel(in_ref, out_ref):
-    seen = in_ref[...].astype(F32)
-    table = seen[:, 0:8, :].reshape(512, 128).astype(BF16)
-    want = seen[:, 8:16, :].reshape(512, 128)
+    parts = [in_ref[:, i].astype(F32) for i in range(3)]
+    table = jnp.concatenate(parts[0:2], axis=1).reshape(512, 128).astype(BF16)
+    asked = jnp.concatenate([parts[2], pltpu.roll(parts[2], 96, 2)], axis=1)
+    want = asked.reshape(512, 128)
     spot = lax.broadcasted_iota(jnp.int32, (512, 512), 1).astype(F32)
     lane = lanes((512, 128))
     halves_out = []
     for half in range(2):
         tile = want[:, half * 64 : half * 64 + 1]
-        block = want[:, half * 64 + 32 : half * 64 + 33]
+        block = want[:, half * 64 + 16 : half * 64 + 17]
         upper = block >= 8.0
         key = tile * 8.0 + jnp.where(upper, block - 8.0, block)
         pick = jnp.where(spot == key, 1.0, 0.0).astype(BF16)
@@ -193,32 +197,45 @@
     out_ref[...] = jnp.where(lane < 64, halves_out[0], halves_out[1]).astype(BF16)
 
 
-def edge_picks(rows, first_z):
-    out = lax.broadcasted_iota(jnp.int32, (96, rows), 0)
-    at = lax.broadcasted_iota(jnp.int32, (96, rows), 1)
-    upper = out >= 48
-    place = jnp.where(upper, out - 48, out)
-    z = place // 2 - 2
-    y = place % 2 + jnp.where(upper, 0, 14)
-    hit = (place < 40) & (at // 16 + first_z == z) & (at % 16 == y)
+def row_picks(source_rows):
+    out = lax.broadcasted_iota(jnp.int32, (64, source_rows), 0)
+    at = lax.broadcasted_iota(jnp.int32, (64, source_rows), 1)
+    z = out % 32 // 2
+    y = out % 2 + jnp.where(out < 32, 14, 0)
+    return jnp.where(at == z * 16 + y, 1.0, 0.0).astype(BF16)
+
+
+def slice_picks(source_rows, place_of):
+    out = lax.broadcasted_iota(jnp.int32, (96, source_rows), 0)
+    at = lax.broadcasted_iota(jnp.int32, (96, source_rows), 1)
+    place = jnp.where(out >= 48, out - 48, out)
+    z = place // 20 + jnp.where(out >= 48, 0, 14)
+    y = place % 20 - 2
+    hit = (place < 40) & (at == place_of(z, y))
     return jnp.where(hit, 1.0, 0.0).astype(BF16)
 
 
-def edges_kernel(scan_ref, turned_ref, rows_ref):
+def edges_kernel(scan_ref, turned_ref, up_ref, down_ref, inner_ref):
     scan = scan_ref[...].reshape(256, 256)
     turned_ref[...] = dot_nt(column_order(), scan).astype(BF16)
-    rows_ref[...] = dot(edge_picks(256, 0), scan).astype(BF16)
-
-
-def sides_kernel(idx_ref, rows_ref, lo_ref, hi_ref, up_ref, down_ref):
-    gz = idx_ref[0]
+    rows = dot(row_picks(256), scan).astype(BF16)
+    up_ref[...] = rows[0:32]
+    down_ref[...] = rows[32:64]
+    inner = slice_picks(256, lambda z, y: jnp.where((y >= 0) & (y < 16), z * 16 + y, -1))
+    inner_ref[...] = dot(inner, scan).astype(BF16)
+
+
+def sides_kernel(idx_ref, inner_ref, lo_ref, hi_ref, last_ref, first_ref):
+    gy = idx_ref[1]
     zero = jnp.zeros((32, 256), BF16)
-    lo = jnp.where(gz > 0, lo_ref[...].reshape(32, 256), zero)
-    hi = jnp.where(gz < idx_ref[2] - 1, hi_ref[...].reshape(32, 256), zero)
-    out = dot(edge_picks(32, -2), lo) + dot(edge_picks(32, 16), hi)
-    out = (out + rows_ref[...].astype(F32)).astype(BF16)
-    up_ref[...] = out[0:48]
-    down_ref[...] = out[48:96]
+    lo = jnp.where(gy > 0, lo_ref[...], zero)
+    hi = jnp.where(gy < idx_ref[3] - 1, hi_ref[...], zero)
+    low = slice_picks(32, lambda z, y: jnp.where(y < 0, z * 2 + y + 2, -1))
+    high = slice_picks(32, lambda z, y: jnp.where(y > 15, z * 2 + y - 16, -1))
+    out = dot(low, lo) + dot(high, hi) + inner_ref[...].astype(F32)
+    out = out.astype(BF16)
+    last_ref[...] = out[0:48]
+    first_ref[...] = out[48:96]
 
 
 def slopes_kernel(
@@ -236,10 +253,10 @@
     z48 = jnp.zeros((48, 256), BF16)
     sides = jnp.concatenate(
         [
-            jnp.where(gz > 0, zlo_ref[...].reshape(32, 256), z32),
-            jnp.where(gz < idx_ref[2] - 1, zhi_ref[...].reshape(32, 256), z32),
-            jnp.where(gy > 0, ylo_ref[...], z48),
-            jnp.where(gy < idx_ref[3] - 1, yhi_ref[...], z48),
+            jnp.where(gz > 0, zlo_ref[...], z48),
+            jnp.where(gz < idx_ref[2] - 1, zhi_ref[...], z48),
+            jnp.where(gy > 0, ylo_ref[...], z32),
+            jnp.where(gy < idx_ref[3] - 1, yhi_ref[...], z32),
         ],
         axis=0,
     )
@@ -262,26 +279,26 @@
         slope_ref[:, a * 256 : a * 256 + 256] = rounded[a]
     g = [v.astype(F32) for v in rounded]
     copies[2].wait()
-    total = jnp.zeros((256, 128), F32)
+    total = jnp.zeros((256, 256), F32)
     for i, (a, b) in enumerate(PAIRS):
-        at = slice(3520 + i * 256, 3776 + i * 256)
-        total = total + dot3(g[a] * g[b], held[at, 0:128], held[at, 128:256])
+        total = total + dot((g[a] * g[b]).astype(BF16), held[3520 + i * 256 : 3776 + i * 256, :])
+    total = total[:, 0:128] + total[:, 128:256]
     pairs = dot3(total.T, held[5056:5312, 0:128], held[5056:5312, 128:256])
     lane = lanes((32, 128))
     hess_ref[...] = jnp.where(lane < 64, pairs[0:32], pltpu.roll(pairs[32:64], 64, 1))
     mags = [jnp.abs(v) for v in g]
     whole = mags[0] + mags[1] + mags[2]
-    lump = jnp.zeros((256, 128), F32)
+    lump = jnp.zeros((256, 256), F32)
     for a in range(3):
         at = slice(5568 + a * 256, 5824 + a * 256)
-        lump = lump + dot3(mags[a] * whole, held[at, 0:128], held[at, 128:256])
-    lh, ll = halves(lump.T)
+        lump = lump + dot((mags[a] * whole).astype(BF16), held[at, :])
+    lh, ll = halves((lump[:, 0:128] + lump[:, 128:256]).T)
     lin = held[5312:5568, 0:128]
     lump_ref[...] = (dot(lh, lin) + dot(ll, lin))[0:16]
 
 
 def forcing_kernel(
-    moved_ref, ref_ref, slope_ref, lump_ref, lh_ref, ll_ref, clin_ref, wire_ref, elem_ref, diff_ref
+    moved_ref, ref_ref, slope_ref, lump_ref, lin_ref, clin_ref, wire_ref, elem_ref, diff_ref
 ):
     low = lanes((8, 128)) < 64
     for c in range(16):
@@ -296,11 +313,13 @@
                 low, pltpu.roll(m0, 64, 1), m1
             )
     diff = ref_ref[...].astype(F32) - diff_ref[...]
-    total = dot3(diff * diff, lh_ref[768:1024, :], ll_ref[768:1024, :])
-    for a in range(3):
+    total = jnp.zeros((256, 256), F32)
+    for a in range(4):
         at = slice(a * 256, a * 256 + 256)
-        total = total + dot3(slope_ref[:, at].astype(F32) * diff, lh_ref[at, :], ll_ref[at, :])
-    h, l = halves(total.T)
+        factor = diff if a == 3 else slope_ref[:, at].astype(F32)
+        h, l = halves(factor * diff)
+        total = total + dot(h, lin_ref[at, :]) + dot(l, lin_ref[at, :])
+    h, l = halves((total[:, 0:128] + total[:, 128:256]).T)
     out = (dot(h, clin_ref[...]) + dot(l, clin_ref[...]))[0:16]
     elem_ref[...] = out[:, 128:256]
     nodes = out[:, 0:128] + pltpu.roll(lump_ref[...], 64, 1)
@@ -468,20 +487,23 @@
     )
     n_gz, n_gy = lax.axis_size("gz"), lax.axis_size("gy")
     idx = jnp.stack([lax.axis_index("gz"), lax.axis_index("gy"), n_gz, n_gy]).astype(jnp.int32)
-    zlo = shift(reference_scan[14:16], "gz", 1)
-    zhi = shift(reference_scan[0:2], "gz", -1)
     (outgoing,) = call(
-        spread_kernel, [((64, 16, 128), BF16)], partner.reshape(1, 1, EX), source, loaded_scan, smem=(0, 1), vmem=60
+        spread_kernel, [((64, 3, 4, 128), BF16)], partner.reshape(1, 1, EX), source, loaded_scan, smem=(0, 1), vmem=60
     )
     pieces = lax.all_to_all(outgoing, "gy", split_axis=0, concat_axis=0, tiled=True)
-    turned, inner = call(edges_kernel, [((256, 256), BF16), ((96, 256), BF16)], reference_scan)
-    up, down = call(sides_kernel, [((48, 256), BF16)] * 2, idx, inner, zlo, zhi, smem=(0,))
+    side, rim = ((32, 256), BF16), ((48, 256), BF16)
+    turned, up, down, inner = call(
+        edges_kernel, [((256, 256), BF16), side, side, ((96, 256), BF16)], reference_scan
+    )
     ylo = shift(up, "gy", 1)
     yhi = shift(down, "gy", -1)
     pieces, ylo, yhi = lax.optimization_barrier((pieces, ylo, yhi))
     (found,) = call(gather_kernel, [((512, 128), BF16)], pieces)
     found, ylo, yhi, turned = lax.optimization_barrier((found, ylo, yhi, turned))
     moved = lax.all_to_all(found.reshape(64, 8, 128), "gy", split_axis=0, concat_axis=0, tiled=True)
+    last, first = call(sides_kernel, [rim, rim], idx, inner, ylo, yhi, smem=(0,))
+    zlo = shift(last, "gz", 1)
+    zhi = shift(first, "gz", -1)
     slopes, hess, lump = call(
         slopes_kernel,
         [((256, 768), BF16), ((32, 128), F32), ((16, 128), F32)],
@@ -498,7 +520,7 @@
     wire, elem = call(
         forcing_kernel,
         [((n_gy, 4, 128), BF16), ((16, 128), F32)],
-        moved.reshape(512, 128), turned, slopes, lump, lin_h, lin_l, col_lin,
+        moved.reshape(512, 128), turned, slopes, lump, beside(lin_h, lin_l), col_lin,
         scratch=[pltpu.VMEM((256, 256), F32)],
     )
     wire, both = lax.optimization_barrier((wire, both))

time: 111 us -> 110 us (level)
  blocking collectives: 8.45 us -> 3.72 us
  starting transfers between devices: 65.4 us -> 68.5 us
  waiting for transfers between devices: 17.8 us -> 20.4 us
    all_gather x1, blocking collectives: 6.4 us -> 1.83 us  [body(): both = lax.all_gather(hess, 'gz', axis_index_groups=pairs, tiled=True)]
    ppermute x10, waiting for transfers between devices: 4.87 us -> 7.67 us  [shift(): lax.ppermute(value, axis, [(i, (i + by) % count) for i in range(count)])]
    all_to_all x1, waiting for transfers between devices: 2.75 us -> 0.35 us  [body(): lax.all_to_all(found.reshape(64, 8, 128), 'gy', split_axis=0, concat_axis...]
    ppermute x10, starting transfers between devices: 18.1 us -> 20.3 us  [shift(): lax.ppermute(value, axis, [(i, (i + by) % count) for i in range(count)])]
    all_to_all x1, waiting for transfers between devices: 3.59 us -> 5.76 us  [body(): lax.all_to_all(outgoing, 'gy', split_axis=0, concat_axis=0, tiled=True)]
    all_to_all x1, starting transfers between devices: 12.1 us -> 14.2 us  [body(): rows = lax.all_to_all(wire, 'gy', split_axis=0, concat_axis=0, tiled=True)]
    all_to_all x1, starting transfers between devices: 8.99 us -> 7.73 us  [body(): lax.all_to_all(found.reshape(64, 8, 128), 'gy', split_axis=0, concat_axis...]
  transfers between devices with their start and end apart: 15 -> 15, of which waited for: 11 -> 12; matrix products, arithmetic and copies ran while one was open for 1% -> 0% of each run, Pallas kernels for 6% -> 5%
where the time goes in v4:
time: 110 us; the launch traced here: 109 us
  starting transfers between devices  68.5 us (62%)
  waiting for transfers between devices  20.4 us (19%)
  Pallas kernels  14.5 us (13%)
  blocking collectives  3.72 us (3%)
    ppermute x10, starting transfers between devices, shift(): lax.ppermute(value, axis, [(i, (i + by) % count) for i in range(count)])  20.3 us
    all_to_all x1, starting transfers between devices, body(): lax.all_to_all(outgoing, 'gy', split_axis=0, concat_axis=0, tiled=True)  19.3 us
    pallas_call x11, Pallas kernels, call(): pl.pallas_call(kernel, out_shape=[jax.ShapeDtypeStruct(s, d) for s, d in...  14.5 us
    all_to_all x1, starting transfers between devices, body(): rows = lax.all_to_all(wire, 'gy', split_axis=0, concat_axis=0, tiled=True)  14.2 us
    all_to_all x1, starting transfers between devices, body(): lax.all_to_all(found.reshape(64, 8, 128), 'gy', split_axis=0, concat_axis...  7.73 us
    ppermute x10, waiting for transfers between devices, shift(): lax.ppermute(value, axis, [(i, (i + by) % count) for i in range(count)])  7.67 us
    ppermute x2, starting transfers between devices, beyond(): return lax.ppermute(value, ('gz', 'gy'), to)  6.91 us
    all_to_all x1, waiting for transfers between devices, body(): lax.all_to_all(outgoing, 'gy', split_axis=0, concat_axis=0, tiled=True)  5.76 us
  transfers between devices with their start and end apart: 15, of which 12 were waited for; matrix products, arithmetic and copies ran while one was open for 0% of the time, Pallas kernels for 5%

profile of v4, /device:TPU:1, one launch (start us, length us, event | category | flops | bytes accessed | tf_op | source)
XLA Modules:
  0.0 108.9 jit_solution(12671902831372700523)
XLA Ops:
  0.6 1.9 %shard_map.86 = bf16[64,3,4,128]{3,2,1,0:T(4,128)(2,1)} custom-call(s32[1,1,16]{2,1,0:T(1,128)} %bitcast.8, s32[1,1,16]{2,1,0:T(1,128)} %source_ref.1, bf16[16,16,256]{2,1,0:T(8,128)(2,1)} %scan_ref.2), custom_call_target="tpu_custom_call" | custom-call | bytes 65536 | tf_op jit(solution)/shard_map/pallas_call | solution.py:135
  2.5 19.3 %all-to-all-start = ((bf16[64,3,4,128]{3,2,1,0:T(4,128)(2,1)}), bf16[64,3,4,128]{3,2,1,0:T(4,128)(2,1)S(1)}, u32[]{:S(2)}, u32[]{:S(2)}) async-start(bf16[64,3,4,128]{3,2,1,0:T(4,128)(2,1)} %shard_map.86), calls=%async_computation | async-start | bytes 393216 | tf_op jit(solution)/shard_map/all_to_all | solution.py:493
  21.8 0.0 copy-start.2
  21.8 0.9 copy-done.2
  22.7 0.3 shard_map.87
  23.0 2.9 %collective-permute-start = (bf16[32,256]{1,0:T(8,128)(2,1)S(1)}, bf16[32,256]{1,0:T(8,128)(2,1)S(1)}, u32[]{:S(2)}, u32[]{:S(2)}) collective-permute-start(bf16[32,256]{1,0:T(8,128)(2,1)S(1)} %get-tuple-element.33), channel_id=1, source_target_pairs={{0,1},{1,2},{2,3},{3,4},{4,5},{5,6},{6,7},{7,8},{8,9},{9,10},{10,1... | collective-permute-start | bytes 49160 | tf_op jit(solution)/shard_map/ppermute | solution.py:475
  25.9 5.7 %collective-permute-start.1 = (bf16[32,256]{1,0:T(8,128)(2,1)S(1)}, bf16[32,256]{1,0:T(8,128)(2,1)S(1)}, u32[]{:S(2)}, u32[]{:S(2)}) collective-permute-start(bf16[32,256]{1,0:T(8,128)(2,1)S(1)} %get-tuple-element.34), channel_id=1, source_target_pairs={{0,63},{1,0},{2,1},{3,2},{4,3},{5,4},{6,5},{7,6},{8,7},{9,8},{10,9... | collective-permute-start | bytes 49160 | tf_op jit(solution)/shard_map/ppermute | solution.py:475
  31.6 1.1 collective-permute-done.lo_ref.ylo_ref
  32.7 0.0 collective-permute-done.1.hi_ref.yhi_ref
  32.7 5.8 %all-to-all-done.in_ref = bf16[64,3,4,128]{3,2,1,0:T(4,128)(2,1)S(1)} async-done(((bf16[64,3,4,128]{3,2,1,0:T(4,128)(2,1)}), bf16[64,3,4,128]{3,2,1,0:T(4,128)(2,1)S(1)}, u32[]{:S(2)}, u32[]{:S(2)}) %all-to-all-start) | async-done | bytes 196640 | tf_op jit(solution)/shard_map/all_to_all | solution.py:493
  38.5 1.4 %shard_map.88 = bf16[512,128]{1,0:T(8,128)(2,1)} custom-call(bf16[64,3,4,128]{3,2,1,0:T(4,128)(2,1)S(1)} %all-to-all-done.in_ref), custom_call_target="tpu_custom_call" | custom-call | bytes 65536 | tf_op jit(solution)/shard_map/pallas_call | solution.py:135
  39.9 7.7 %all-to-all-start.1 = ((bf16[64,8,128]{2,1,0:T(8,128)(2,1)}), bf16[64,8,128]{2,1,0:T(8,128)(2,1)S(1)}, u32[]{:S(2)}, u32[]{:S(2)}) async-start(bf16[64,8,128]{2,1,0:T(8,128)(2,1)} %bitcast.3), calls=%async_computation.1 | async-start | bytes 262144 | tf_op jit(solution)/shard_map/all_to_all | solution.py:503
  47.6 0.1 pad_add_fusion.idx_ref
  47.7 0.7 shard_map.89
  48.4 3.3 %collective-permute-start.2 = (bf16[48,256]{1,0:T(8,128)(2,1)S(1)}, bf16[48,256]{1,0:T(8,128)(2,1)S(1)}, u32[]{:S(2)}, u32[]{:S(2)}) collective-permute-start(bf16[48,256]{1,0:T(8,128)(2,1)S(1)} %get-tuple-element.44), channel_id=1, source_target_pairs={{0,64},{64,128},{128,192},{192,256},{256,320},{320,384},{384,448},... | collective-permute-start | bytes 73736 | tf_op jit(solution)/shard_map/ppermute | solution.py:475
  51.7 0.0 copy-start
  51.7 0.0 copy-start.1
  51.7 0.0 collective-permute-start.3
  51.7 0.9 collective-permute-done.2.zlo_ref
  52.7 2.6 %collective-permute-done.3.zhi_ref = bf16[48,256]{1,0:T(8,128)(2,1)S(1)} collective-permute-done((bf16[48,256]{1,0:T(8,128)(2,1)S(1)}, bf16[48,256]{1,0:T(8,128)(2,1)S(1)}, u32[]{:S(2)}, u32[]{:S(2)}) %collective-permute-start.3) | collective-permute-done | bytes 24608 | tf_op jit(solution)/shard_map/ppermute | solution.py:475
  55.3 4.1 %shard_map.90 = (bf16[256,768]{1,0:T(8,128)(2,1)S(1)}, f32[32,128]{1,0:T(8,128)S(1)}, f32[16,128]{1,0:T(8,128)S(1)}) custom-call(s32[4]{0:T(128)S(1)} %pad_add_fusion.idx_ref, bf16[256,256]{1,0:T(8,128)(2,1)S(1)} %get-tuple-element.40.turned_ref.ref_ref, bf16[48,256]{1,0:T(8,128)(2,1)S(1)} %collective-permute-done.2.zlo_ref, ...), custom_call_target="tpu_custom_call" | custom-call | flops 4000000000 | bytes 65536 | tf_op jit(solution)/shard_map/pallas_call | solution.py:135
  59.4 1.8 %all_gather.9 = f32[64,128]{1,0:T(8,128)S(1)} all-gather(f32[32,128]{1,0:T(8,128)S(1)} %get-tuple-element.46.own_ref), channel_id=1, replica_groups={{0,64},{128,192},{256,320},{384,448},{1,65},{129,193},{257,321},{385,44..., dimensions={0}, use_global_device_ids=true | all-gather | bytes 49152 | tf_op jit(solution)/shard_map/all_gather | solution.py:518
  61.2 0.4 all-to-all-done.1
  61.5 0.0 copy-done
  61.6 0.0 copy-done.1
  61.6 1.5 %shard_map.91 = (bf16[64,4,128]{2,1,0:T(4,128)(2,1)}, f32[16,128]{1,0:T(8,128)S(1)}) custom-call(bf16[512,128]{1,0:T(8,128)(2,1)S(1)} %bitcast.6, bf16[256,256]{1,0:T(8,128)(2,1)S(1)} %get-tuple-element.40.turned_ref.ref_ref, bf16[256,768]{1,0:T(8,128)(2,1)S(1)} %get-tuple-element.48.slope_ref, f32[16,128]{1,0:T(8,128)S(1)} %get-tuple-element.49.lump_ref, ...), custom_call_target="tpu_custom_call" | custom-call | bytes 65536 | tf_op jit(solution)/shard_map/pallas_call | solution.py:135
  63.0 14.2 %all-to-all-start.2 = ((bf16[64,4,128]{2,1,0:T(4,128)(2,1)}), bf16[64,4,128]{2,1,0:T(4,128)(2,1)S(1)}, u32[]{:S(2)}, u32[]{:S(2)}) async-start(bf16[64,4,128]{2,1,0:T(4,128)(2,1)} %get-tuple-element.52), calls=%async_computation.2 | async-start | bytes 131072 | tf_op jit(solution)/shard_map/all_to_all | solution.py:527
  77.2 3.8 %collective-permute-start.7 = (f32[64,128]{1,0:T(8,128)S(1)}, f32[64,128]{1,0:T(8,128)S(1)}, u32[]{:S(2)}, u32[]{:S(2)}) collective-permute-start(f32[64,128]{1,0:T(8,128)S(1)} %all_gather.9), channel_id=1, source_target_pairs={{0,62},{1,63},{2,0},{3,1},{4,2},{5,3},{6,4},{7,5},{8,6},{9,7},{10,... | collective-permute-start | bytes 98312 | tf_op jit(solution)/shard_map/ppermute | solution.py:535
  81.1 3.1 %collective-permute-start.6 = (f32[64,128]{1,0:T(8,128)S(1)}, f32[64,128]{1,0:T(8,128)S(1)}, u32[]{:S(2)}, u32[]{:S(2)}) collective-permute-start(f32[64,128]{1,0:T(8,128)S(1)} %all_gather.9), channel_id=1, source_target_pairs={{0,63},{1,0},{2,1},{3,2},{4,3},{5,4},{6,5},{7,6},{8,7},{9,8},{10,9... | collective-permute-start | bytes 98312 | tf_op jit(solution)/shard_map/ppermute | solution.py:535
  84.2 2.5 %collective-permute-done.7 = f32[64,128]{1,0:T(8,128)S(1)} collective-permute-done((f32[64,128]{1,0:T(8,128)S(1)}, f32[64,128]{1,0:T(8,128)S(1)}, u32[]{:S(2)}, u32[]{:S(2)}) %collective-permute-start.7) | collective-permute-done | bytes 32800 | tf_op jit(solution)/shard_map/ppermute | solution.py:535
  86.7 2.8 %collective-permute-done.6 = f32[64,128]{1,0:T(8,128)S(1)} collective-permute-done((f32[64,128]{1,0:T(8,128)S(1)}, f32[64,128]{1,0:T(8,128)S(1)}, u32[]{:S(2)}, u32[]{:S(2)}) %collective-permute-start.6) | collective-permute-done | bytes 32800 | tf_op jit(solution)/shard_map/ppermute | solution.py:535
  89.5 1.3 %all-to-all-done.2.wire_ref = bf16[64,4,128]{2,1,0:T(4,128)(2,1)S(1)} async-done(((bf16[64,4,128]{2,1,0:T(4,128)(2,1)}), bf16[64,4,128]{2,1,0:T(4,128)(2,1)S(1)}, u32[]{:S(2)}, u32[]{:S(2)}) %all-to-all-start.2) | async-done | bytes 65568 | tf_op jit(solution)/shard_map/all_to_all | solution.py:527
  90.8 0.6 shard_map.92
  91.4 1.9 %collective-permute-start.5 = (f32[8,128]{1,0:T(8,128)S(1)}, f32[8,128]{1,0:T(8,128)S(1)}, u32[]{:S(2)}, u32[]{:S(2)}) collective-permute-start(f32[8,128]{1,0:T(8,128)S(1)} %get-tuple-element.53.n0_ref), channel_id=1, source_target_pairs={{0,448},{64,0},{128,64},{192,128},{256,192},{320,256},{384,320},{4... | collective-permute-start | bytes 12296 | tf_op jit(solution)/shard_map/ppermute | solution.py:475
  93.3 1.1 %collective-permute-start.4 = (f32[8,128]{1,0:T(8,128)S(1)}, f32[8,128]{1,0:T(8,128)S(1)}, u32[]{:S(2)}, u32[]{:S(2)}) collective-permute-start(f32[8,128]{1,0:T(8,128)S(1)} %get-tuple-element.54.n1_ref), channel_id=1, source_target_pairs={{0,64},{64,128},{128,192},{192,256},{256,320},{320,384},{384,448},... | collective-permute-start | bytes 12296 | tf_op jit(solution)/shard_map/ppermute | solution.py:475
  94.4 1.9 %all-gather = f32[256,128]{1,0:T(8,128)S(1)} all-gather(f32[128,128]{1,0:T(8,128)S(1)} %pad_maximum_fusion), channel_id=2, replica_groups={{0,64},{128,192},{256,320},{384,448},{1,65},{129,193},{257,321},{385,44..., dimensions={0}, use_global_device_ids=true | all-gather | bytes 196608 | tf_op jit(solution)/shard_map/all_gather | solution.py:538
  96.3 0.6 shard_map.93.hess_ref
  97.0 0.0 collective-permute-done.5.hi_ref
  97.0 0.0 collective-permute-done.4.lo_ref
  97.0 1.1 shard_map.94
  98.0 1.7 %collective-permute-start.9 = (f32[8,128]{1,0:T(8,128)S(1)}, f32[8,128]{1,0:T(8,128)S(1)}, u32[]{:S(2)}, u32[]{:S(2)}) collective-permute-start(f32[8,128]{1,0:T(8,128)S(1)} %get-tuple-element.56.m0_in), channel_id=1, source_target_pairs={{0,448},{64,0},{128,64},{192,128},{256,192},{320,256},{384,320},{4... | collective-permute-start | bytes 12296 | tf_op jit(solution)/shard_map/ppermute | solution.py:475
  99.8 0.0 collective-permute-start.8
  99.8 1.3 %collective-permute-done.9.hi_ref = f32[8,128]{1,0:T(8,128)S(1)} collective-permute-done((f32[8,128]{1,0:T(8,128)S(1)}, f32[8,128]{1,0:T(8,128)S(1)}, u32[]{:S(2)}, u32[]{:S(2)}) %collective-permute-start.9) | collective-permute-done | bytes 4128 | tf_op jit(solution)/shard_map/ppermute | solution.py:475
  101.1 0.6 collective-permute-done.8.lo_ref
  101.7 1.0 shard_map.95
  102.7 3.6 %collective-permute-start.11 = (f32[8,128]{1,0:T(8,128)S(1)}, f32[8,128]{1,0:T(8,128)S(1)}, u32[]{:S(2)}, u32[]{:S(2)}) collective-permute-start(f32[8,128]{1,0:T(8,128)S(1)} %get-tuple-element.60.m0_in), channel_id=1, source_target_pairs={{0,448},{64,0},{128,64},{192,128},{256,192},{320,256},{384,320},{4... | collective-permute-start | bytes 12296 | tf_op jit(solution)/shard_map/ppermute | solution.py:475
  106.3 0.0 collective-permute-start.10
  106.3 0.8 collective-permute-done.11.hi_ref
  107.1 0.3 collective-permute-done.10.lo_ref
  107.4 1.4 %shard_map.96 = (f32[3,1,1,17]{3,2,1,0:T(1,128)}, f32[1,1,16]{2,1,0:T(1,128)}) custom-call(s32[4]{0:T(128)S(1)} %pad_add_fusion.idx_ref, f32[8,128]{1,0:T(8,128)S(1)} %get-tuple-element.60.m0_in, f32[8,128]{1,0:T(8,128)S(1)} %get-tuple-element.61.m1_in, f32[8,128]{1,0:T(8,128)S(1)} %collective-permute-done.10.lo_ref, ...), custom_call_target="tpu_custom_call" | custom-call | bytes 65536 | tf_op jit(solution)/shard_map/pallas_call | solution.py:135
  (1 shorter events, 0.0 us)
Async XLA Ops:
  2.5 35.9 %all-to-all-start = ((bf16[64,3,4,128]{3,2,1,0:T(4,128)(2,1)}), bf16[64,3,4,128]{3,2,1,0:T(4,128)(2,1)S(1)}, u32[]{:S(2)}, u32[]{:S(2)}) async-start(bf16[64,3,4,128]{3,2,1,0:T(4,128)(2,1)} %shard_map.86), calls=%async_computation | async-start | bytes 393216 | tf_op jit(solution)/shard_map/all_to_all | solution.py:493
  21.8 0.9 copy-start.2
  23.0 9.7 %collective-permute-start = (bf16[32,256]{1,0:T(8,128)(2,1)S(1)}, bf16[32,256]{1,0:T(8,128)(2,1)S(1)}, u32[]{:S(2)}, u32[]{:S(2)}) collective-permute-start(bf16[32,256]{1,0:T(8,128)(2,1)S(1)} %get-tuple-element.33), channel_id=1, source_target_pairs={{0,1},{1,2},{2,3},{3,4},{4,5},{5,6},{6,7},{7,8},{8,9},{9,10},{10,1... | collective-permute-start | bytes 49160 | tf_op jit(solution)/shard_map/ppermute | solution.py:475
  25.9 6.8 %collective-permute-start.1 = (bf16[32,256]{1,0:T(8,128)(2,1)S(1)}, bf16[32,256]{1,0:T(8,128)(2,1)S(1)}, u32[]{:S(2)}, u32[]{:S(2)}) collective-permute-start(bf16[32,256]{1,0:T(8,128)(2,1)S(1)} %get-tuple-element.34), channel_id=1, source_target_pairs={{0,63},{1,0},{2,1},{3,2},{4,3},{5,4},{6,5},{7,6},{8,7},{9,8},{10,9... | collective-permute-start | bytes 49160 | tf_op jit(solution)/shard_map/ppermute | solution.py:475
  39.9 21.7 %all-to-all-start.1 = ((bf16[64,8,128]{2,1,0:T(8,128)(2,1)}), bf16[64,8,128]{2,1,0:T(8,128)(2,1)S(1)}, u32[]{:S(2)}, u32[]{:S(2)}) async-start(bf16[64,8,128]{2,1,0:T(8,128)(2,1)} %bitcast.3), calls=%async_computation.1 | async-start | bytes 262144 | tf_op jit(solution)/shard_map/all_to_all | solution.py:503
  48.4 4.3 %collective-permute-start.2 = (bf16[48,256]{1,0:T(8,128)(2,1)S(1)}, bf16[48,256]{1,0:T(8,128)(2,1)S(1)}, u32[]{:S(2)}, u32[]{:S(2)}) collective-permute-start(bf16[48,256]{1,0:T(8,128)(2,1)S(1)} %get-tuple-element.44), channel_id=1, source_target_pairs={{0,64},{64,128},{128,192},{192,256},{256,320},{320,384},{384,448},... | collective-permute-start | bytes 73736 | tf_op jit(solution)/shard_map/ppermute | solution.py:475
  51.7 9.8 %copy-start = (bf16[1024,256]{1,0:T(8,128)(2,1)S(1)}, bf16[1024,256]{1,0:T(8,128)(2,1)}, u32[]{:S(2)}) copy-start(bf16[1024,256]{1,0:T(8,128)(2,1)} %constant.20.clone.lin_ref) | copy-start | bytes 1572868
  51.7 9.8 %copy-start.1 = (bf16[256,256]{1,0:T(8,128)(2,1)S(1)}, bf16[256,256]{1,0:T(8,128)(2,1)}, u32[]{:S(2)}) copy-start(bf16[256,256]{1,0:T(8,128)(2,1)} %constant.21.clone.clin_ref) | copy-start | bytes 393220
  51.7 3.5 %collective-permute-start.3 = (bf16[48,256]{1,0:T(8,128)(2,1)S(1)}, bf16[48,256]{1,0:T(8,128)(2,1)S(1)}, u32[]{:S(2)}, u32[]{:S(2)}) collective-permute-start(bf16[48,256]{1,0:T(8,128)(2,1)S(1)} %get-tuple-element.45), channel_id=1, source_target_pairs={{0,448},{64,0},{128,64},{192,128},{256,192},{320,256},{384,320},{4... | collective-permute-start | bytes 73736 | tf_op jit(solution)/shard_map/ppermute | solution.py:475
  63.0 27.8 %all-to-all-start.2 = ((bf16[64,4,128]{2,1,0:T(4,128)(2,1)}), bf16[64,4,128]{2,1,0:T(4,128)(2,1)S(1)}, u32[]{:S(2)}, u32[]{:S(2)}) async-start(bf16[64,4,128]{2,1,0:T(4,128)(2,1)} %get-tuple-element.52), calls=%async_computation.2 | async-start | bytes 131072 | tf_op jit(solution)/shard_map/all_to_all | solution.py:527
  77.2 9.4 %collective-permute-start.7 = (f32[64,128]{1,0:T(8,128)S(1)}, f32[64,128]{1,0:T(8,128)S(1)}, u32[]{:S(2)}, u32[]{:S(2)}) collective-permute-start(f32[64,128]{1,0:T(8,128)S(1)} %all_gather.9), channel_id=1, source_target_pairs={{0,62},{1,63},{2,0},{3,1},{4,2},{5,3},{6,4},{7,5},{8,6},{9,7},{10,... | collective-permute-start | bytes 98312 | tf_op jit(solution)/shard_map/ppermute | solution.py:535
  81.1 8.4 %collective-permute-start.6 = (f32[64,128]{1,0:T(8,128)S(1)}, f32[64,128]{1,0:T(8,128)S(1)}, u32[]{:S(2)}, u32[]{:S(2)}) collective-permute-start(f32[64,128]{1,0:T(8,128)S(1)} %all_gather.9), channel_id=1, source_target_pairs={{0,63},{1,0},{2,1},{3,2},{4,3},{5,4},{6,5},{7,6},{8,7},{9,8},{10,9... | collective-permute-start | bytes 98312 | tf_op jit(solution)/shard_map/ppermute | solution.py:535
  91.4 5.6 %collective-permute-start.5 = (f32[8,128]{1,0:T(8,128)S(1)}, f32[8,128]{1,0:T(8,128)S(1)}, u32[]{:S(2)}, u32[]{:S(2)}) collective-permute-start(f32[8,128]{1,0:T(8,128)S(1)} %get-tuple-element.53.n0_ref), channel_id=1, source_target_pairs={{0,448},{64,0},{128,64},{192,128},{256,192},{320,256},{384,320},{4... | collective-permute-start | bytes 12296 | tf_op jit(solution)/shard_map/ppermute | solution.py:475
  93.3 3.7 %collective-permute-start.4 = (f32[8,128]{1,0:T(8,128)S(1)}, f32[8,128]{1,0:T(8,128)S(1)}, u32[]{:S(2)}, u32[]{:S(2)}) collective-permute-start(f32[8,128]{1,0:T(8,128)S(1)} %get-tuple-element.54.n1_ref), channel_id=1, source_target_pairs={{0,64},{64,128},{128,192},{192,256},{256,320},{320,384},{384,448},... | collective-permute-start | bytes 12296 | tf_op jit(solution)/shard_map/ppermute | solution.py:475
  98.0 3.0 %collective-permute-start.9 = (f32[8,128]{1,0:T(8,128)S(1)}, f32[8,128]{1,0:T(8,128)S(1)}, u32[]{:S(2)}, u32[]{:S(2)}) collective-permute-start(f32[8,128]{1,0:T(8,128)S(1)} %get-tuple-element.56.m0_in), channel_id=1, source_target_pairs={{0,448},{64,0},{128,64},{192,128},{256,192},{320,256},{384,320},{4... | collective-permute-start | bytes 12296 | tf_op jit(solution)/shard_map/ppermute | solution.py:475
  99.8 1.9 %collective-permute-start.8 = (f32[8,128]{1,0:T(8,128)S(1)}, f32[8,128]{1,0:T(8,128)S(1)}, u32[]{:S(2)}, u32[]{:S(2)}) collective-permute-start(f32[8,128]{1,0:T(8,128)S(1)} %get-tuple-element.57.m1_in), channel_id=1, source_target_pairs={{0,64},{64,128},{128,192},{192,256},{256,320},{320,384},{384,448},... | collective-permute-start | bytes 12296 | tf_op jit(solution)/shard_map/ppermute | solution.py:475
  102.7 4.4 %collective-permute-start.11 = (f32[8,128]{1,0:T(8,128)S(1)}, f32[8,128]{1,0:T(8,128)S(1)}, u32[]{:S(2)}, u32[]{:S(2)}) collective-permute-start(f32[8,128]{1,0:T(8,128)S(1)} %get-tuple-element.60.m0_in), channel_id=1, source_target_pairs={{0,448},{64,0},{128,64},{192,128},{256,192},{320,256},{384,320},{4... | collective-permute-start | bytes 12296 | tf_op jit(solution)/shard_map/ppermute | solution.py:475
  106.3 1.2 %collective-permute-start.10 = (f32[8,128]{1,0:T(8,128)S(1)}, f32[8,128]{1,0:T(8,128)S(1)}, u32[]{:S(2)}, u32[]{:S(2)}) collective-permute-start(f32[8,128]{1,0:T(8,128)S(1)} %get-tuple-element.61.m1_in), channel_id=1, source_target_pairs={{0,64},{64,128},{128,192},{192,256},{256,320},{320,384},{384,448},... | collective-permute-start | bytes 12296 | tf_op jit(solution)/shard_map/ppermute | solution.py:475

commit v5 on v4

--- a/solution.py
+++ b/solution.py
@@ -246,8 +246,7 @@
     for i, (low, high) in enumerate(((0, 1024), (1024, 3520), (3520, 6592))):
         at = slice(low, high)
         copies.append(pltpu.make_async_copy(table_ref.at[at], held.at[at], sems.at[i]))
-    for copy in copies:
-        copy.start()
+    copies[0].start()
     gz, gy = idx_ref[0], idx_ref[1]
     z32 = jnp.zeros((32, 256), BF16)
     z48 = jnp.zeros((48, 256), BF16)
@@ -262,6 +261,8 @@
     )
     rim = dot_nt(column_order(), sides).astype(BF16)
     copies[0].wait()
+    copies[1].start()
+    copies[2].start()
     mid = dot(held[0:1024, :], turned_ref[...])
     rim = dot(held[0:1024, :], rim)
     smooth = (mid[0:256] + mid[256:512], rim[0:256] + rim[256:512])

time: 110 us -> 111 us (level)
  transfers between devices with their start and end apart: 15 -> 15, of which waited for: 12 -> 11; matrix products, arithmetic and copies ran while one was open for 0% -> 0% of each run, Pallas kernels for 5% -> 6%
where the time goes in v5:
time: 111 us; the launch traced here: 110 us
  starting transfers between devices  68.8 us (62%)
  waiting for transfers between devices  20.1 us (18%)
  Pallas kernels  15.3 us (14%)
  blocking collectives  3.72 us (3%)
    ppermute x10, starting transfers between devices, shift(): lax.ppermute(value, axis, [(i, (i + by) % count) for i in range(count)])  20.3 us
    all_to_all x1, starting transfers between devices, body(): lax.all_to_all(outgoing, 'gy', split_axis=0, concat_axis=0, tiled=True)  19.3 us
    pallas_call x11, Pallas kernels, call(): pl.pallas_call(kernel, out_shape=[jax.ShapeDtypeStruct(s, d) for s, d in...  15.3 us
    all_to_all x1, starting transfers between devices, body(): rows = lax.all_to_all(wire, 'gy', split_axis=0, concat_axis=0, tiled=True)  14.6 us
    all_to_all x1, starting transfers between devices, body(): lax.all_to_all(found.reshape(64, 8, 128), 'gy', split_axis=0, concat_axis...  7.73 us
    ppermute x10, waiting for transfers between devices, shift(): lax.ppermute(value, axis, [(i, (i + by) % count) for i in range(count)])  7.67 us
    ppermute x2, starting transfers between devices, beyond(): return lax.ppermute(value, ('gz', 'gy'), to)  6.91 us
    all_to_all x1, waiting for transfers between devices, body(): lax.all_to_all(outgoing, 'gy', split_axis=0, concat_axis=0, tiled=True)  5.76 us
  transfers between devices with their start and end apart: 15, of which 11 were waited for; matrix products, arithmetic and copies ran while one was open for 0% of the time, Pallas kernels for 6%

profile of v5, /device:TPU:1, one launch (start us, length us, event | category | flops | bytes accessed | tf_op | source)
XLA Modules:
  0.0 109.7 jit_solution(7394803463422991712)
XLA Ops:
  0.6 1.9 %shard_map.86 = bf16[64,3,4,128]{3,2,1,0:T(4,128)(2,1)} custom-call(s32[1,1,16]{2,1,0:T(1,128)} %bitcast.8, s32[1,1,16]{2,1,0:T(1,128)} %source_ref.1, bf16[16,16,256]{2,1,0:T(8,128)(2,1)} %scan_ref.2), custom_call_target="tpu_custom_call" | custom-call | bytes 65536 | tf_op jit(solution)/shard_map/pallas_call | solution.py:135
  2.5 19.3 %all-to-all-start = ((bf16[64,3,4,128]{3,2,1,0:T(4,128)(2,1)}), bf16[64,3,4,128]{3,2,1,0:T(4,128)(2,1)S(1)}, u32[]{:S(2)}, u32[]{:S(2)}) async-start(bf16[64,3,4,128]{3,2,1,0:T(4,128)(2,1)} %shard_map.86), calls=%async_computation | async-start | bytes 393216 | tf_op jit(solution)/shard_map/all_to_all | solution.py:494
  21.8 0.0 copy-start.2
  21.8 0.9 copy-done.2
  22.7 0.3 shard_map.87
  23.0 2.9 %collective-permute-start = (bf16[32,256]{1,0:T(8,128)(2,1)S(1)}, bf16[32,256]{1,0:T(8,128)(2,1)S(1)}, u32[]{:S(2)}, u32[]{:S(2)}) collective-permute-start(bf16[32,256]{1,0:T(8,128)(2,1)S(1)} %get-tuple-element.33), channel_id=1, source_target_pairs={{0,1},{1,2},{2,3},{3,4},{4,5},{5,6},{6,7},{7,8},{8,9},{9,10},{10,1... | collective-permute-start | bytes 49160 | tf_op jit(solution)/shard_map/ppermute | solution.py:476
  25.9 5.7 %collective-permute-start.1 = (bf16[32,256]{1,0:T(8,128)(2,1)S(1)}, bf16[32,256]{1,0:T(8,128)(2,1)S(1)}, u32[]{:S(2)}, u32[]{:S(2)}) collective-permute-start(bf16[32,256]{1,0:T(8,128)(2,1)S(1)} %get-tuple-element.34), channel_id=1, source_target_pairs={{0,63},{1,0},{2,1},{3,2},{4,3},{5,4},{6,5},{7,6},{8,7},{9,8},{10,9... | collective-permute-start | bytes 49160 | tf_op jit(solution)/shard_map/ppermute | solution.py:476
  31.6 1.1 collective-permute-done.lo_ref.ylo_ref
  32.7 0.0 collective-permute-done.1.hi_ref.yhi_ref
  32.7 5.8 %all-to-all-done.in_ref = bf16[64,3,4,128]{3,2,1,0:T(4,128)(2,1)S(1)} async-done(((bf16[64,3,4,128]{3,2,1,0:T(4,128)(2,1)}), bf16[64,3,4,128]{3,2,1,0:T(4,128)(2,1)S(1)}, u32[]{:S(2)}, u32[]{:S(2)}) %all-to-all-start) | async-done | bytes 196640 | tf_op jit(solution)/shard_map/all_to_all | solution.py:494
  38.5 1.4 %shard_map.88 = bf16[512,128]{1,0:T(8,128)(2,1)} custom-call(bf16[64,3,4,128]{3,2,1,0:T(4,128)(2,1)S(1)} %all-to-all-done.in_ref), custom_call_target="tpu_custom_call" | custom-call | bytes 65536 | tf_op jit(solution)/shard_map/pallas_call | solution.py:135
  39.9 7.7 %all-to-all-start.1 = ((bf16[64,8,128]{2,1,0:T(8,128)(2,1)}), bf16[64,8,128]{2,1,0:T(8,128)(2,1)S(1)}, u32[]{:S(2)}, u32[]{:S(2)}) async-start(bf16[64,8,128]{2,1,0:T(8,128)(2,1)} %bitcast.3), calls=%async_computation.1 | async-start | bytes 262144 | tf_op jit(solution)/shard_map/all_to_all | solution.py:504
  47.6 0.1 pad_add_fusion.idx_ref
  47.7 0.7 shard_map.89
  48.4 3.3 %collective-permute-start.2 = (bf16[48,256]{1,0:T(8,128)(2,1)S(1)}, bf16[48,256]{1,0:T(8,128)(2,1)S(1)}, u32[]{:S(2)}, u32[]{:S(2)}) collective-permute-start(bf16[48,256]{1,0:T(8,128)(2,1)S(1)} %get-tuple-element.44), channel_id=1, source_target_pairs={{0,64},{64,128},{128,192},{192,256},{256,320},{320,384},{384,448},... | collective-permute-start | bytes 73736 | tf_op jit(solution)/shard_map/ppermute | solution.py:476
  51.7 0.0 copy-start
  51.7 0.0 copy-start.1
  51.7 0.0 collective-permute-start.3
  51.7 0.9 collective-permute-done.2.zlo_ref
  52.7 2.6 %collective-permute-done.3.zhi_ref = bf16[48,256]{1,0:T(8,128)(2,1)S(1)} collective-permute-done((bf16[48,256]{1,0:T(8,128)(2,1)S(1)}, bf16[48,256]{1,0:T(8,128)(2,1)S(1)}, u32[]{:S(2)}, u32[]{:S(2)}) %collective-permute-start.3) | collective-permute-done | bytes 24608 | tf_op jit(solution)/shard_map/ppermute | solution.py:476
  55.3 4.9 %shard_map.90 = (bf16[256,768]{1,0:T(8,128)(2,1)S(1)}, f32[32,128]{1,0:T(8,128)S(1)}, f32[16,128]{1,0:T(8,128)S(1)}) custom-call(s32[4]{0:T(128)S(1)} %pad_add_fusion.idx_ref, bf16[256,256]{1,0:T(8,128)(2,1)S(1)} %get-tuple-element.40.turned_ref.ref_ref, bf16[48,256]{1,0:T(8,128)(2,1)S(1)} %collective-permute-done.2.zlo_ref, ...), custom_call_target="tpu_custom_call" | custom-call | flops 4000000000 | bytes 65536 | tf_op jit(solution)/shard_map/pallas_call | solution.py:135
  60.2 1.8 %all_gather.9 = f32[64,128]{1,0:T(8,128)S(1)} all-gather(f32[32,128]{1,0:T(8,128)S(1)} %get-tuple-element.46.own_ref), channel_id=1, replica_groups={{0,64},{128,192},{256,320},{384,448},{1,65},{129,193},{257,321},{385,44..., dimensions={0}, use_global_device_ids=true | all-gather | bytes 49152 | tf_op jit(solution)/shard_map/all_gather | solution.py:519
  62.0 0.0 all-to-all-done.1
  62.0 0.0 copy-done
  62.0 0.0 copy-done.1
  62.0 1.5 %shard_map.91 = (bf16[64,4,128]{2,1,0:T(4,128)(2,1)}, f32[16,128]{1,0:T(8,128)S(1)}) custom-call(bf16[512,128]{1,0:T(8,128)(2,1)S(1)} %bitcast.6, bf16[256,256]{1,0:T(8,128)(2,1)S(1)} %get-tuple-element.40.turned_ref.ref_ref, bf16[256,768]{1,0:T(8,128)(2,1)S(1)} %get-tuple-element.48.slope_ref, f32[16,128]{1,0:T(8,128)S(1)} %get-tuple-element.49.lump_ref, ...), custom_call_target="tpu_custom_call" | custom-call | bytes 65536 | tf_op jit(solution)/shard_map/pallas_call | solution.py:135
  63.5 14.6 %all-to-all-start.2 = ((bf16[64,4,128]{2,1,0:T(4,128)(2,1)}), bf16[64,4,128]{2,1,0:T(4,128)(2,1)S(1)}, u32[]{:S(2)}, u32[]{:S(2)}) async-start(bf16[64,4,128]{2,1,0:T(4,128)(2,1)} %get-tuple-element.52), calls=%async_computation.2 | async-start | bytes 131072 | tf_op jit(solution)/shard_map/all_to_all | solution.py:528
  78.0 3.8 %collective-permute-start.7 = (f32[64,128]{1,0:T(8,128)S(1)}, f32[64,128]{1,0:T(8,128)S(1)}, u32[]{:S(2)}, u32[]{:S(2)}) collective-permute-start(f32[64,128]{1,0:T(8,128)S(1)} %all_gather.9), channel_id=1, source_target_pairs={{0,62},{1,63},{2,0},{3,1},{4,2},{5,3},{6,4},{7,5},{8,6},{9,7},{10,... | collective-permute-start | bytes 98312 | tf_op jit(solution)/shard_map/ppermute | solution.py:536
  81.9 3.1 %collective-permute-start.6 = (f32[64,128]{1,0:T(8,128)S(1)}, f32[64,128]{1,0:T(8,128)S(1)}, u32[]{:S(2)}, u32[]{:S(2)}) collective-permute-start(f32[64,128]{1,0:T(8,128)S(1)} %all_gather.9), channel_id=1, source_target_pairs={{0,63},{1,0},{2,1},{3,2},{4,3},{5,4},{6,5},{7,6},{8,7},{9,8},{10,9... | collective-permute-start | bytes 98312 | tf_op jit(solution)/shard_map/ppermute | solution.py:536
  85.0 2.5 %collective-permute-done.7 = f32[64,128]{1,0:T(8,128)S(1)} collective-permute-done((f32[64,128]{1,0:T(8,128)S(1)}, f32[64,128]{1,0:T(8,128)S(1)}, u32[]{:S(2)}, u32[]{:S(2)}) %collective-permute-start.7) | collective-permute-done | bytes 32800 | tf_op jit(solution)/shard_map/ppermute | solution.py:536
  87.5 2.8 %collective-permute-done.6 = f32[64,128]{1,0:T(8,128)S(1)} collective-permute-done((f32[64,128]{1,0:T(8,128)S(1)}, f32[64,128]{1,0:T(8,128)S(1)}, u32[]{:S(2)}, u32[]{:S(2)}) %collective-permute-start.6) | collective-permute-done | bytes 32800 | tf_op jit(solution)/shard_map/ppermute | solution.py:536
  90.3 1.3 %all-to-all-done.2.wire_ref = bf16[64,4,128]{2,1,0:T(4,128)(2,1)S(1)} async-done(((bf16[64,4,128]{2,1,0:T(4,128)(2,1)}), bf16[64,4,128]{2,1,0:T(4,128)(2,1)S(1)}, u32[]{:S(2)}, u32[]{:S(2)}) %all-to-all-start.2) | async-done | bytes 65568 | tf_op jit(solution)/shard_map/all_to_all | solution.py:528
  91.6 0.6 shard_map.92
  92.2 1.9 %collective-permute-start.5 = (f32[8,128]{1,0:T(8,128)S(1)}, f32[8,128]{1,0:T(8,128)S(1)}, u32[]{:S(2)}, u32[]{:S(2)}) collective-permute-start(f32[8,128]{1,0:T(8,128)S(1)} %get-tuple-element.53.n0_ref), channel_id=1, source_target_pairs={{0,448},{64,0},{128,64},{192,128},{256,192},{320,256},{384,320},{4... | collective-permute-start | bytes 12296 | tf_op jit(solution)/shard_map/ppermute | solution.py:476
  94.1 1.1 %collective-permute-start.4 = (f32[8,128]{1,0:T(8,128)S(1)}, f32[8,128]{1,0:T(8,128)S(1)}, u32[]{:S(2)}, u32[]{:S(2)}) collective-permute-start(f32[8,128]{1,0:T(8,128)S(1)} %get-tuple-element.54.n1_ref), channel_id=1, source_target_pairs={{0,64},{64,128},{128,192},{192,256},{256,320},{320,384},{384,448},... | collective-permute-start | bytes 12296 | tf_op jit(solution)/shard_map/ppermute | solution.py:476
  95.2 1.9 %all-gather = f32[256,128]{1,0:T(8,128)S(1)} all-gather(f32[128,128]{1,0:T(8,128)S(1)} %pad_maximum_fusion), channel_id=2, replica_groups={{0,64},{128,192},{256,320},{384,448},{1,65},{129,193},{257,321},{385,44..., dimensions={0}, use_global_device_ids=true | all-gather | bytes 196608 | tf_op jit(solution)/shard_map/all_gather | solution.py:539
  97.1 0.6 shard_map.93.hess_ref
  97.8 0.0 collective-permute-done.5.hi_ref
  97.8 0.0 collective-permute-done.4.lo_ref
  97.8 1.1 shard_map.94
  98.8 1.7 %collective-permute-start.9 = (f32[8,128]{1,0:T(8,128)S(1)}, f32[8,128]{1,0:T(8,128)S(1)}, u32[]{:S(2)}, u32[]{:S(2)}) collective-permute-start(f32[8,128]{1,0:T(8,128)S(1)} %get-tuple-element.56.m0_in), channel_id=1, source_target_pairs={{0,448},{64,0},{128,64},{192,128},{256,192},{320,256},{384,320},{4... | collective-permute-start | bytes 12296 | tf_op jit(solution)/shard_map/ppermute | solution.py:476
  100.6 0.0 collective-permute-start.8
  100.6 1.3 %collective-permute-done.9.hi_ref = f32[8,128]{1,0:T(8,128)S(1)} collective-permute-done((f32[8,128]{1,0:T(8,128)S(1)}, f32[8,128]{1,0:T(8,128)S(1)}, u32[]{:S(2)}, u32[]{:S(2)}) %collective-permute-start.9) | collective-permute-done | bytes 4128 | tf_op jit(solution)/shard_map/ppermute | solution.py:476
  101.9 0.6 collective-permute-done.8.lo_ref
  102.5 1.0 shard_map.95
  103.5 3.6 %collective-permute-start.11 = (f32[8,128]{1,0:T(8,128)S(1)}, f32[8,128]{1,0:T(8,128)S(1)}, u32[]{:S(2)}, u32[]{:S(2)}) collective-permute-start(f32[8,128]{1,0:T(8,128)S(1)} %get-tuple-element.60.m0_in), channel_id=1, source_target_pairs={{0,448},{64,0},{128,64},{192,128},{256,192},{320,256},{384,320},{4... | collective-permute-start | bytes 12296 | tf_op jit(solution)/shard_map/ppermute | solution.py:476
  107.1 0.0 collective-permute-start.10
  107.1 0.8 collective-permute-done.11.hi_ref
  107.9 0.3 collective-permute-done.10.lo_ref
  108.2 1.4 %shard_map.96 = (f32[3,1,1,17]{3,2,1,0:T(1,128)}, f32[1,1,16]{2,1,0:T(1,128)}) custom-call(s32[4]{0:T(128)S(1)} %pad_add_fusion.idx_ref, f32[8,128]{1,0:T(8,128)S(1)} %get-tuple-element.60.m0_in, f32[8,128]{1,0:T(8,128)S(1)} %get-tuple-element.61.m1_in, f32[8,128]{1,0:T(8,128)S(1)} %collective-permute-done.10.lo_ref, ...), custom_call_target="tpu_custom_call" | custom-call | bytes 65536 | tf_op jit(solution)/shard_map/pallas_call | solution.py:135
  (1 shorter events, 0.0 us)
Async XLA Ops:
  2.5 35.9 %all-to-all-start = ((bf16[64,3,4,128]{3,2,1,0:T(4,128)(2,1)}), bf16[64,3,4,128]{3,2,1,0:T(4,128)(2,1)S(1)}, u32[]{:S(2)}, u32[]{:S(2)}) async-start(bf16[64,3,4,128]{3,2,1,0:T(4,128)(2,1)} %shard_map.86), calls=%async_computation | async-start | bytes 393216 | tf_op jit(solution)/shard_map/all_to_all | solution.py:494
  21.8 0.9 copy-start.2
  23.0 9.7 %collective-permute-start = (bf16[32,256]{1,0:T(8,128)(2,1)S(1)}, bf16[32,256]{1,0:T(8,128)(2,1)S(1)}, u32[]{:S(2)}, u32[]{:S(2)}) collective-permute-start(bf16[32,256]{1,0:T(8,128)(2,1)S(1)} %get-tuple-element.33), channel_id=1, source_target_pairs={{0,1},{1,2},{2,3},{3,4},{4,5},{5,6},{6,7},{7,8},{8,9},{9,10},{10,1... | collective-permute-start | bytes 49160 | tf_op jit(solution)/shard_map/ppermute | solution.py:476
  25.9 6.8 %collective-permute-start.1 = (bf16[32,256]{1,0:T(8,128)(2,1)S(1)}, bf16[32,256]{1,0:T(8,128)(2,1)S(1)}, u32[]{:S(2)}, u32[]{:S(2)}) collective-permute-start(bf16[32,256]{1,0:T(8,128)(2,1)S(1)} %get-tuple-element.34), channel_id=1, source_target_pairs={{0,63},{1,0},{2,1},{3,2},{4,3},{5,4},{6,5},{7,6},{8,7},{9,8},{10,9... | collective-permute-start | bytes 49160 | tf_op jit(solution)/shard_map/ppermute | solution.py:476
  39.9 22.1 %all-to-all-start.1 = ((bf16[64,8,128]{2,1,0:T(8,128)(2,1)}), bf16[64,8,128]{2,1,0:T(8,128)(2,1)S(1)}, u32[]{:S(2)}, u32[]{:S(2)}) async-start(bf16[64,8,128]{2,1,0:T(8,128)(2,1)} %bitcast.3), calls=%async_computation.1 | async-start | bytes 262144 | tf_op jit(solution)/shard_map/all_to_all | solution.py:504
  48.4 4.3 %collective-permute-start.2 = (bf16[48,256]{1,0:T(8,128)(2,1)S(1)}, bf16[48,256]{1,0:T(8,128)(2,1)S(1)}, u32[]{:S(2)}, u32[]{:S(2)}) collective-permute-start(bf16[48,256]{1,0:T(8,128)(2,1)S(1)} %get-tuple-element.44), channel_id=1, source_target_pairs={{0,64},{64,128},{128,192},{192,256},{256,320},{320,384},{384,448},... | collective-permute-start | bytes 73736 | tf_op jit(solution)/shard_map/ppermute | solution.py:476
  51.7 10.3 %copy-start = (bf16[1024,256]{1,0:T(8,128)(2,1)S(1)}, bf16[1024,256]{1,0:T(8,128)(2,1)}, u32[]{:S(2)}) copy-start(bf16[1024,256]{1,0:T(8,128)(2,1)} %constant.20.clone.lin_ref) | copy-start | bytes 1572868
  51.7 10.3 %copy-start.1 = (bf16[256,256]{1,0:T(8,128)(2,1)S(1)}, bf16[256,256]{1,0:T(8,128)(2,1)}, u32[]{:S(2)}) copy-start(bf16[256,256]{1,0:T(8,128)(2,1)} %constant.21.clone.clin_ref) | copy-start | bytes 393220
  51.7 3.5 %collective-permute-start.3 = (bf16[48,256]{1,0:T(8,128)(2,1)S(1)}, bf16[48,256]{1,0:T(8,128)(2,1)S(1)}, u32[]{:S(2)}, u32[]{:S(2)}) collective-permute-start(bf16[48,256]{1,0:T(8,128)(2,1)S(1)} %get-tuple-element.45), channel_id=1, source_target_pairs={{0,448},{64,0},{128,64},{192,128},{256,192},{320,256},{384,320},{4... | collective-permute-start | bytes 73736 | tf_op jit(solution)/shard_map/ppermute | solution.py:476
  63.5 28.1 %all-to-all-start.2 = ((bf16[64,4,128]{2,1,0:T(4,128)(2,1)}), bf16[64,4,128]{2,1,0:T(4,128)(2,1)S(1)}, u32[]{:S(2)}, u32[]{:S(2)}) async-start(bf16[64,4,128]{2,1,0:T(4,128)(2,1)} %get-tuple-element.52), calls=%async_computation.2 | async-start | bytes 131072 | tf_op jit(solution)/shard_map/all_to_all | solution.py:528
  78.0 9.4 %collective-permute-start.7 = (f32[64,128]{1,0:T(8,128)S(1)}, f32[64,128]{1,0:T(8,128)S(1)}, u32[]{:S(2)}, u32[]{:S(2)}) collective-permute-start(f32[64,128]{1,0:T(8,128)S(1)} %all_gather.9), channel_id=1, source_target_pairs={{0,62},{1,63},{2,0},{3,1},{4,2},{5,3},{6,4},{7,5},{8,6},{9,7},{10,... | collective-permute-start | bytes 98312 | tf_op jit(solution)/shard_map/ppermute | solution.py:536
  81.9 8.4 %collective-permute-start.6 = (f32[64,128]{1,0:T(8,128)S(1)}, f32[64,128]{1,0:T(8,128)S(1)}, u32[]{:S(2)}, u32[]{:S(2)}) collective-permute-start(f32[64,128]{1,0:T(8,128)S(1)} %all_gather.9), channel_id=1, source_target_pairs={{0,63},{1,0},{2,1},{3,2},{4,3},{5,4},{6,5},{7,6},{8,7},{9,8},{10,9... | collective-permute-start | bytes 98312 | tf_op jit(solution)/shard_map/ppermute | solution.py:536
  92.2 5.6 %collective-permute-start.5 = (f32[8,128]{1,0:T(8,128)S(1)}, f32[8,128]{1,0:T(8,128)S(1)}, u32[]{:S(2)}, u32[]{:S(2)}) collective-permute-start(f32[8,128]{1,0:T(8,128)S(1)} %get-tuple-element.53.n0_ref), channel_id=1, source_target_pairs={{0,448},{64,0},{128,64},{192,128},{256,192},{320,256},{384,320},{4... | collective-permute-start | bytes 12296 | tf_op jit(solution)/shard_map/ppermute | solution.py:476
  94.1 3.7 %collective-permute-start.4 = (f32[8,128]{1,0:T(8,128)S(1)}, f32[8,128]{1,0:T(8,128)S(1)}, u32[]{:S(2)}, u32[]{:S(2)}) collective-permute-start(f32[8,128]{1,0:T(8,128)S(1)} %get-tuple-element.54.n1_ref), channel_id=1, source_target_pairs={{0,64},{64,128},{128,192},{192,256},{256,320},{320,384},{384,448},... | collective-permute-start | bytes 12296 | tf_op jit(solution)/shard_map/ppermute | solution.py:476
  98.8 3.0 %collective-permute-start.9 = (f32[8,128]{1,0:T(8,128)S(1)}, f32[8,128]{1,0:T(8,128)S(1)}, u32[]{:S(2)}, u32[]{:S(2)}) collective-permute-start(f32[8,128]{1,0:T(8,128)S(1)} %get-tuple-element.56.m0_in), channel_id=1, source_target_pairs={{0,448},{64,0},{128,64},{192,128},{256,192},{320,256},{384,320},{4... | collective-permute-start | bytes 12296 | tf_op jit(solution)/shard_map/ppermute | solution.py:476
  100.6 1.9 %collective-permute-start.8 = (f32[8,128]{1,0:T(8,128)S(1)}, f32[8,128]{1,0:T(8,128)S(1)}, u32[]{:S(2)}, u32[]{:S(2)}) collective-permute-start(f32[8,128]{1,0:T(8,128)S(1)} %get-tuple-element.57.m1_in), channel_id=1, source_target_pairs={{0,64},{64,128},{128,192},{192,256},{256,320},{320,384},{384,448},... | collective-permute-start | bytes 12296 | tf_op jit(solution)/shard_map/ppermute | solution.py:476
  103.5 4.4 %collective-permute-start.11 = (f32[8,128]{1,0:T(8,128)S(1)}, f32[8,128]{1,0:T(8,128)S(1)}, u32[]{:S(2)}, u32[]{:S(2)}) collective-permute-start(f32[8,128]{1,0:T(8,128)S(1)} %get-tuple-element.60.m0_in), channel_id=1, source_target_pairs={{0,448},{64,0},{128,64},{192,128},{256,192},{320,256},{384,320},{4... | collective-permute-start | bytes 12296 | tf_op jit(solution)/shard_map/ppermute | solution.py:476
  107.1 1.2 %collective-permute-start.10 = (f32[8,128]{1,0:T(8,128)S(1)}, f32[8,128]{1,0:T(8,128)S(1)}, u32[]{:S(2)}, u32[]{:S(2)}) collective-permute-start(f32[8,128]{1,0:T(8,128)S(1)} %get-tuple-element.61.m1_in), channel_id=1, source_target_pairs={{0,64},{64,128},{128,192},{192,256},{256,320},{320,384},{384,448},... | collective-permute-start | bytes 12296 | tf_op jit(solution)/shard_map/ppermute | solution.py:476
